TPU v7x, 32 devices: a whole 2x2x4 slice. The times are simulated.
32 devices in a mesh: ctx: 4 (over y, x), chan: 8 (over z, core).
Axes of the slice: x: 2, y: 2, z: 4, core: 2. Of those that a mesh axis runs over, the one named last changes fastest.
Arguments:
- featurized: bfloat16 [8192, 3, 8192], P('ctx', None, 'chan'), may hold values from -6 to 6
- short_filter: float32 [3, 3, 8192], P(None, None, 'chan'), may hold values from -2.5 to 2.5
- decay_rate: float32 [512, 16], P('chan'), as said below
- residue: float32 [512, 16], P('chan'), may hold values from -2.5 to 2.5
- skip_gain: float32 [8192], P('chan'), may hold values from 0.25 to 1.5
- out_weight: bfloat16 [8192, 4096], P('chan'), may hold values from -0.0625 to 0.0625
Outputs:
- output: bfloat16 [8192, 4096], P(('ctx', 'chan'))
Inputs may be any that keep to these rules, and one draw needn't show every extreme that they name: `decay_rate`: each rate is at least 0.2 / 8192.
All inputs are finite; a program needn't handle non-finite values.
Results may differ from a plain program's by a relative error of at most 0.02.
Values may be sent and summed in bfloat16 or wider, within the bound.
No kernel may reach another device: no remote copies, remote signals or barrier semaphores. Data moves between devices by JAX's collectives and lax.ppermute only.
A program may use at most 320 MiB of HBM per device.

v0:
```python
import jax
import jax.numpy as jnp
from jax import lax
from jax.sharding import PartitionSpec as P


def shifted(value, axis, steps):
    count = lax.axis_size(axis)
    first, last = (max(0, -steps), min(count, count - steps))
    return lax.ppermute(value, axis, [(source, source + steps) for source in range(first, last)])


def own_block(local_filter, source_t, tile_count):
    filters, tok_rows = local_filter.shape
    group = source_t.shape[1]
    width = tok_rows // tile_count
    padded = jnp.concatenate([jnp.zeros((filters, width), jnp.float32), local_filter], axis=1)
    offsets = (
        jnp.arange(width, dtype=jnp.int32)[:, None]
        - jnp.arange(width, dtype=jnp.int32)[None, :]
        + width
    )
    tiles = source_t.reshape(filters, group, tile_count, width)
    summed = jnp.zeros((filters, group, tile_count, width), jnp.float32)
    for lag_tile in range(tile_count):
        segment = padded[:, lag_tile * width : lag_tile * width + 2 * width]
        toeplitz = jnp.take(segment, offsets, axis=1)
        product = jnp.einsum(
            "fts,fgps->fgpt",
            toeplitz,
            tiles[:, :, : tile_count - lag_tile],
            precision=lax.Precision.HIGHEST,
        )
        summed = summed.at[:, :, lag_tile:].add(product)
    return summed.reshape(filters, group, tok_rows)


def on_device(featurized, short_filter, decay_rate, residue, skip_gain, out_weight):
    tok_rows = featurized.shape[0]
    channels = featurized.shape[2]
    filters = decay_rate.shape[0]
    group = channels // filters
    rim_rows = shifted(featurized[tok_rows - 2 :], "ctx", 1)
    extended = jnp.concatenate([rim_rows, featurized], axis=0).astype(jnp.float32)
    shortened = (
        short_filter[0] * extended[2:]
        + short_filter[1] * extended[1:-1]
        + short_filter[2] * extended[:-2]
    )
    query_part = shortened[:, 0]
    gated = (shortened[:, 1] * shortened[:, 2]).astype(jnp.bfloat16)
    gated_float = gated.astype(jnp.float32)
    scaled = residue * jnp.sqrt(-jnp.expm1(-2.0 * decay_rate))
    positions = jnp.arange(tok_rows, dtype=jnp.float32)
    powers = jnp.exp(-decay_rate[:, :, None] * positions)
    tails = jnp.exp(-decay_rate[:, :, None] * (tok_rows - positions))
    signals_t = gated_float.reshape(tok_rows, filters, group).transpose(1, 2, 0)
    local_state = jnp.einsum("fmt,fgt->fmg", tails, signals_t, precision=lax.Precision.HIGHEST)
    own_index = lax.axis_index("ctx")
    piece = lax.all_gather(
        local_state[None].astype(jnp.bfloat16), "ctx", axis=0, tiled=True
    ).astype(jnp.float32)
    lags = own_index - 1 - jnp.arange(piece.shape[0], dtype=jnp.int32)
    spans = jnp.maximum(lags, 0).astype(jnp.float32) * tok_rows
    weights = jnp.where(
        lags[:, None, None] >= 0, jnp.exp(-decay_rate[None] * spans[:, None, None]), 0.0
    )
    carried = jnp.zeros_like(local_state) + jnp.einsum(
        "kfm,kfmg->fmg", weights, piece, precision=lax.Precision.HIGHEST
    )
    far_part = jnp.einsum(
        "fmt,fmg->fgt", scaled[:, :, None] * powers, carried, precision=lax.Precision.HIGHEST
    )
    local_filter = jnp.einsum("fm,fmt->ft", scaled, powers, precision=lax.Precision.HIGHEST)
    tile_count = tok_rows // 256
    near_part = own_block(local_filter, signals_t, tile_count)
    long_conv = (near_part + far_part).transpose(2, 0, 1).reshape(tok_rows, channels)
    mixed_rows = (query_part * (long_conv + skip_gain * gated_float)).astype(jnp.bfloat16)
    partial_value = jnp.dot(mixed_rows, out_weight, preferred_element_type=jnp.float32)
    result = lax.psum_scatter(
        partial_value.astype(jnp.bfloat16), "chan", scatter_dimension=0, tiled=True
    )
    return result


def solution(mesh):
    return jax.shard_map(
        on_device,
        mesh=mesh,
        in_specs=(
            P("ctx", None, "chan"),
            P(None, None, "chan"),
            P("chan", None),
            P("chan", None),
            P("chan"),
            P("chan", None),
        ),
        out_specs=P(("ctx", "chan"), None),
        check_vma=False,
    )
```

profile of v0, /device:TPU:16, one launch (start us, length us, event | category | flops | bytes accessed | tf_op | source)
XLA Modules:
  0.0 2679.6 jit_solution(4767787791432122685)
XLA Ops:
  37.4 215.9 %gather_fusion = f32[65536,64]{1,0:T(8,128)} fusion(f32[64,512]{0,1:T(8,128)S(1)} %get-tuple-element.121, s32[65536]{0:T(1024)S(1)} %broadcast_clamp_fusion), kind=kCustom, calls=%fused_computation.clone | custom fusion | bytes 33816576 | tf_op jit(solution)/shard_map/jit(_take)/gather | solution.py:27
  253.3 26.2 copy.56
  279.5 215.9 %gather_fusion.1 = f32[65536,64]{1,0:T(8,128)} fusion(f32[64,512]{0,1:T(8,128)S(1)} %get-tuple-element.120, s32[65536]{0:T(1024)S(1)} %broadcast_clamp_fusion), kind=kCustom, calls=%fused_computation.1.clone | custom fusion | bytes 33816576 | tf_op jit(solution)/shard_map/jit(_take)/gather | solution.py:27
  495.4 26.1 copy.58
  521.5 215.9 %gather_fusion.2 = f32[65536,64]{1,0:T(8,128)} fusion(f32[64,512]{0,1:T(8,128)S(1)} %get-tuple-element.119, s32[65536]{0:T(1024)S(1)} %broadcast_clamp_fusion), kind=kCustom, calls=%fused_computation.2.clone | custom fusion | bytes 33816576 | tf_op jit(solution)/shard_map/jit(_take)/gather | solution.py:27
  737.5 26.2 copy.61
  763.7 215.9 %gather_fusion.3 = f32[65536,64]{1,0:T(8,128)} fusion(f32[64,512]{0,1:T(8,128)S(1)} %copy-done.4, s32[65536]{0:T(1024)S(1)} %broadcast_clamp_fusion), kind=kCustom, calls=%fused_computation.3.clone | custom fusion | bytes 33816576 | tf_op jit(solution)/shard_map/jit(_take)/gather | solution.py:27
  979.6 26.2 copy.64
  1005.8 215.9 %gather_fusion.4 = f32[65536,64]{1,0:T(8,128)} fusion(f32[64,512]{0,1:T(8,128)S(1)} %copy-done.3, s32[65536]{0:T(1024)S(1)} %broadcast_clamp_fusion), kind=kCustom, calls=%fused_computation.4.clone | custom fusion | bytes 33816576 | tf_op jit(solution)/shard_map/jit(_take)/gather | solution.py:27
  1221.7 26.2 copy.67
  1248.0 215.9 %gather_fusion.5 = f32[65536,64]{1,0:T(8,128)} fusion(f32[64,512]{0,1:T(8,128)S(1)} %copy-done.2, s32[65536]{0:T(1024)S(1)} %broadcast_clamp_fusion), kind=kCustom, calls=%fused_computation.5.clone | custom fusion | bytes 33816576 | tf_op jit(solution)/shard_map/jit(_take)/gather | solution.py:27
  1463.9 26.2 copy.70
  1490.1 215.9 %gather_fusion.6 = f32[65536,64]{1,0:T(8,128)} fusion(f32[64,512]{0,1:T(8,128)S(1)} %copy-done.1, s32[65536]{0:T(1024)S(1)} %broadcast_clamp_fusion), kind=kCustom, calls=%fused_computation.6.clone | custom fusion | bytes 33816576 | tf_op jit(solution)/shard_map/jit(_take)/gather | solution.py:27
  1706.0 26.2 copy.73
  1732.2 215.9 %gather_fusion.7 = f32[65536,64]{1,0:T(8,128)} fusion(f32[64,512]{0,1:T(8,128)S(1)} %copy-done, s32[65536]{0:T(1024)S(1)} %broadcast_clamp_fusion), kind=kCustom, calls=%fused_computation.7.clone | custom fusion | bytes 33816576 | tf_op jit(solution)/shard_map/jit(_take)/gather | solution.py:27
  1948.2 26.2 copy.76
  1991.7 35.9 %fusion = f32[2048,3,1024]{0,2,1:T(8,128)} fusion(f32[2050,3,1024]{0,2,1:T(8,128)} %maximum_convert_fusion, f32[3,1024]{1,0:T(4,128)S(1)} %copy-done.17, f32[3,1024]{1,0:T(4,128)S(1)} %copy-done.18, f32[3,1024]{1,0:T(4,128)S(1)} %copy-done.16), kind=kLoop, calls=%fused_computation.9 | loop fusion | flops 31457280 | bytes 100700160 | tf_op jit(solution)/shard_map/add | solution.py:46
  2119.8 46.6 %scatter-add.24 = f32[64,16,8,256]{3,2,1,0:T(8,128)} dynamic-update-slice(f32[64,16,8,256]{3,2,1,0:T(8,128)} %fusion.14, f32[64,16,7,256]{3,2,1,0:T(8,128)} %slice_add_fusion.2, s32[]{:T(128)} %constant.252.clone.1, s32[]{:T(128)} %constant.252.clone.1, s32[]{:T(128)} %constant.253.clone.1, s32[]{:T(128)} %constant.252.clone.1) | dynamic-update-slice | bytes 14680068 | tf_op jit(solution)/shard_map/scatter-add | solution.py:34
  2195.8 46.6 %scatter-add.25 = f32[64,16,8,256]{3,2,1,0:T(8,128)} dynamic-update-slice(f32[64,16,8,256]{3,2,1,0:T(8,128)} %scatter-add.24, f32[64,16,6,256]{3,2,1,0:T(8,128)} %slice_add_fusion.1, s32[]{:T(128)} %constant.252.clone.1, s32[]{:T(128)} %constant.252.clone.1, s32[]{:T(128)} %constant.254.clone.1, s32[]{:T(128)} %constant.252.clone.1) | dynamic-update-slice | bytes 12582916 | tf_op jit(solution)/shard_map/scatter-add | solution.py:34
  2256.9 46.6 %scatter-add.26 = f32[64,16,8,256]{3,2,1,0:T(8,128)} dynamic-update-slice(f32[64,16,8,256]{3,2,1,0:T(8,128)} %scatter-add.25, f32[64,16,5,256]{3,2,1,0:T(8,128)} %slice_add_fusion, s32[]{:T(128)} %constant.252.clone.1, s32[]{:T(128)} %constant.252.clone.1, s32[]{:T(128)} %constant.255.clone.1, s32[]{:T(128)} %constant.252.clone.1) | dynamic-update-slice | bytes 10485764 | tf_op jit(solution)/shard_map/scatter-add | solution.py:34
  2343.9 46.2 %scatter-add.30 = f32[64,16,8,256]{3,2,1,0:T(8,128)} dynamic-update-slice(f32[64,16,8,256]{3,2,1,0:T(8,128)} %get-tuple-element.112, f32[64,16,3,256]{3,2,1,0:T(4,128)} %slice_add_fusion.3, s32[]{:T(128)} %constant.252.clone.1, s32[]{:T(128)} %constant.252.clone.1, s32[]{:T(128)} %constant.257.clone.1, s32[]{:T(128)} %constant.252.clone.1) | dynamic-update-slice | bytes 6291460 | tf_op jit(solution)/shard_map/scatter-add | solution.py:34
  2408.9 23.5 scatter-add.34
  2482.4 24.0 convolution_convert_fusion
  2506.4 165.9 %reduce-scatter.2.cloned.1.call-done = bf16[256,4096]{1,0:T(8,128)(2,1)} async-done(((bf16[2048,4096]{1,0:T(8,128)(2,1)}), bf16[256,4096]{1,0:T(8,128)(2,1)}) %reduce-scatter.2.cloned.1.call-update) | async-done | bytes 2097168 | tf_op jit(solution)/shard_map/reduce_scatter | solution.py:80
  (92 shorter events, 293.2 us)
Async XLA Ops:
  6.5 2665.8 %reduce-scatter.2.cloned.1.call-start = ((), (), s32[]{:S(2)}) async-start(), calls=%async_computation.1 | async-start | bytes 18874368 | tf_op jit(solution)/shard_map/reduce_scatter | solution.py:80
  7.9 1966.4 %collective-permute-start = (bf16[2,3,1024]{2,0,1:T(2,128)(2,1)}, bf16[2,3,1024]{2,0,1:T(2,128)(2,1)}, u32[]{:S(2)}, u32[]{:S(2)}) collective-permute-start(bf16[2,3,1024]{2,0,1:T(2,128)(2,1)} %slice.309), channel_id=1, source_target_pairs={{0,8},{8,16},{16,24},{1,9},{9,17},{17,25},{2,10},{10,18},{18,26},{... | collective-permute-start | bytes 36872 | tf_op jit(solution)/shard_map/ppermute | solution.py:10
  14.8 2.7 copy-start.14
  14.9 22.5 copy-start.11
  737.4 26.2 copy-start.4
  979.6 26.2 copy-start.3
  1221.7 26.2 copy-start.2
  1463.9 26.2 copy-start.1
  1706.0 26.2 copy-start
  1975.5 16.2 copy-start.16
  1975.5 16.2 copy-start.17
  1975.5 16.1 copy-start.18
  2034.1 5.1 copy-start.7
  2035.6 4.7 copy-start.5
  2035.7 6.8 copy-start.9
  2303.5 9.8 copy-start.8
  2343.8 51.5 %copy-start.10 = (bf16[64,16,1,256]{3,2,1,0:T(2,128)(2,1)S(1)}, bf16[64,16,1,256]{3,2,1,0:T(2,128)(2,1)}, u32[]{:S(2)}) copy-start(bf16[64,16,1,256]{3,2,1,0:T(2,128)(2,1)} %slice.381) | copy-start | bytes 1572868
  2432.4 9.5 copy-start.12
  2432.4 9.5 copy-start.19
  2441.9 20.9 copy-start.13
  2441.9 21.7 copy-start.6
  2441.9 21.7 copy-start.15
  2463.6 8.2 copy-start.20
Sparse Core Ops, SparseCore 0:
  2506.5 165.7 reduce-scatter.1
where the time goes:
time: 2700 us; the launch traced here: 2680 us
  local copies, waits for them, and re-layouts  2190 us (81%)
  waiting for transfers between devices  166 us (6%)
  matrix products  154 us (6%)
  other arithmetic  142 us (5%)
    gather x16, local copies, waits for them, and re-layouts, own_block(): toeplitz = jnp.take(segment, offsets, axis=1)  1940 us
    scatter-add x5, local copies, waits for them, and re-layouts, own_block(): summed = summed.at[:, :, lag_tile:].add(product)  209 us
    reduce_scatter x1, waiting for transfers between devices, on_device(): lax.psum_scatter(partial_value.astype(jnp.bfloat16), 'chan', scatter_dime...  166 us
    dot_general x8, matrix products, own_block(): jnp.einsum('fts,fgps->fgpt', toeplitz, tiles[:, :, :tile_count - lag_tile...  113 us
  transfers between devices with their start and end apart: 2, of which 1 were waited for; matrix products, arithmetic and copies ran while one was open for 73% of the time, Pallas kernels for 0%

commit v1 on v0

v1 whole, which is shorter than its diff:
```python
import functools

import jax
import jax.numpy as jnp
from jax import lax
from jax.experimental import pallas as pl
from jax.experimental.pallas import tpu as pltpu
from jax.sharding import PartitionSpec as P

LANES = 128
CHUNK = 128
BF16 = jnp.bfloat16
F32 = jnp.float32


def params(mib=48):
    return pltpu.CompilerParams(vmem_limit_bytes=mib << 20)


def cost(flops, moved):
    return pl.CostEstimate(flops=int(flops), bytes_accessed=int(moved), transcendentals=0)


def iota(shape, dim):
    return lax.broadcasted_iota(jnp.int32, shape, dim)


def toeplitz_kernel(modes, rate_ref, scale_ref, tile_ref):
    filters = LANES // modes
    reach = iota((LANES, CHUNK), 1).astype(F32)
    terms = scale_ref[...] * jnp.exp(-rate_ref[...] * reach)
    taps = terms.reshape(filters, modes, CHUNK).sum(axis=1)
    keep = iota((CHUNK, CHUNK), 0) <= iota((CHUNK, CHUNK), 1)
    for f in range(filters):
        rows = jnp.broadcast_to(taps[f : f + 1], (CHUNK, CHUNK))
        rolled = pltpu.roll(rows, 0, 1, stride=1, stride_axis=0)
        tile_ref[f] = jnp.where(keep, rolled, 0.0).astype(BF16)


def short_conv(stream, stage_ref, x_ref, rim_ref, taps_ref, k):
    at = 8 + k * CHUNK
    return (
        taps_ref[0, stream : stream + 1, :] * stage_ref[at : at + CHUNK, :]
        + taps_ref[1, stream : stream + 1, :] * stage_ref[at - 1 : at - 1 + CHUNK, :]
        + taps_ref[2, stream : stream + 1, :] * stage_ref[at - 2 : at - 2 + CHUNK, :]
    )


def stage(stream, stage_ref, x_ref, rim_ref):
    stage_ref[0:8, :] = jnp.zeros((8, LANES), F32)
    stage_ref[6:8, :] = rim_ref[stream].astype(F32)
    stage_ref[8:, :] = x_ref[0].astype(F32)


def diagonal(modes, group):
    return (iota((LANES, LANES), 0) // modes) == (iota((LANES, LANES), 1) // group)


def dot(a, b, dims=((1,), (0,))):
    return lax.dot_general(a, b, (dims, ((), ())), preferred_element_type=F32)


def gate_kernel(modes, group, k_ref, v_ref, rim_ref, taps_ref, rate_ref, gated_ref, state_ref, k_stage, v_stage):
    stage(1, k_stage, k_ref, rim_ref)
    stage(2, v_stage, v_ref, rim_ref)
    rate = rate_ref[...]
    ends = jnp.exp(-rate * (CHUNK - 1 - iota((LANES, CHUNK), 1)).astype(F32)).astype(BF16)
    fade = jnp.exp(-rate * CHUNK)
    state = jnp.zeros((LANES, LANES), F32)
    for k in range(gated_ref.shape[0] // CHUNK):
        gated = (
            short_conv(1, k_stage, k_ref, rim_ref, taps_ref, k) * short_conv(2, v_stage, v_ref, rim_ref, taps_ref, k)
        ).astype(BF16)
        gated_ref[k * CHUNK : (k + 1) * CHUNK, :] = gated
        state = fade * state + dot(ends, gated)
    state = jnp.where(diagonal(modes, group), state, 0.0).astype(BF16)
    fold = (iota((group, LANES), 0) == lax.rem(iota((group, LANES), 1), group)).astype(BF16)
    state_ref[...] = dot(fold, state, ((1,), (1,))).astype(BF16)


def near_kernel(
    modes,
    group,
    gated_ref,
    tile_ref,
    q_ref,
    rim_ref,
    taps_ref,
    gain_ref,
    row_rate_ref,
    row_scale_ref,
    near_ref,
    query_ref,
    q_stage,
    sources,
    sums,
):
    stage(0, q_stage, q_ref, rim_ref)
    filters = LANES // group
    chunks = gated_ref.shape[0] // CHUNK
    eye = (iota((CHUNK, CHUNK), 0) == iota((CHUNK, CHUNK), 1)).astype(BF16)
    for k in range(0, chunks, 2):
        turned = dot(eye, gated_ref[k * CHUNK : (k + 2) * CHUNK, :], ((1,), (1,))).astype(BF16)
        sources[k] = turned[:, :CHUNK]
        sources[k + 1] = turned[:, CHUNK:]
    for f in range(filters):
        rows = slice(f * group, (f + 1) * group)
        block = sources[:, rows, :].reshape(chunks * group, CHUNK)
        sums[:, rows, :] = dot(block, tile_ref[f]).astype(BF16).reshape(chunks, group, CHUNK)
    row_rate = row_rate_ref[0]
    ends = jnp.exp(-row_rate * (CHUNK - 1 - iota((CHUNK, LANES), 0)).astype(F32)).astype(BF16)
    reads = (row_scale_ref[0] * jnp.exp(-row_rate * (iota((CHUNK, LANES), 0) + 1).astype(F32))).astype(BF16)
    both = jnp.concatenate([eye, reads], axis=1)
    fade = jnp.exp(-row_rate * CHUNK)
    own_modes = diagonal(group, modes)
    gain = gain_ref[...]
    state = jnp.zeros((LANES, LANES), F32)
    for k in range(chunks):
        rows = slice(k * CHUNK, (k + 1) * CHUNK)
        summed = dot(both, jnp.concatenate([sums[k], state.astype(BF16)], axis=1), ((1,), (1,)))
        state = fade * state + jnp.where(own_modes, dot(sources[k], ends), 0.0)
        near_ref[rows, :] = (summed + gain * gated_ref[rows, :].astype(F32)).astype(BF16)
        query_ref[rows, :] = short_conv(0, q_stage, q_ref, rim_ref, taps_ref, k).astype(BF16)


def mix_kernel(modes, group, parts, core_ref, near_ref, query_ref, *rest):
    *piece_refs, row_rate_ref, row_scale_ref, keep_ref, give_ref, mixed_ref = rest
    tok_rows = near_ref.shape[0]
    size = tok_rows // (2 * parts)
    core = core_ref[0]
    row_rate = row_rate_ref[0]
    carried = jnp.zeros((group, LANES), F32)
    for d, piece_ref in enumerate(piece_refs):
        carried = carried + jnp.exp(-row_rate * float(d * tok_rows)) * piece_ref[...].astype(F32)
    state = jnp.where(diagonal(group, modes), jnp.concatenate([carried] * (LANES // group), axis=0), 0.0).astype(BF16)
    reads = row_scale_ref[0] * jnp.exp(-row_rate * (iota((CHUNK, LANES), 0) + 1).astype(F32))
    for k in range(tok_rows // CHUNK):
        rows = slice(k * CHUNK, (k + 1) * CHUNK)
        fade = jnp.exp(-row_rate * float(k * CHUNK))
        far = dot((reads * fade).astype(BF16), state, ((1,), (1,)))
        mixed = (query_ref[rows, :].astype(F32) * (near_ref[rows, :].astype(F32) + far)).astype(BF16)
        width = min(size, CHUNK)
        for piece in range(0, CHUNK, width):
            block, inner = divmod(k * CHUNK + piece, size)
            side = lax.rem(core + block, 2)
            mixed_ref[side, block // 2, inner : inner + width, :] = mixed[piece : piece + width]
    keep_ref[...] = mixed_ref[0]
    give_ref[...] = mixed_ref[1]


def product_kernel(which_ref, own_ref, other_ref, own_w_ref, other_w_ref, out_ref):
    out_ref[...] = (dot(own_ref[0], own_w_ref[...]) + dot(other_ref[0], other_w_ref[...])).astype(BF16)


def product(which, own, other, own_w, other_w, part, split):
    _, rows, depth = own.shape
    width = own_w.shape[1] // split
    tile = min(512, width)
    steps = width // tile
    grid_spec = pltpu.PrefetchScalarGridSpec(
        num_scalar_prefetch=1,
        grid=(steps,),
        in_specs=[
            pl.BlockSpec((1, rows, depth), lambda j, which: (which[0], 0, 0)),
            pl.BlockSpec((1, rows, depth), lambda j, which: (which[0], 0, 0)),
            pl.BlockSpec((depth, tile), lambda j, which: (0, part * steps + j)),
            pl.BlockSpec((depth, tile), lambda j, which: (0, part * steps + j)),
        ],
        out_specs=pl.BlockSpec((rows, tile), lambda j, which: (0, j)),
    )
    return pl.pallas_call(
        product_kernel,
        grid_spec=grid_spec,
        out_shape=jax.ShapeDtypeStruct((rows, width), BF16),
        compiler_params=params(),
        cost_estimate=cost(4 * rows * depth * width, 4 * depth * width + 6 * rows * width),
        name="product",
    )(which.reshape(1).astype(jnp.int32), own, other, own_w, other_w)


def shifted(value, axis, steps):
    count = lax.axis_size(axis)
    return lax.ppermute(value, axis, [(i, i + steps) for i in range(count - steps)])


def on_device(featurized, short_filter, decay_rate, residue, skip_gain, out_weight):
    tok_rows, streams, channels = featurized.shape
    filters, modes = decay_rate.shape
    group = channels // filters
    blocks = channels // LANES
    ctx_count = lax.axis_size("ctx")
    parts = lax.axis_size("chan") // 2
    chan_index = lax.axis_index("chan")
    place, core = chan_index // 2, chan_index % 2
    swap = [(i, i ^ 1) for i in range(2 * parts)]

    rim = shifted(featurized[tok_rows - 2 :], "ctx", 1).transpose(1, 0, 2)
    other_weight = lax.ppermute(out_weight, "chan", swap)
    features = featurized.transpose(1, 0, 2)
    scaled = residue * jnp.sqrt(-jnp.expm1(-2.0 * decay_rate))
    rate_cols = jnp.broadcast_to(decay_rate.reshape(-1, 1), (filters * modes, LANES))
    scale_cols = jnp.broadcast_to(scaled.reshape(-1, 1), (filters * modes, LANES))
    rate_rows = decay_rate.reshape(blocks, 1, LANES)
    scale_rows = scaled.reshape(blocks, 1, LANES)
    per_block = LANES // group

    square = pl.BlockSpec((LANES, LANES), lambda g: (g, 0))
    tile_spec = pl.BlockSpec((per_block, CHUNK, CHUNK), lambda g: (g, 0, 0))
    lanes_spec = pl.BlockSpec((tok_rows, LANES), lambda g: (0, g))
    rim_spec = pl.BlockSpec((streams, 2, LANES), lambda g: (0, 0, g))
    taps_spec = pl.BlockSpec((3, streams, LANES), lambda g: (0, 0, g))
    state_spec = pl.BlockSpec((group, LANES), lambda g: (g, 0))

    def stream_spec(i):
        return pl.BlockSpec((1, tok_rows, LANES), lambda g: (i, 0, g))

    tiles = pl.pallas_call(
        functools.partial(toeplitz_kernel, modes),
        grid=(blocks,),
        in_specs=[square, square],
        out_specs=tile_spec,
        out_shape=jax.ShapeDtypeStruct((filters, CHUNK, CHUNK), BF16),
        compiler_params=params(),
        cost_estimate=cost(filters * CHUNK * CHUNK * 40, filters * CHUNK * CHUNK * 4),
        name="toeplitz",
    )(rate_cols, scale_cols)

    stage_shape = pltpu.VMEM((8 + tok_rows, LANES), F32)
    wide = jax.ShapeDtypeStruct((tok_rows, channels), BF16)
    gated, state = pl.pallas_call(
        functools.partial(gate_kernel, modes, group),
        grid=(blocks,),
        in_specs=[stream_spec(1), stream_spec(2), rim_spec, taps_spec, square],
        out_specs=[lanes_spec, state_spec],
        out_shape=[wide, jax.ShapeDtypeStruct((blocks * group, LANES), BF16)],
        scratch_shapes=[stage_shape, stage_shape],
        compiler_params=params(),
        cost_estimate=cost(tok_rows * channels * 256, tok_rows * channels * 6),
        name="gate",
    )(features, features, rim, short_filter, rate_cols)

    pieces = [shifted(state, "ctx", d) for d in range(1, ctx_count)]

    row_spec = pl.BlockSpec((1, 1, LANES), lambda g: (g, 0, 0))
    chunks = tok_rows // CHUNK
    near, query = pl.pallas_call(
        functools.partial(near_kernel, modes, group),
        grid=(blocks,),
        in_specs=[
            lanes_spec,
            tile_spec,
            stream_spec(0),
            rim_spec,
            taps_spec,
            pl.BlockSpec((1, LANES), lambda g: (0, g)),
            row_spec,
            row_spec,
        ],
        out_specs=[lanes_spec, lanes_spec],
        out_shape=[wide, wide],
        scratch_shapes=[
            stage_shape,
            pltpu.VMEM((chunks, LANES, CHUNK), BF16),
            pltpu.VMEM((chunks, LANES, CHUNK), BF16),
        ],
        compiler_params=params(),
        cost_estimate=cost(tok_rows * channels * 1024, tok_rows * channels * 8),
        name="near",
    )(gated, tiles, features, rim, short_filter, skip_gain.reshape(1, channels), rate_rows, scale_rows)

    size = tok_rows // (2 * parts)
    out_spec = pl.BlockSpec((parts, size, LANES), lambda g, core: (0, 0, g))
    lanes_two = pl.BlockSpec((tok_rows, LANES), lambda g, core: (0, g))
    row_two = pl.BlockSpec((1, 1, LANES), lambda g, core: (g, 0, 0))
    part_shape = jax.ShapeDtypeStruct((parts, size, channels), BF16)
    keep, give = pl.pallas_call(
        functools.partial(mix_kernel, modes, group, parts),
        grid_spec=pltpu.PrefetchScalarGridSpec(
            num_scalar_prefetch=1,
            grid=(blocks,),
            in_specs=[lanes_two, lanes_two]
            + [pl.BlockSpec((group, LANES), lambda g, core: (g, 0))] * len(pieces)
            + [row_two, row_two],
            out_specs=[out_spec, out_spec],
            scratch_shapes=[pltpu.VMEM((2, parts, size, LANES), BF16)],
        ),
        out_shape=[part_shape, part_shape],
        compiler_params=params(),
        cost_estimate=cost(tok_rows * channels * 256, tok_rows * channels * 8),
        name="mix",
    )(core.reshape(1).astype(jnp.int32), near, query, *pieces, rate_rows, scale_rows)

    other = lax.ppermute(give, "chan", swap)

    split = 2
    last = parts - 1
    multiply = lambda which, j: product(jnp.clip(which, 0, last), keep, other, out_weight, other_weight, j, split)
    up = [None] * split
    down = [None] * split
    for s in range(1, parts):
        senders = range(0, min(s, last))
        up_pairs = [(2 * i + c, 2 * i + 2 + c) for i in senders for c in (0, 1)]
        down_pairs = [(2 * (last - i) + c, 2 * (last - i) - 2 + c) for i in senders for c in (0, 1)]
        for j in range(split):
            if s == 1:
                first = multiply(jnp.where(place == 0, last, 0), j)
                up[j], down[j] = first, first
            else:
                up[j] = (multiply(parts - s + place, j).astype(F32) + up[j].astype(F32)).astype(BF16)
                down[j] = (multiply(s - parts + place, j).astype(F32) + down[j].astype(F32)).astype(BF16)
            up[j] = lax.ppermute(up[j], "chan", up_pairs)
            down[j] = lax.ppermute(down[j], "chan", down_pairs)
    outs = [
        (multiply(place, j).astype(F32) + up[j].astype(F32) + down[j].astype(F32)).astype(BF16) for j in range(split)
    ]
    return jnp.concatenate(outs, axis=1)


def solution(mesh):
    return jax.shard_map(
        on_device,
        mesh=mesh,
        in_specs=(
            P("ctx", None, "chan"),
            P(None, None, "chan"),
            P("chan", None),
            P("chan", None),
            P("chan"),
            P("chan", None),
        ),
        out_specs=P(("ctx", "chan"), None),
        check_vma=False,
    )
```

time: 2700 us -> 223 us (0.08)
  local copies, waits for them, and re-layouts: 2190 us -> 4.31 us
  matrix products: 154 us -> 0 us
  other arithmetic: 142 us -> 16.3 us
  waiting for transfers between devices: 166 us -> 58.5 us
  Pallas kernels: 0 us -> 103 us
  starting transfers between devices: 3.98 us -> 38.6 us
    gather x16 -> x0, local copies, waits for them, and re-layouts: 1940 us -> none  [own_block(): toeplitz = jnp.take(segment, offsets, axis=1)]
    scatter-add x5 -> x0, local copies, waits for them, and re-layouts: 209 us -> none  [own_block(): summed = summed.at[:, :, lag_tile:].add(product)]
    reduce_scatter x1 -> x0, waiting for transfers between devices: 166 us -> none  [on_device(): lax.psum_scatter(partial_value.astype(jnp.bfloat16), 'chan', scatter_dime...]
    dot_general x11 -> x0, matrix products: 154 us -> none  [the longest x8 113 us: own_block(): jnp.einsum('fts,fgps->fgpt', toeplitz, tiles[:, :, :tile_count - lag_tile...]
    pallas_call x0 -> x16, Pallas kernels: none -> 103 us  [the longest x12 67.4 us: product(): pl.pallas_call(product_kernel, grid_spec=grid_spec, out_shape=jax.ShapeDt...]
    add x6 -> x0, other arithmetic: 88 us -> none  [the longest x5 52.1 us: own_block(): summed = summed.at[:, :, lag_tile:].add(product)]
    ppermute x1 -> x18, waiting for transfers between devices: 0.01 us -> 58.5 us  [the longest x6 47.9 us: on_device(): down[j] = lax.ppermute(down[j], 'chan', down_pairs)]
    ppermute x1 -> x18, starting transfers between devices: 3.98 us -> 38.6 us  [the longest x6 14.4 us: on_device(): up[j] = lax.ppermute(up[j], 'chan', up_pairs)]
  transfers between devices with their start and end apart: 2 -> 18, of which waited for: 1 -> 8; matrix products, arithmetic and copies ran while one was open for 73% -> 7% of each run, Pallas kernels for 0% -> 44%
where the time goes in v1:
time: 223 us; the launch traced here: 222 us
  Pallas kernels  103 us (46%)
  waiting for transfers between devices  58.5 us (26%)
  starting transfers between devices  38.6 us (17%)
  other arithmetic  16.3 us (7%)
  local copies, waits for them, and re-layouts  4.31 us (2%)
    pallas_call x12, Pallas kernels, product(): pl.pallas_call(product_kernel, grid_spec=grid_spec, out_shape=jax.ShapeDt...  67.4 us
    ppermute x6, waiting for transfers between devices, on_device(): down[j] = lax.ppermute(down[j], 'chan', down_pairs)  47.9 us
    pallas_call x1, Pallas kernels, on_device(): pl.pallas_call(functools.partial(near_kernel, modes, group), grid=(blocks...  15.5 us
    ppermute x6, starting transfers between devices, on_device(): up[j] = lax.ppermute(up[j], 'chan', up_pairs)  14.4 us
    ppermute x6, starting transfers between devices, on_device(): down[j] = lax.ppermute(down[j], 'chan', down_pairs)  14.2 us
    ppermute x4, starting transfers between devices, shifted(): lax.ppermute(value, axis, [(i, i + steps) for i in range(count - steps)])  10 us
    pallas_call x1, Pallas kernels, on_device(): pl.pallas_call(functools.partial(gate_kernel, modes, group), grid=(blocks...  9.95 us
    pallas_call x1, Pallas kernels, on_device(): pl.pallas_call(functools.partial(mix_kernel, modes, group, parts), grid_s...  9.16 us
  transfers between devices with their start and end apart: 18, of which 8 were waited for; matrix products, arithmetic and copies ran while one was open for 7% of the time, Pallas kernels for 44%

profile of v1, /device:TPU:16, one launch (start us, length us, event | category | flops | bytes accessed | tf_op | source)
XLA Modules:
  0.0 221.5 jit_solution(11064796017817136235)
XLA Ops:
  0.8 3.4 %collective-permute-start = (bf16[2,3,1024]{2,0,1:T(2,128)(2,1)S(1)}, bf16[2,3,1024]{2,0,1:T(2,128)(2,1)S(1)}, u32[]{:S(2)}, u32[]{:S(2)}) collective-permute-start(bf16[2,3,1024]{2,0,1:T(2,128)(2,1)S(1)} %slice.3), channel_id=1, source_target_pairs={{0,8},{8,16},{16,24},{1,9},{9,17},{17,25},{2,10},{10,18},{18,26},{... | collective-permute-start | bytes 36872 | tf_op jit(solution)/shard_map/ppermute | solution.py:183
  7.9 9.9 %gate.1 = (bf16[2048,1024]{1,0:T(8,128)(2,1)S(1)}, bf16[128,128]{1,0:T(8,128)(2,1)S(1)}) custom-call(bf16[3,2048,1024]{2,1,0:T(8,128)(2,1)} %bitcast.19, bf16[3,2048,1024]{2,1,0:T(8,128)(2,1)} %bitcast.20, bf16[3,2,1024]{2,1,0:T(2,128)(2,1)S(1)} %bitcast.12, f32[3,3,1024]{2,1,0:T(4,128)S(1)} %copy-done.1, f32[1024,128]{1,0:T(8,128)S(1)} %broadcast_in_dim.15.rate_ref), custom_call_target="tpu_custom_call" | custom-call | flops 536870912 | bytes 12582912 | tf_op jit(solution)/shard_map/gate/pallas_call | solution.py:230
  19.8 3.4 %collective-permute-start.1 = (bf16[128,128]{1,0:T(8,128)(2,1)S(1)}, bf16[128,128]{1,0:T(8,128)(2,1)S(1)}, u32[]{:S(2)}, u32[]{:S(2)}) collective-permute-start(bf16[128,128]{1,0:T(8,128)(2,1)S(1)} %get-tuple-element.14), channel_id=1, source_target_pairs={{0,8},{8,16},{16,24},{1,9},{9,17},{17,25},{2,10},{10,18},{18,26},{... | collective-permute-start | bytes 98312 | tf_op jit(solution)/shard_map/ppermute | solution.py:183
  26.5 15.5 %near.1 = (bf16[2048,1024]{1,0:T(8,128)(2,1)}, bf16[2048,1024]{1,0:T(8,128)(2,1)}) custom-call(bf16[2048,1024]{1,0:T(8,128)(2,1)} %copy-done, bf16[64,128,128]{2,1,0:T(8,128)(2,1)S(1)} %toeplitz.1.tile_ref, bf16[3,2048,1024]{2,1,0:T(8,128)(2,1)} %bitcast.21, bf16[3,2,1024]{2,1,0:T(2,128)(2,1)S(1)} %bitcast.13, f32[3,3,1024]{2,1,0:T(4,128)S(1)} %copy-done.1, ...), custom_call_target="tpu_custom_call" | custom-call | flops 2147483648 | bytes 16777216 | tf_op jit(solution)/shard_map/near/pallas_call | solution.py:246
  42.0 9.2 %mix.1 = (bf16[4,256,1024]{2,1,0:T(8,128)(2,1)S(1)}, bf16[4,256,1024]{2,1,0:T(8,128)(2,1)}) custom-call(s32[1]{0:T(128)} %bitcast.1.core_ref, bf16[2048,1024]{1,0:T(8,128)(2,1)} %get-tuple-element.12.near_ref, bf16[2048,1024]{1,0:T(8,128)(2,1)} %get-tuple-element.13.query_ref, bf16[128,128]{1,0:T(8,128)(2,1)S(1)} %collective-permute-done.1.rest_0_, ...), custom_call_target="tpu_custom_call" | custom-call | flops 536870912 | bytes 16777216 | tf_op jit(solution)/shard_map/mix/pallas_call | solution.py:276
  51.2 4.5 %collective-permute-done.4.other_ref = bf16[4,256,1024]{2,1,0:T(8,128)(2,1)} collective-permute-done((bf16[4,256,1024]{2,1,0:T(8,128)(2,1)}, bf16[4,256,1024]{2,1,0:T(8,128)(2,1)}, u32[]{:S(2)}, u32[]{:S(2)}) %collective-permute-start.4) | collective-permute-done | bytes 2097184 | tf_op jit(solution)/shard_map/ppermute | solution.py:293
  55.7 5.6 %product.21 = bf16[256,2048]{1,0:T(8,128)(2,1)S(1)} custom-call(s32[1]{0:T(128)} %bitcast.9.which_ref, bf16[4,256,1024]{2,1,0:T(8,128)(2,1)S(1)} %get-tuple-element.15.own_ref, bf16[4,256,1024]{2,1,0:T(8,128)(2,1)} %collective-permute-done.4.other_ref, bf16[1024,4096]{1,0:T(8,128)(2,1)} %own_w_ref.23, bf16[1024,4096]{1,0:T(8,128)(2,1)} %collective-permute-done.5.other_w_ref), custom_call_target="tpu_custom_call" | custom-call | flops 2147483648 | bytes 11534336 | tf_op jit(solution)/shard_map/product/pallas_call | solution.py:171
  64.3 5.6 %product.15 = bf16[256,2048]{1,0:T(8,128)(2,1)S(1)} custom-call(s32[1]{0:T(128)} %bitcast.9.which_ref, bf16[4,256,1024]{2,1,0:T(8,128)(2,1)S(1)} %get-tuple-element.15.own_ref, bf16[4,256,1024]{2,1,0:T(8,128)(2,1)} %collective-permute-done.4.other_ref, bf16[1024,4096]{1,0:T(8,128)(2,1)} %own_w_ref.23, bf16[1024,4096]{1,0:T(8,128)(2,1)} %collective-permute-done.5.other_w_ref), custom_call_target="tpu_custom_call" | custom-call | flops 2147483648 | bytes 11534336 | tf_op jit(solution)/shard_map/product/pallas_call | solution.py:171
  71.9 5.6 %product.23 = bf16[256,2048]{1,0:T(8,128)(2,1)S(1)} custom-call(s32[1]{0:T(128)} %bitcast.11.which_ref, bf16[4,256,1024]{2,1,0:T(8,128)(2,1)S(1)} %get-tuple-element.15.own_ref, bf16[4,256,1024]{2,1,0:T(8,128)(2,1)} %collective-permute-done.4.other_ref, bf16[1024,4096]{1,0:T(8,128)(2,1)} %own_w_ref.23, bf16[1024,4096]{1,0:T(8,128)(2,1)} %collective-permute-done.5.other_w_ref), custom_call_target="tpu_custom_call" | custom-call | flops 2147483648 | bytes 11534336 | tf_op jit(solution)/shard_map/product/pallas_call | solution.py:171
  77.5 5.6 %product.17 = bf16[256,2048]{1,0:T(8,128)(2,1)S(1)} custom-call(s32[1]{0:T(128)} %bitcast.11.which_ref, bf16[4,256,1024]{2,1,0:T(8,128)(2,1)S(1)} %get-tuple-element.15.own_ref, bf16[4,256,1024]{2,1,0:T(8,128)(2,1)} %collective-permute-done.4.other_ref, bf16[1024,4096]{1,0:T(8,128)(2,1)} %own_w_ref.23, bf16[1024,4096]{1,0:T(8,128)(2,1)} %collective-permute-done.5.other_w_ref), custom_call_target="tpu_custom_call" | custom-call | flops 2147483648 | bytes 11534336 | tf_op jit(solution)/shard_map/product/pallas_call | solution.py:171
  83.2 5.6 %product.22 = bf16[256,2048]{1,0:T(8,128)(2,1)S(1)} custom-call(s32[1]{0:T(128)} %bitcast.10.which_ref, bf16[4,256,1024]{2,1,0:T(8,128)(2,1)S(1)} %get-tuple-element.15.own_ref, bf16[4,256,1024]{2,1,0:T(8,128)(2,1)} %collective-permute-done.4.other_ref, bf16[1024,4096]{1,0:T(8,128)(2,1)} %own_w_ref.23, bf16[1024,4096]{1,0:T(8,128)(2,1)} %collective-permute-done.5.other_w_ref), custom_call_target="tpu_custom_call" | custom-call | flops 2147483648 | bytes 11534336 | tf_op jit(solution)/shard_map/product/pallas_call | solution.py:171
  88.8 5.7 %product.16 = bf16[256,2048]{1,0:T(8,128)(2,1)S(1)} custom-call(s32[1]{0:T(128)} %bitcast.10.which_ref, bf16[4,256,1024]{2,1,0:T(8,128)(2,1)S(1)} %get-tuple-element.15.own_ref, bf16[4,256,1024]{2,1,0:T(8,128)(2,1)} %collective-permute-done.4.other_ref, bf16[1024,4096]{1,0:T(8,128)(2,1)} %own_w_ref.23, bf16[1024,4096]{1,0:T(8,128)(2,1)} %collective-permute-done.5.other_w_ref), custom_call_target="tpu_custom_call" | custom-call | flops 2147483648 | bytes 11534336 | tf_op jit(solution)/shard_map/product/pallas_call | solution.py:171
  94.5 5.6 %product.20 = bf16[256,2048]{1,0:T(8,128)(2,1)S(1)} custom-call(s32[1]{0:T(128)} %bitcast.8.which_ref, bf16[4,256,1024]{2,1,0:T(8,128)(2,1)S(1)} %get-tuple-element.15.own_ref, bf16[4,256,1024]{2,1,0:T(8,128)(2,1)} %collective-permute-done.4.other_ref, bf16[1024,4096]{1,0:T(8,128)(2,1)} %own_w_ref.23, bf16[1024,4096]{1,0:T(8,128)(2,1)} %collective-permute-done.5.other_w_ref), custom_call_target="tpu_custom_call" | custom-call | flops 2147483648 | bytes 11534336 | tf_op jit(solution)/shard_map/product/pallas_call | solution.py:171
  100.1 5.6 %product.14 = bf16[256,2048]{1,0:T(8,128)(2,1)S(1)} custom-call(s32[1]{0:T(128)} %bitcast.8.which_ref, bf16[4,256,1024]{2,1,0:T(8,128)(2,1)S(1)} %get-tuple-element.15.own_ref, bf16[4,256,1024]{2,1,0:T(8,128)(2,1)} %collective-permute-done.4.other_ref, bf16[1024,4096]{1,0:T(8,128)(2,1)} %own_w_ref.23, bf16[1024,4096]{1,0:T(8,128)(2,1)} %collective-permute-done.5.other_w_ref), custom_call_target="tpu_custom_call" | custom-call | flops 2147483648 | bytes 11534336 | tf_op jit(solution)/shard_map/product/pallas_call | solution.py:171
  105.7 5.6 %product.19 = bf16[256,2048]{1,0:T(8,128)(2,1)S(1)} custom-call(s32[1]{0:T(128)} %bitcast.7.which_ref, bf16[4,256,1024]{2,1,0:T(8,128)(2,1)S(1)} %get-tuple-element.15.own_ref, bf16[4,256,1024]{2,1,0:T(8,128)(2,1)} %collective-permute-done.4.other_ref, bf16[1024,4096]{1,0:T(8,128)(2,1)} %own_w_ref.23, bf16[1024,4096]{1,0:T(8,128)(2,1)} %collective-permute-done.5.other_w_ref), custom_call_target="tpu_custom_call" | custom-call | flops 2147483648 | bytes 11534336 | tf_op jit(solution)/shard_map/product/pallas_call | solution.py:171
  111.4 5.6 %product.13 = bf16[256,2048]{1,0:T(8,128)(2,1)S(1)} custom-call(s32[1]{0:T(128)} %bitcast.7.which_ref, bf16[4,256,1024]{2,1,0:T(8,128)(2,1)S(1)} %get-tuple-element.15.own_ref, bf16[4,256,1024]{2,1,0:T(8,128)(2,1)} %collective-permute-done.4.other_ref, bf16[1024,4096]{1,0:T(8,128)(2,1)} %own_w_ref.23, bf16[1024,4096]{1,0:T(8,128)(2,1)} %collective-permute-done.5.other_w_ref), custom_call_target="tpu_custom_call" | custom-call | flops 2147483648 | bytes 11534336 | tf_op jit(solution)/shard_map/product/pallas_call | solution.py:171
  126.4 4.6 %collective-permute-start.10 = (bf16[256,2048]{1,0:T(8,128)(2,1)S(1)}, bf16[256,2048]{1,0:T(8,128)(2,1)S(1)}, u32[]{:S(2)}, u32[]{:S(2)}) collective-permute-start(bf16[256,2048]{1,0:T(8,128)(2,1)S(1)} %add_convert_fusion.7), channel_id=1, source_target_pairs={{6,4},{7,5},{4,2},{5,3},{14,12},{15,13},{12,10},{13,11},{22,20},{2... | collective-permute-start | bytes 3145736 | tf_op jit(solution)/shard_map/ppermute | solution.py:312
  132.7 15.8 %collective-permute-done.16 = bf16[256,2048]{1,0:T(8,128)(2,1)S(1)} collective-permute-done((bf16[256,2048]{1,0:T(8,128)(2,1)S(1)}, bf16[256,2048]{1,0:T(8,128)(2,1)S(1)}, u32[]{:S(2)}, u32[]{:S(2)}) %collective-permute-start.16) | collective-permute-done | bytes 1048608 | tf_op jit(solution)/shard_map/ppermute | solution.py:312
  152.8 4.5 %collective-permute-start.14 = (bf16[256,2048]{1,0:T(8,128)(2,1)}, bf16[256,2048]{1,0:T(8,128)(2,1)}, u32[]{:S(2)}, u32[]{:S(2)}) collective-permute-start(bf16[256,2048]{1,0:T(8,128)(2,1)} %add_convert_fusion.3), channel_id=1, source_target_pairs={{0,2},{1,3},{2,4},{3,5},{4,6},{5,7},{8,10},{9,11},{10,12},{11,13},... | collective-permute-start | bytes 3145736 | tf_op jit(solution)/shard_map/ppermute | solution.py:311
  157.3 13.7 %collective-permute-done.10 = bf16[256,2048]{1,0:T(8,128)(2,1)S(1)} collective-permute-done((bf16[256,2048]{1,0:T(8,128)(2,1)S(1)}, bf16[256,2048]{1,0:T(8,128)(2,1)S(1)}, u32[]{:S(2)}, u32[]{:S(2)}) %collective-permute-start.10) | collective-permute-done | bytes 1048608 | tf_op jit(solution)/shard_map/ppermute | solution.py:312
  175.6 4.9 %collective-permute-start.8 = (bf16[256,2048]{1,0:T(8,128)(2,1)}, bf16[256,2048]{1,0:T(8,128)(2,1)}, u32[]{:S(2)}, u32[]{:S(2)}) collective-permute-start(bf16[256,2048]{1,0:T(8,128)(2,1)} %add_convert_fusion.8), channel_id=1, source_target_pairs={{0,2},{1,3},{2,4},{3,5},{4,6},{5,7},{8,10},{9,11},{10,12},{11,13},... | collective-permute-start | bytes 3145736 | tf_op jit(solution)/shard_map/ppermute | solution.py:311
  180.5 5.6 %product.18 = bf16[256,2048]{1,0:T(8,128)(2,1)S(1)} custom-call(s32[1]{0:T(128)} %bitcast.which_ref, bf16[4,256,1024]{2,1,0:T(8,128)(2,1)S(1)} %get-tuple-element.15.own_ref, bf16[4,256,1024]{2,1,0:T(8,128)(2,1)} %collective-permute-done.4.other_ref, bf16[1024,4096]{1,0:T(8,128)(2,1)} %own_w_ref.23, bf16[1024,4096]{1,0:T(8,128)(2,1)} %collective-permute-done.5.other_w_ref), custom_call_target="tpu_custom_call" | custom-call | flops 2147483648 | bytes 11534336 | tf_op jit(solution)/shard_map/product/pallas_call | solution.py:171
  186.2 5.6 %product.12 = bf16[256,2048]{1,0:T(8,128)(2,1)S(1)} custom-call(s32[1]{0:T(128)} %bitcast.which_ref, bf16[4,256,1024]{2,1,0:T(8,128)(2,1)S(1)} %get-tuple-element.15.own_ref, bf16[4,256,1024]{2,1,0:T(8,128)(2,1)} %collective-permute-done.4.other_ref, bf16[1024,4096]{1,0:T(8,128)(2,1)} %own_w_ref.23, bf16[1024,4096]{1,0:T(8,128)(2,1)} %collective-permute-done.5.other_w_ref), custom_call_target="tpu_custom_call" | custom-call | flops 2147483648 | bytes 11534336 | tf_op jit(solution)/shard_map/product/pallas_call | solution.py:171
  198.6 16.6 %collective-permute-done.11 = bf16[256,2048]{1,0:T(8,128)(2,1)} collective-permute-done((bf16[256,2048]{1,0:T(8,128)(2,1)}, bf16[256,2048]{1,0:T(8,128)(2,1)}, u32[]{:S(2)}, u32[]{:S(2)}) %collective-permute-start.11) | collective-permute-done | bytes 1048608 | tf_op jit(solution)/shard_map/ppermute | solution.py:312
  (55 shorter events, 47.7 us)
Async XLA Ops:
  0.0 55.7 %collective-permute-start.5 = (bf16[1024,4096]{1,0:T(8,128)(2,1)}, bf16[1024,4096]{1,0:T(8,128)(2,1)}, u32[]{:S(2)}, u32[]{:S(2)}) collective-permute-start(bf16[1024,4096]{1,0:T(8,128)(2,1)} %own_w_ref.23), channel_id=1, source_target_pairs={{0,1},{1,0},{2,3},{3,2},{4,5},{5,4},{6,7},{7,6},{8,9},{9,8},{10,11... | collective-permute-start | bytes 25165832 | tf_op jit(solution)/shard_map/ppermute | solution.py:198
  0.8 7.1 %collective-permute-start = (bf16[2,3,1024]{2,0,1:T(2,128)(2,1)S(1)}, bf16[2,3,1024]{2,0,1:T(2,128)(2,1)S(1)}, u32[]{:S(2)}, u32[]{:S(2)}) collective-permute-start(bf16[2,3,1024]{2,0,1:T(2,128)(2,1)S(1)} %slice.3), channel_id=1, source_target_pairs={{0,8},{8,16},{16,24},{1,9},{9,17},{17,25},{2,10},{10,18},{18,26},{... | collective-permute-start | bytes 36872 | tf_op jit(solution)/shard_map/ppermute | solution.py:183
  6.1 1.8 copy-start.1
  7.9 18.6 %copy-start.2 = (f32[1024]{0:T(1024)S(1)}, f32[1024]{0:T(1024)}, u32[]{:S(2)}) copy-start(f32[1024]{0:T(1024)} %param.10) | copy-start | bytes 12292
  17.9 1.9 copy-start
  19.8 22.2 %collective-permute-start.1 = (bf16[128,128]{1,0:T(8,128)(2,1)S(1)}, bf16[128,128]{1,0:T(8,128)(2,1)S(1)}, u32[]{:S(2)}, u32[]{:S(2)}) collective-permute-start(bf16[128,128]{1,0:T(8,128)(2,1)S(1)} %get-tuple-element.14), channel_id=1, source_target_pairs={{0,8},{8,16},{16,24},{1,9},{9,17},{17,25},{2,10},{10,18},{18,26},{... | collective-permute-start | bytes 98312 | tf_op jit(solution)/shard_map/ppermute | solution.py:183
  23.2 18.8 %collective-permute-start.2 = (bf16[128,128]{1,0:T(8,128)(2,1)S(1)}, bf16[128,128]{1,0:T(8,128)(2,1)S(1)}, u32[]{:S(2)}, u32[]{:S(2)}) collective-permute-start(bf16[128,128]{1,0:T(8,128)(2,1)S(1)} %get-tuple-element.14), channel_id=1, source_target_pairs={{0,16},{8,24},{1,17},{9,25},{2,18},{10,26},{3,19},{11,27},{4,20},{... | collective-permute-start | bytes 98312 | tf_op jit(solution)/shard_map/ppermute | solution.py:183
  25.2 16.9 %collective-permute-start.3 = (bf16[128,128]{1,0:T(8,128)(2,1)S(1)}, bf16[128,128]{1,0:T(8,128)(2,1)S(1)}, u32[]{:S(2)}, u32[]{:S(2)}) collective-permute-start(bf16[128,128]{1,0:T(8,128)(2,1)S(1)} %get-tuple-element.14), channel_id=1, source_target_pairs={{0,24},{1,25},{2,26},{3,27},{4,28},{5,29},{6,30},{7,31}} | collective-permute-start | bytes 98312 | tf_op jit(solution)/shard_map/ppermute | solution.py:183
  51.2 4.5 %collective-permute-start.4 = (bf16[4,256,1024]{2,1,0:T(8,128)(2,1)}, bf16[4,256,1024]{2,1,0:T(8,128)(2,1)}, u32[]{:S(2)}, u32[]{:S(2)}) collective-permute-start(bf16[4,256,1024]{2,1,0:T(8,128)(2,1)} %get-tuple-element.16), channel_id=1, source_target_pairs={{0,1},{1,0},{2,3},{3,2},{4,5},{5,4},{6,7},{7,6},{8,9},{9,8},{10,11... | collective-permute-start | bytes 6291464 | tf_op jit(solution)/shard_map/ppermute | solution.py:293
  61.3 55.7 %collective-permute-start.15 = (bf16[256,2048]{1,0:T(8,128)(2,1)S(1)}, bf16[256,2048]{1,0:T(8,128)(2,1)}, u32[]{:S(2)}, u32[]{:S(2)}) collective-permute-start(bf16[256,2048]{1,0:T(8,128)(2,1)S(1)} %product.21), channel_id=1, source_target_pairs={{6,4},{7,5},{14,12},{15,13},{22,20},{23,21},{30,28},{31,29}} | collective-permute-start | bytes 3145736 | tf_op jit(solution)/shard_map/ppermute | solution.py:312
  62.6 59.2 %collective-permute-start.12 = (bf16[256,2048]{1,0:T(8,128)(2,1)S(1)}, bf16[256,2048]{1,0:T(8,128)(2,1)}, u32[]{:S(2)}, u32[]{:S(2)}) collective-permute-start(bf16[256,2048]{1,0:T(8,128)(2,1)S(1)} %product.21), channel_id=1, source_target_pairs={{0,2},{1,3},{8,10},{9,11},{16,18},{17,19},{24,26},{25,27}} | collective-permute-start | bytes 3145736 | tf_op jit(solution)/shard_map/ppermute | solution.py:311
  69.9 54.9 %collective-permute-start.9 = (bf16[256,2048]{1,0:T(8,128)(2,1)S(1)}, bf16[256,2048]{1,0:T(8,128)(2,1)}, u32[]{:S(2)}, u32[]{:S(2)}) collective-permute-start(bf16[256,2048]{1,0:T(8,128)(2,1)S(1)} %product.15), channel_id=1, source_target_pairs={{6,4},{7,5},{14,12},{15,13},{22,20},{23,21},{30,28},{31,29}} | collective-permute-start | bytes 3145736 | tf_op jit(solution)/shard_map/ppermute | solution.py:312
  71.2 59.8 %collective-permute-start.6 = (bf16[256,2048]{1,0:T(8,128)(2,1)S(1)}, bf16[256,2048]{1,0:T(8,128)(2,1)S(1)}, u32[]{:S(2)}, u32[]{:S(2)}) collective-permute-start(bf16[256,2048]{1,0:T(8,128)(2,1)S(1)} %product.15), channel_id=1, source_target_pairs={{0,2},{1,3},{8,10},{9,11},{16,18},{17,19},{24,26},{25,27}} | collective-permute-start | bytes 3145736 | tf_op jit(solution)/shard_map/ppermute | solution.py:311
  118.6 29.9 %collective-permute-start.16 = (bf16[256,2048]{1,0:T(8,128)(2,1)S(1)}, bf16[256,2048]{1,0:T(8,128)(2,1)S(1)}, u32[]{:S(2)}, u32[]{:S(2)}) collective-permute-start(bf16[256,2048]{1,0:T(8,128)(2,1)S(1)} %add_convert_fusion.2), channel_id=1, source_target_pairs={{6,4},{7,5},{4,2},{5,3},{14,12},{15,13},{12,10},{13,11},{22,20},{2... | collective-permute-start | bytes 3145736 | tf_op jit(solution)/shard_map/ppermute | solution.py:312
  123.5 27.9 %collective-permute-start.13 = (bf16[256,2048]{1,0:T(8,128)(2,1)S(1)}, bf16[256,2048]{1,0:T(8,128)(2,1)S(1)}, u32[]{:S(2)}, u32[]{:S(2)}) collective-permute-start(bf16[256,2048]{1,0:T(8,128)(2,1)S(1)} %add_convert_fusion.4), channel_id=1, source_target_pairs={{0,2},{1,3},{2,4},{3,5},{8,10},{9,11},{10,12},{11,13},{16,18},{17,... | collective-permute-start | bytes 3145736 | tf_op jit(solution)/shard_map/ppermute | solution.py:311
  126.4 44.5 %collective-permute-start.10 = (bf16[256,2048]{1,0:T(8,128)(2,1)S(1)}, bf16[256,2048]{1,0:T(8,128)(2,1)S(1)}, u32[]{:S(2)}, u32[]{:S(2)}) collective-permute-start(bf16[256,2048]{1,0:T(8,128)(2,1)S(1)} %add_convert_fusion.7), channel_id=1, source_target_pairs={{6,4},{7,5},{4,2},{5,3},{14,12},{15,13},{12,10},{13,11},{22,20},{2... | collective-permute-start | bytes 3145736 | tf_op jit(solution)/shard_map/ppermute | solution.py:312
  131.4 42.9 %collective-permute-start.7 = (bf16[256,2048]{1,0:T(8,128)(2,1)S(1)}, bf16[256,2048]{1,0:T(8,128)(2,1)S(1)}, u32[]{:S(2)}, u32[]{:S(2)}) collective-permute-start(bf16[256,2048]{1,0:T(8,128)(2,1)S(1)} %add_convert_fusion.9), channel_id=1, source_target_pairs={{0,2},{1,3},{2,4},{3,5},{8,10},{9,11},{10,12},{11,13},{16,18},{17,... | collective-permute-start | bytes 3145736 | tf_op jit(solution)/shard_map/ppermute | solution.py:311
  148.9 44.6 %collective-permute-start.17 = (bf16[256,2048]{1,0:T(8,128)(2,1)S(1)}, bf16[256,2048]{1,0:T(8,128)(2,1)}, u32[]{:S(2)}, u32[]{:S(2)}) collective-permute-start(bf16[256,2048]{1,0:T(8,128)(2,1)S(1)} %add_convert_fusion.1), channel_id=1, source_target_pairs={{6,4},{7,5},{4,2},{5,3},{2,0},{3,1},{14,12},{15,13},{12,10},{13,11... | collective-permute-start | bytes 3145736 | tf_op jit(solution)/shard_map/ppermute | solution.py:312
  152.8 43.7 %collective-permute-start.14 = (bf16[256,2048]{1,0:T(8,128)(2,1)}, bf16[256,2048]{1,0:T(8,128)(2,1)}, u32[]{:S(2)}, u32[]{:S(2)}) collective-permute-start(bf16[256,2048]{1,0:T(8,128)(2,1)} %add_convert_fusion.3), channel_id=1, source_target_pairs={{0,2},{1,3},{2,4},{3,5},{4,6},{5,7},{8,10},{9,11},{10,12},{11,13},... | collective-permute-start | bytes 3145736 | tf_op jit(solution)/shard_map/ppermute | solution.py:311
  172.4 42.9 %collective-permute-start.11 = (bf16[256,2048]{1,0:T(8,128)(2,1)}, bf16[256,2048]{1,0:T(8,128)(2,1)}, u32[]{:S(2)}, u32[]{:S(2)}) collective-permute-start(bf16[256,2048]{1,0:T(8,128)(2,1)} %add_convert_fusion.6), channel_id=1, source_target_pairs={{6,4},{7,5},{4,2},{5,3},{2,0},{3,1},{14,12},{15,13},{12,10},{13,11... | collective-permute-start | bytes 3145736 | tf_op jit(solution)/shard_map/ppermute | solution.py:312
  175.6 42.2 %collective-permute-start.8 = (bf16[256,2048]{1,0:T(8,128)(2,1)}, bf16[256,2048]{1,0:T(8,128)(2,1)}, u32[]{:S(2)}, u32[]{:S(2)}) collective-permute-start(bf16[256,2048]{1,0:T(8,128)(2,1)} %add_convert_fusion.8), channel_id=1, source_target_pairs={{0,2},{1,3},{2,4},{3,5},{4,6},{5,7},{8,10},{9,11},{10,12},{11,13},... | collective-permute-start | bytes 3145736 | tf_op jit(solution)/shard_map/ppermute | solution.py:311

commit v2 on v1

v2 whole, which is shorter than its diff:
```python
import functools

import jax
import jax.numpy as jnp
from jax import lax
from jax.experimental import pallas as pl
from jax.experimental.pallas import tpu as pltpu
from jax.sharding import PartitionSpec as P

LANES = 128
CHUNK = 128
BF16 = jnp.bfloat16
F32 = jnp.float32


def params(mib=48):
    return pltpu.CompilerParams(vmem_limit_bytes=mib << 20)


def cost(flops, moved):
    return pl.CostEstimate(flops=int(flops) // 64, bytes_accessed=int(moved) // 64, transcendentals=0)


def iota(shape, dim):
    return lax.broadcasted_iota(jnp.int32, shape, dim)


def toeplitz_kernel(modes, rate_ref, scale_ref, tile_ref):
    filters = LANES // modes
    reach = iota((LANES, CHUNK), 1).astype(F32)
    terms = scale_ref[...] * jnp.exp(-rate_ref[...] * reach)
    taps = terms.reshape(filters, modes, CHUNK).sum(axis=1)
    keep = iota((CHUNK, CHUNK), 0) <= iota((CHUNK, CHUNK), 1)
    for f in range(filters):
        rows = jnp.broadcast_to(taps[f : f + 1], (CHUNK, CHUNK))
        rolled = pltpu.roll(rows, 0, 1, stride=1, stride_axis=0)
        tile_ref[f] = jnp.where(keep, rolled, 0.0).astype(BF16)


def short_conv(stream, stage_ref, x_ref, rim_ref, taps_ref, k):
    at = 8 + k * CHUNK
    return (
        taps_ref[0, stream : stream + 1, :] * stage_ref[at : at + CHUNK, :]
        + taps_ref[1, stream : stream + 1, :] * stage_ref[at - 1 : at - 1 + CHUNK, :]
        + taps_ref[2, stream : stream + 1, :] * stage_ref[at - 2 : at - 2 + CHUNK, :]
    )


def stage(stream, stage_ref, x_ref, rim_ref):
    stage_ref[0:8, :] = jnp.zeros((8, LANES), F32)
    stage_ref[6:8, :] = rim_ref[stream].astype(F32)
    stage_ref[8:, :] = x_ref[0].astype(F32)


def diagonal(modes, group):
    return (iota((LANES, LANES), 0) // modes) == (iota((LANES, LANES), 1) // group)


def dot(a, b, dims=((1,), (0,))):
    return lax.dot_general(a, b, (dims, ((), ())), preferred_element_type=F32)


def gate_kernel(
    modes, group, k_ref, v_ref, rim_ref, taps_ref, rate_ref, gated_ref, start_ref, state_ref, k_stage, v_stage
):
    stage(1, k_stage, k_ref, rim_ref)
    stage(2, v_stage, v_ref, rim_ref)
    rate = rate_ref[...]
    ends = jnp.exp(-rate * (CHUNK - 1 - iota((LANES, CHUNK), 1)).astype(F32)).astype(BF16)
    fade = jnp.exp(-rate * CHUNK)
    state = jnp.zeros((LANES, LANES), F32)
    chunks = gated_ref.shape[0] // CHUNK
    per_block = chunks // start_ref.shape[0]
    own_modes = diagonal(modes, group)
    spots = (iota((group, LANES), 0) == lax.rem(iota((group, LANES), 1), group)).astype(BF16)
    fold = lambda value: dot(spots, jnp.where(own_modes, value, 0.0).astype(BF16), ((1,), (1,))).astype(BF16)
    for k in range(chunks):
        if k % per_block == 0:
            start_ref[k // per_block] = fold(state)
        gated = (
            short_conv(1, k_stage, k_ref, rim_ref, taps_ref, k) * short_conv(2, v_stage, v_ref, rim_ref, taps_ref, k)
        ).astype(BF16)
        gated_ref[k * CHUNK : (k + 1) * CHUNK, :] = gated
        state = fade * state + dot(ends, gated)
    state_ref[...] = fold(state)


def spread(modes, group, folded):
    return jnp.where(diagonal(group, modes), jnp.concatenate([folded] * (LANES // group), axis=0), 0.0)


def near_kernel(
    modes,
    group,
    window_ref,
    gated_ref,
    start_ref,
    tile_ref,
    q_ref,
    before_ref,
    rim_ref,
    taps_ref,
    gain_ref,
    row_rate_ref,
    row_scale_ref,
    *rest,
):
    near_ref, query_ref, q_stage, sources, sums = rest[-5:]

    stage(0, q_stage, q_ref, rim_ref)

    @pl.when(window_ref[0] > 0)
    def _():
        q_stage[6:8, :] = before_ref[0].astype(F32)[before_ref.shape[1] - 2 :]

    filters = LANES // group
    chunks = gated_ref.shape[0] // CHUNK
    eye = (iota((CHUNK, CHUNK), 0) == iota((CHUNK, CHUNK), 1)).astype(BF16)
    for k in range(0, chunks, 2):
        turned = dot(eye, gated_ref[k * CHUNK : (k + 2) * CHUNK, :], ((1,), (1,))).astype(BF16)
        sources[k] = turned[:, :CHUNK]
        sources[k + 1] = turned[:, CHUNK:]
    for f in range(filters):
        rows = slice(f * group, (f + 1) * group)
        block = sources[:, rows, :].reshape(chunks * group, CHUNK)
        sums[:, rows, :] = dot(block, tile_ref[f]).astype(BF16).reshape(chunks, group, CHUNK)
    row_rate = row_rate_ref[0]
    ends = jnp.exp(-row_rate * (CHUNK - 1 - iota((CHUNK, LANES), 0)).astype(F32)).astype(BF16)
    reads = (row_scale_ref[0] * jnp.exp(-row_rate * (iota((CHUNK, LANES), 0) + 1).astype(F32))).astype(BF16)
    both = jnp.concatenate([eye, reads], axis=1)
    fade = jnp.exp(-row_rate * CHUNK)
    own_modes = diagonal(group, modes)
    gain = gain_ref[...]
    state = spread(modes, group, start_ref[0].astype(F32))
    for k in range(chunks):
        rows = slice(k * CHUNK, (k + 1) * CHUNK)
        summed = dot(both, jnp.concatenate([sums[k], state.astype(BF16)], axis=1), ((1,), (1,)))
        state = fade * state + jnp.where(own_modes, dot(sources[k], ends), 0.0)
        near_ref[rows, :] = (summed + gain * gated_ref[rows, :].astype(F32)).astype(BF16)
        query_ref[rows, :] = short_conv(0, q_stage, q_ref, rim_ref, taps_ref, k).astype(BF16)


def mix_kernel(modes, group, tok_rows, size, where_ref, near_ref, query_ref, *rest):
    *piece_refs, row_rate_ref, row_scale_ref, keep_ref, give_ref, mixed_ref = rest
    core = where_ref[0]
    first = (where_ref[1] * near_ref.shape[0]).astype(F32)
    row_rate = row_rate_ref[0]
    carried = jnp.zeros((group, LANES), F32)
    for d, piece_ref in enumerate(piece_refs):
        carried = carried + jnp.exp(-row_rate * float(d * tok_rows)) * piece_ref[...].astype(F32)
    state = spread(modes, group, carried).astype(BF16)
    reads = row_scale_ref[0] * jnp.exp(-row_rate * (iota((CHUNK, LANES), 0) + 1).astype(F32))
    for k in range(near_ref.shape[0] // CHUNK):
        rows = slice(k * CHUNK, (k + 1) * CHUNK)
        fade = jnp.exp(-row_rate * (first + float(k * CHUNK)))
        far = dot((reads * fade).astype(BF16), state, ((1,), (1,)))
        mixed = (query_ref[rows, :].astype(F32) * (near_ref[rows, :].astype(F32) + far)).astype(BF16)
        width = min(size, CHUNK)
        for piece in range(0, CHUNK, width):
            block, inner = divmod(k * CHUNK + piece, size)
            side = lax.rem(core + block, 2)
            mixed_ref[side, block // 2, inner : inner + width, :] = mixed[piece : piece + width]
    keep_ref[...] = mixed_ref[0]
    give_ref[...] = mixed_ref[1]


def product_kernel(which_ref, own_ref, other_ref, own_w_ref, other_w_ref, out_ref):
    out_ref[...] = (dot(own_ref[0], own_w_ref[...]) + dot(other_ref[0], other_w_ref[...])).astype(BF16)


def product(which, own, other, own_w, other_w, part, split, other_which=None):
    _, rows, depth = own.shape
    width = own_w.shape[1] // split
    tile = min(1024, width)
    steps = width // tile
    grid_spec = pltpu.PrefetchScalarGridSpec(
        num_scalar_prefetch=1,
        grid=(steps,),
        in_specs=[
            pl.BlockSpec((1, rows, depth), lambda j, which: (which[0], 0, 0)),
            pl.BlockSpec((1, rows, depth), lambda j, which: (which[1], 0, 0)),
            pl.BlockSpec((depth, tile), lambda j, which: (0, part * steps + j)),
            pl.BlockSpec((depth, tile), lambda j, which: (0, part * steps + j)),
        ],
        out_specs=pl.BlockSpec((rows, tile), lambda j, which: (0, j)),
    )
    return pl.pallas_call(
        product_kernel,
        grid_spec=grid_spec,
        out_shape=jax.ShapeDtypeStruct((rows, width), BF16),
        compiler_params=params(),
        cost_estimate=cost(4 * rows * depth * width, 4 * depth * width + 6 * rows * width),
        name="product",
    )(jnp.stack([which, which if other_which is None else other_which]).astype(jnp.int32), own, other, own_w, other_w)


def shifted(value, axis, steps):
    count = lax.axis_size(axis)
    return lax.ppermute(value, axis, [(i, i + steps) for i in range(count - steps)])


def tie(*values):
    return lax.optimization_barrier(values)


def add(*values):
    total = values[0].astype(F32)
    for value in values[1:]:
        total = total + value.astype(F32)
    return total.astype(BF16)


def pairs(hops):
    return [(2 * i + c, 2 * j + c) for i, j in hops for c in (0, 1)]


def sum_over_line(place, keep, other, out_weight, other_weight):
    parts = keep.shape[0]
    split = 2
    last = parts - 1
    multiply = lambda which, j: product(jnp.clip(which, 0, last), keep, other, out_weight, other_weight, j, split)
    up = [None] * split
    down = [None] * split
    for s in range(1, parts):
        senders = range(0, min(s, last))
        up_pairs = [(2 * i + c, 2 * i + 2 + c) for i in senders for c in (0, 1)]
        down_pairs = [(2 * (last - i) + c, 2 * (last - i) - 2 + c) for i in senders for c in (0, 1)]
        for j in range(split):
            if s == 1:
                first = multiply(jnp.where(place == 0, last, 0), j)
                up[j], down[j] = first, first
            else:
                up[j] = (multiply(parts - s + place, j).astype(F32) + up[j].astype(F32)).astype(BF16)
                down[j] = (multiply(s - parts + place, j).astype(F32) + down[j].astype(F32)).astype(BF16)
            up[j] = lax.ppermute(up[j], "chan", up_pairs)
            down[j] = lax.ppermute(down[j], "chan", down_pairs)
    outs = [
        (multiply(place, j).astype(F32) + up[j].astype(F32) + down[j].astype(F32)).astype(BF16) for j in range(split)
    ]
    return jnp.concatenate(outs, axis=1)


def on_device(featurized, short_filter, decay_rate, residue, skip_gain, out_weight):
    tok_rows, streams, channels = featurized.shape
    filters, modes = decay_rate.shape
    group = channels // filters
    blocks = channels // LANES
    ctx_count = lax.axis_size("ctx")
    parts = lax.axis_size("chan") // 2
    chan_index = lax.axis_index("chan")
    place, core = chan_index // 2, chan_index % 2
    swap = [(i, i ^ 1) for i in range(2 * parts)]

    rim = shifted(featurized[tok_rows - 2 :], "ctx", 1).transpose(1, 0, 2)
    other_weight = lax.ppermute(out_weight, "chan", swap)
    features = featurized.transpose(1, 0, 2)
    scaled = residue * jnp.sqrt(-jnp.expm1(-2.0 * decay_rate))
    rate_cols = jnp.broadcast_to(decay_rate.reshape(-1, 1), (filters * modes, LANES))
    scale_cols = jnp.broadcast_to(scaled.reshape(-1, 1), (filters * modes, LANES))
    rate_rows = decay_rate.reshape(blocks, 1, LANES)
    scale_rows = scaled.reshape(blocks, 1, LANES)
    per_block = LANES // group

    square = pl.BlockSpec((LANES, LANES), lambda g: (g, 0))
    tile_spec = pl.BlockSpec((per_block, CHUNK, CHUNK), lambda g: (g, 0, 0))
    lanes_spec = pl.BlockSpec((tok_rows, LANES), lambda g: (0, g))
    rim_spec = pl.BlockSpec((streams, 2, LANES), lambda g: (0, 0, g))
    taps_spec = pl.BlockSpec((3, streams, LANES), lambda g: (0, 0, g))
    state_spec = pl.BlockSpec((group, LANES), lambda g: (g, 0))

    def stream_spec(i):
        return pl.BlockSpec((1, tok_rows, LANES), lambda g: (i, 0, g))

    tiles = pl.pallas_call(
        functools.partial(toeplitz_kernel, modes),
        grid=(blocks,),
        in_specs=[square, square],
        out_specs=tile_spec,
        out_shape=jax.ShapeDtypeStruct((filters, CHUNK, CHUNK), BF16),
        compiler_params=params(),
        cost_estimate=cost(filters * CHUNK * CHUNK * 40, filters * CHUNK * CHUNK * 4),
        name="toeplitz",
    )(rate_cols, scale_cols)

    stage_shape = pltpu.VMEM((8 + tok_rows, LANES), F32)
    wide = jax.ShapeDtypeStruct((tok_rows, channels), BF16)
    gated, starts, state = pl.pallas_call(
        functools.partial(gate_kernel, modes, group),
        grid=(blocks,),
        in_specs=[stream_spec(1), stream_spec(2), rim_spec, taps_spec, square],
        out_specs=[lanes_spec, pl.BlockSpec((parts, group, LANES), lambda g: (0, g, 0)), state_spec],
        out_shape=[
            wide,
            jax.ShapeDtypeStruct((parts, blocks * group, LANES), BF16),
            jax.ShapeDtypeStruct((blocks * group, LANES), BF16),
        ],
        scratch_shapes=[stage_shape, stage_shape],
        compiler_params=params(),
        cost_estimate=cost(tok_rows * channels * 256, tok_rows * channels * 6),
        name="gate",
    )(features, features, rim, short_filter, rate_cols)

    pieces = [shifted(state, "ctx", d) for d in range(1, ctx_count)]

    row_spec = pl.BlockSpec((1, 1, LANES), lambda g, at: (g, 0, 0))
    size = tok_rows // (2 * parts)
    tail = 16

    def convolve(source, window, rows, *earlier):
        spans = rows // tail
        window_spec = pl.BlockSpec((rows, LANES), lambda g, at: (at[0], g))
        return pl.pallas_call(
            functools.partial(near_kernel, modes, group),
            grid_spec=pltpu.PrefetchScalarGridSpec(
                num_scalar_prefetch=1,
                grid=(blocks,),
                in_specs=[
                    window_spec,
                    pl.BlockSpec((1, group, LANES), lambda g, at: (at[0], g, 0)),
                    pl.BlockSpec((per_block, CHUNK, CHUNK), lambda g, at: (g, 0, 0)),
                    pl.BlockSpec((1, rows, LANES), lambda g, at: (0, at[0], g)),
                    pl.BlockSpec((1, tail, LANES), lambda g, at: (0, jnp.maximum(at[0] * spans - 1, 0), g)),
                    pl.BlockSpec((streams, 2, LANES), lambda g, at: (0, 0, g)),
                    pl.BlockSpec((3, streams, LANES), lambda g, at: (0, 0, g)),
                    pl.BlockSpec((1, LANES), lambda g, at: (0, g)),
                    row_spec,
                    row_spec,
                ]
                + [pl.BlockSpec(memory_space=pl.ANY)] * len(earlier),
                out_specs=[pl.BlockSpec((rows, LANES), lambda g, at: (0, g))] * 2,
                scratch_shapes=[
                    pltpu.VMEM((8 + rows, LANES), F32),
                    pltpu.VMEM((rows // CHUNK, LANES, CHUNK), BF16),
                    pltpu.VMEM((rows // CHUNK, LANES, CHUNK), BF16),
                ],
            ),
            out_shape=[jax.ShapeDtypeStruct((rows, channels), BF16)] * 2,
            compiler_params=params(),
            cost_estimate=cost(rows * channels * 1024, rows * channels * 8),
            name="near",
        )(
            window.reshape(1).astype(jnp.int32),
            source,
            starts,
            tiles,
            features,
            features,
            rim,
            short_filter,
            skip_gain.reshape(1, channels),
            rate_rows,
            scale_rows,
            *earlier,
        )

    def finish(near, query, window):
        rows = near.shape[0]
        held = rows // (2 * size)
        out_spec = pl.BlockSpec((held, size, LANES), lambda g, at: (0, 0, g))
        return pl.pallas_call(
            functools.partial(mix_kernel, modes, group, tok_rows, size),
            grid_spec=pltpu.PrefetchScalarGridSpec(
                num_scalar_prefetch=1,
                grid=(blocks,),
                in_specs=[pl.BlockSpec((rows, LANES), lambda g, at: (0, g))] * 2
                + [pl.BlockSpec((group, LANES), lambda g, at: (g, 0))] * len(pieces)
                + [row_spec, row_spec],
                out_specs=[out_spec, out_spec],
                scratch_shapes=[pltpu.VMEM((2, held, size, LANES), BF16)],
            ),
            out_shape=[jax.ShapeDtypeStruct((held, size, channels), BF16)] * 2,
            compiler_params=params(),
            cost_estimate=cost(rows * channels * 256, rows * channels * 8),
            name="mix",
        )(jnp.stack([core, window]).astype(jnp.int32), near, query, *pieces, rate_rows, scale_rows)

    nothing = core * 0
    if parts != 4:
        keep, give = finish(*convolve(gated, nothing, tok_rows), nothing)
        return sum_over_line(place, keep, lax.ppermute(give, "chan", swap), out_weight, other_weight)

    far, far_inner = jnp.where(place < 2, 3, 0), jnp.where(place < 2, 2, 1)
    close, close_inner = 3 - far, 3 - far_inner
    at_end = (place == 0) | (place == 3)
    inward, across, outward = pairs([(0, 1), (3, 2)]), pairs([(1, 2), (2, 1)]), pairs([(1, 0), (2, 3)])
    send = lambda value, hops: lax.ppermute(value, "chan", hops)

    keep, give = finish(*convolve(gated, far, tok_rows // parts), far)
    other = send(give, swap)
    first = product(nothing, keep, other, out_weight, other_weight, 0, 1)
    from_end = send(first, inward)

    keep, give = finish(*convolve(gated, nothing, tok_rows, first), nothing)
    swapped = lambda which: send(lax.dynamic_slice_in_dim(give, which, 1, 0), swap)
    multiply = lambda which, other: product(which, keep, other, out_weight, other_weight, 0, 1, nothing)
    half = out_weight.shape[1] // 2
    halves = lambda value: (value[:, :half], value[:, half:])
    second = multiply(far_inner, swapped(far_inner))
    through = send(second, inward)
    crossed = [send(value, across) for value in halves(add(first, from_end))]
    which = jnp.where(at_end, close_inner, close)
    third = multiply(which, swapped(which))
    last = send(add(third, jnp.concatenate(crossed, axis=1)), inward + outward)
    inner = [send(value, across) for value in halves(add(second, through))]
    own = multiply(place, swapped(place))
    return add(own, last, jnp.concatenate(inner, axis=1))


def solution(mesh):
    return jax.shard_map(
        on_device,
        mesh=mesh,
        in_specs=(
            P("ctx", None, "chan"),
            P(None, None, "chan"),
            P("chan", None),
            P("chan", None),
            P("chan"),
            P("chan", None),
        ),
        out_specs=P(("ctx", "chan"), None),
        check_vma=False,
    )
```

time: 223 us -> 208 us (0.933)
  waiting for transfers between devices: 58.5 us -> 80.2 us
  Pallas kernels: 103 us -> 85.8 us
  starting transfers between devices: 38.6 us -> 27 us
  other arithmetic: 16.3 us -> 7.96 us
    pallas_call x12 -> x4, Pallas kernels: 67.4 us -> 37.3 us  [product(): pl.pallas_call(product_kernel, grid_spec=grid_spec, out_shape=jax.ShapeDt...]
    ppermute x13 -> x11, waiting for transfers between devices: 58.5 us -> 80.2 us  [on_device(): send = lambda value, hops: lax.ppermute(value, 'chan', hops)]
    ppermute x13 -> x11, starting transfers between devices: 28.5 us -> 14.7 us  [on_device(): send = lambda value, hops: lax.ppermute(value, 'chan', hops)]
    pallas_call x2 -> x4, Pallas kernels: 24.7 us -> 36.5 us  [the longest x2 23.8 us: convolve(): pl.pallas_call(functools.partial(near_kernel, modes, group), grid_spec=pl...]
    convert_element_type x10 -> x4, other arithmetic: 14.1 us -> 6.92 us  [add(): return total.astype(BF16)]
  transfers between devices with their start and end apart: 18 -> 16, of which waited for: 8 -> 9; matrix products, arithmetic and copies ran while one was open for 7% -> 4% of each run, Pallas kernels for 44% -> 37%
where the time goes in v2:
time: 208 us; the launch traced here: 207 us
  Pallas kernels  85.8 us (41%)
  waiting for transfers between devices  80.2 us (39%)
  starting transfers between devices  27 us (13%)
  other arithmetic  7.96 us (4%)
  local copies, waits for them, and re-layouts  5.76 us (3%)
    ppermute x11, waiting for transfers between devices, on_device(): send = lambda value, hops: lax.ppermute(value, 'chan', hops)  80.2 us
    pallas_call x4, Pallas kernels, product(): pl.pallas_call(product_kernel, grid_spec=grid_spec, out_shape=jax.ShapeDt...  37.3 us
    pallas_call x2, Pallas kernels, convolve(): pl.pallas_call(functools.partial(near_kernel, modes, group), grid_spec=pl...  23.8 us
    ppermute x11, starting transfers between devices, on_device(): send = lambda value, hops: lax.ppermute(value, 'chan', hops)  14.7 us
    pallas_call x2, Pallas kernels, finish(): pl.pallas_call(functools.partial(mix_kernel, modes, group, tok_rows, size...  12.6 us
    ppermute x4, starting transfers between devices, shifted(): lax.ppermute(value, axis, [(i, i + steps) for i in range(count - steps)])  12.2 us
    pallas_call x1, Pallas kernels, on_device(): pl.pallas_call(functools.partial(gate_kernel, modes, group), grid=(blocks...  10.7 us
    convert_element_type x4, other arithmetic, add(): return total.astype(BF16)  6.92 us
  transfers between devices with their start and end apart: 16, of which 9 were waited for; matrix products, arithmetic and copies ran while one was open for 4% of the time, Pallas kernels for 37%

profile of v2, /device:TPU:16, one launch (start us, length us, event | category | flops | bytes accessed | tf_op | source)
XLA Modules:
  0.0 207.1 jit_solution(3949415068410039442)
XLA Ops:
  0.8 3.4 %collective-permute-start = (bf16[2,3,1024]{2,0,1:T(2,128)(2,1)S(1)}, bf16[2,3,1024]{2,0,1:T(2,128)(2,1)S(1)}, u32[]{:S(2)}, u32[]{:S(2)}) collective-permute-start(bf16[2,3,1024]{2,0,1:T(2,128)(2,1)S(1)} %slice.15), channel_id=1, source_target_pairs={{0,8},{8,16},{16,24},{1,9},{9,17},{17,25},{2,10},{10,18},{18,26},{... | collective-permute-start | bytes 36872 | tf_op jit(solution)/shard_map/ppermute | solution.py:199
  6.8 10.7 %gate.1 = (bf16[2048,1024]{1,0:T(8,128)(2,1)S(1)}, bf16[4,128,128]{2,1,0:T(8,128)(2,1)S(1)}, bf16[128,128]{1,0:T(8,128)(2,1)S(1)}) custom-call(bf16[3,2048,1024]{2,1,0:T(8,128)(2,1)} %bitcast.23, bf16[3,2048,1024]{2,1,0:T(8,128)(2,1)} %bitcast.24, bf16[3,2,1024]{2,1,0:T(2,128)(2,1)S(1)} %bitcast.10, f32[3,3,1024]{2,1,0:T(4,128)S(1)} %copy-done.1, ...), custom_call_target="tpu_custom_call" | custom-call | flops 8388608 | bytes 196608 | tf_op jit(solution)/shard_map/gate/pallas_call | solution.py:287
  17.5 2.0 copy-done
  19.5 4.1 %collective-permute-start.1 = (bf16[128,128]{1,0:T(8,128)(2,1)S(1)}, bf16[128,128]{1,0:T(8,128)(2,1)S(1)}, u32[]{:S(2)}, u32[]{:S(2)}) collective-permute-start(bf16[128,128]{1,0:T(8,128)(2,1)S(1)} %get-tuple-element.20), channel_id=1, source_target_pairs={{0,8},{8,16},{16,24},{1,9},{9,17},{17,25},{2,10},{10,18},{18,26},{... | collective-permute-start | bytes 98312 | tf_op jit(solution)/shard_map/ppermute | solution.py:199
  23.6 3.4 %collective-permute-start.2 = (bf16[128,128]{1,0:T(8,128)(2,1)S(1)}, bf16[128,128]{1,0:T(8,128)(2,1)S(1)}, u32[]{:S(2)}, u32[]{:S(2)}) collective-permute-start(bf16[128,128]{1,0:T(8,128)(2,1)S(1)} %get-tuple-element.20), channel_id=1, source_target_pairs={{0,16},{8,24},{1,17},{9,25},{2,18},{10,26},{3,19},{11,27},{4,20},{... | collective-permute-start | bytes 98312 | tf_op jit(solution)/shard_map/ppermute | solution.py:199
  30.3 7.9 %near.2 = (bf16[512,1024]{1,0:T(8,128)(2,1)S(1)}, bf16[512,1024]{1,0:T(8,128)(2,1)S(1)}) custom-call(s32[1]{0:T(128)} %bitcast.7.window_ref, bf16[2048,1024]{1,0:T(8,128)(2,1)} %copy-done, bf16[4,128,128]{2,1,0:T(8,128)(2,1)S(1)} %get-tuple-element.17.start_ref, bf16[64,128,128]{2,1,0:T(8,128)(2,1)S(1)} %toeplitz.1.tile_ref, ...), custom_call_target="tpu_custom_call" | custom-call | flops 8388608 | bytes 65536 | tf_op jit(solution)/shard_map/near/pallas_call | solution.py:312
  38.3 3.5 %mix.2 = (bf16[1,256,1024]{2,1,0:T(8,128)(2,1)S(1)}, bf16[1,256,1024]{2,1,0:T(8,128)(2,1)S(1)}) custom-call(s32[2]{0:T(128)S(1)} %get-tuple-element.35.where_ref, bf16[512,1024]{1,0:T(8,128)(2,1)S(1)} %get-tuple-element.18.near_ref, bf16[512,1024]{1,0:T(8,128)(2,1)S(1)} %get-tuple-element.19.query_ref, bf16[128,128]{1,0:T(8,128)(2,1)S(1)} %collective-permute-done.1.rest_0_, ...), custom_call_target="tpu_custom_call" | custom-call | flops 2097152 | bytes 65536 | tf_op jit(solution)/shard_map/mix/pallas_call | solution.py:360
  43.8 10.1 %product.4.rest_0_ = bf16[256,4096]{1,0:T(8,128)(2,1)} custom-call(s32[2]{0:T(128)S(1)} %broadcast_1_which_ref.2.which_ref, bf16[1,256,1024]{2,1,0:T(8,128)(2,1)S(1)} %get-tuple-element.21.own_ref, bf16[1,256,1024]{2,1,0:T(8,128)(2,1)S(1)} %collective-permute-done.4.other_ref, bf16[1024,4096]{1,0:T(8,128)(2,1)} %own_w_ref.7, ...), custom_call_target="tpu_custom_call" | custom-call | flops 67108864 | bytes 360448 | tf_op jit(solution)/shard_map/product/pallas_call | solution.py:187
  55.2 15.9 %near.3 = (bf16[2048,1024]{1,0:T(8,128)(2,1)}, bf16[2048,1024]{1,0:T(8,128)(2,1)}) custom-call(s32[1]{0:T(128)} %constant.35.clone.1.window_ref, bf16[2048,1024]{1,0:T(8,128)(2,1)} %copy-done, bf16[4,128,128]{2,1,0:T(8,128)(2,1)S(1)} %get-tuple-element.17.start_ref, bf16[64,128,128]{2,1,0:T(8,128)(2,1)S(1)} %toeplitz.1.tile_ref, ...), custom_call_target="tpu_custom_call" | custom-call | flops 33554432 | bytes 262144 | tf_op jit(solution)/shard_map/near/pallas_call | solution.py:312
  71.1 9.1 %mix.3 = (bf16[4,256,1024]{2,1,0:T(8,128)(2,1)S(1)}, bf16[4,256,1024]{2,1,0:T(8,128)(2,1)S(1)}) custom-call(s32[2]{0:T(128)S(1)} %get-tuple-element.34.where_ref, bf16[2048,1024]{1,0:T(8,128)(2,1)} %get-tuple-element.23.near_ref, bf16[2048,1024]{1,0:T(8,128)(2,1)} %get-tuple-element.24.query_ref, bf16[128,128]{1,0:T(8,128)(2,1)S(1)} %collective-permute-done.1.rest_0_, ...), custom_call_target="tpu_custom_call" | custom-call | flops 8388608 | bytes 262144 | tf_op jit(solution)/shard_map/mix/pallas_call | solution.py:360
  82.3 9.1 %product.7 = bf16[256,4096]{1,0:T(8,128)(2,1)S(1)} custom-call(s32[2]{0:T(128)S(1)} %pad_add_fusion.which_ref, bf16[4,256,1024]{2,1,0:T(8,128)(2,1)S(1)} %get-tuple-element.25.own_ref, bf16[1,256,1024]{2,1,0:T(8,128)(2,1)S(1)} %collective-permute-done.12.other_ref, bf16[1024,4096]{1,0:T(8,128)(2,1)} %own_w_ref.7, ...), custom_call_target="tpu_custom_call" | custom-call | flops 67108864 | bytes 360448 | tf_op jit(solution)/shard_map/product/pallas_call | solution.py:187
  92.7 11.9 %collective-permute-done.8 = bf16[256,4096]{1,0:T(8,128)(2,1)} collective-permute-done((bf16[256,4096]{1,0:T(8,128)(2,1)}, bf16[256,4096]{1,0:T(8,128)(2,1)}, u32[]{:S(2)}, u32[]{:S(2)}) %collective-permute-start.8) | collective-permute-done | bytes 2097184 | tf_op jit(solution)/shard_map/ppermute | solution.py:386
  104.6 3.0 %add_convert_fusion.3 = bf16[256,4096]{1,0:T(8,128)(2,1)S(1)} fusion(bf16[256,4096]{1,0:T(8,128)(2,1)} %collective-permute-done.8, bf16[256,4096]{1,0:T(8,128)(2,1)} %product.4.rest_0_), kind=kLoop, calls=%fused_computation.3 | loop fusion | flops 4194304 | bytes 6291456 | tf_op jit(solution)/shard_map/convert_element_type | solution.py:210
  107.9 2.4 %collective-permute-start.10 = (bf16[256,2048]{1,0:T(8,128)(2,1)S(1)}, bf16[256,2048]{1,0:T(8,128)(2,1)S(1)}, u32[]{:S(2)}, u32[]{:S(2)}) collective-permute-start(bf16[256,2048]{1,0:T(8,128)(2,1)S(1)} %get-tuple-element.33), channel_id=1, source_target_pairs={{2,4},{3,5},{4,2},{5,3},{10,12},{11,13},{12,10},{13,11},{18,20},{1... | collective-permute-start | bytes 3145736 | tf_op jit(solution)/shard_map/ppermute | solution.py:386
  110.2 3.5 %collective-permute-start.9 = (bf16[256,2048]{1,0:T(8,128)(2,1)S(1)}, bf16[256,2048]{1,0:T(8,128)(2,1)S(1)}, u32[]{:S(2)}, u32[]{:S(2)}) collective-permute-start(bf16[256,2048]{1,0:T(8,128)(2,1)S(1)} %get-tuple-element.32), channel_id=1, source_target_pairs={{2,4},{3,5},{4,2},{5,3},{10,12},{11,13},{12,10},{13,11},{18,20},{1... | collective-permute-start | bytes 3145736 | tf_op jit(solution)/shard_map/ppermute | solution.py:386
  115.7 9.1 %product.6 = bf16[256,4096]{1,0:T(8,128)(2,1)S(1)} custom-call(s32[2]{0:T(128)S(1)} %pad_add_fusion.1.which_ref, bf16[4,256,1024]{2,1,0:T(8,128)(2,1)S(1)} %get-tuple-element.25.own_ref, bf16[1,256,1024]{2,1,0:T(8,128)(2,1)S(1)} %collective-permute-done.7.other_ref, bf16[1024,4096]{1,0:T(8,128)(2,1)} %own_w_ref.7, ...), custom_call_target="tpu_custom_call" | custom-call | flops 67108864 | bytes 360448 | tf_op jit(solution)/shard_map/product/pallas_call | solution.py:187
  124.8 11.1 %collective-permute-done.10 = bf16[256,2048]{1,0:T(8,128)(2,1)S(1)} collective-permute-done((bf16[256,2048]{1,0:T(8,128)(2,1)S(1)}, bf16[256,2048]{1,0:T(8,128)(2,1)S(1)}, u32[]{:S(2)}, u32[]{:S(2)}) %collective-permute-start.10) | collective-permute-done | bytes 1048608 | tf_op jit(solution)/shard_map/ppermute | solution.py:386
  135.8 19.9 %collective-permute-done.9 = bf16[256,2048]{1,0:T(8,128)(2,1)S(1)} collective-permute-done((bf16[256,2048]{1,0:T(8,128)(2,1)S(1)}, bf16[256,2048]{1,0:T(8,128)(2,1)S(1)}, u32[]{:S(2)}, u32[]{:S(2)}) %collective-permute-start.9) | collective-permute-done | bytes 1048608 | tf_op jit(solution)/shard_map/ppermute | solution.py:386
  157.7 2.4 %collective-permute-start.14 = (bf16[256,2048]{1,0:T(8,128)(2,1)S(1)}, bf16[256,2048]{1,0:T(8,128)(2,1)S(1)}, u32[]{:S(2)}, u32[]{:S(2)}) collective-permute-start(bf16[256,2048]{1,0:T(8,128)(2,1)S(1)} %get-tuple-element.27), channel_id=1, source_target_pairs={{2,4},{3,5},{4,2},{5,3},{10,12},{11,13},{12,10},{13,11},{18,20},{1... | collective-permute-start | bytes 3145736 | tf_op jit(solution)/shard_map/ppermute | solution.py:386
  160.1 3.5 %collective-permute-start.15 = (bf16[256,2048]{1,0:T(8,128)(2,1)S(1)}, bf16[256,2048]{1,0:T(8,128)(2,1)S(1)}, u32[]{:S(2)}, u32[]{:S(2)}) collective-permute-start(bf16[256,2048]{1,0:T(8,128)(2,1)S(1)} %get-tuple-element.28), channel_id=1, source_target_pairs={{2,4},{3,5},{4,2},{5,3},{10,12},{11,13},{12,10},{13,11},{18,20},{1... | collective-permute-start | bytes 3145736 | tf_op jit(solution)/shard_map/ppermute | solution.py:386
  165.5 9.1 %product.5 = bf16[256,4096]{1,0:T(8,128)(2,1)S(1)} custom-call(s32[2]{0:T(128)S(1)} %pad_add_fusion.3.which_ref, bf16[4,256,1024]{2,1,0:T(8,128)(2,1)S(1)} %get-tuple-element.25.own_ref, bf16[1,256,1024]{2,1,0:T(8,128)(2,1)S(1)} %collective-permute-done.6.other_ref, bf16[1024,4096]{1,0:T(8,128)(2,1)} %own_w_ref.7, ...), custom_call_target="tpu_custom_call" | custom-call | flops 67108864 | bytes 360448 | tf_op jit(solution)/shard_map/product/pallas_call | solution.py:187
  174.6 11.1 %collective-permute-done.14 = bf16[256,2048]{1,0:T(8,128)(2,1)S(1)} collective-permute-done((bf16[256,2048]{1,0:T(8,128)(2,1)S(1)}, bf16[256,2048]{1,0:T(8,128)(2,1)S(1)}, u32[]{:S(2)}, u32[]{:S(2)}) %collective-permute-start.14) | collective-permute-done | bytes 1048608 | tf_op jit(solution)/shard_map/ppermute | solution.py:386
  185.7 19.0 %collective-permute-done.15 = bf16[256,2048]{1,0:T(8,128)(2,1)S(1)} collective-permute-done((bf16[256,2048]{1,0:T(8,128)(2,1)S(1)}, bf16[256,2048]{1,0:T(8,128)(2,1)S(1)}, u32[]{:S(2)}, u32[]{:S(2)}) %collective-permute-start.15) | collective-permute-done | bytes 1048608 | tf_op jit(solution)/shard_map/ppermute | solution.py:386
  204.7 2.4 %add_convert_fusion = bf16[256,4096]{1,0:T(8,128)(2,1)} fusion(bf16[256,4096]{1,0:T(8,128)(2,1)S(1)} %collective-permute-done.11, bf16[256,4096]{1,0:T(8,128)(2,1)S(1)} %product.5, bf16[256,2048]{1,0:T(8,128)(2,1)S(1)} %collective-permute-done.15, bf16[256,2048]{1,0:T(8,128)(2,1)S(1)} %collective-permute-done.14), kind=kLoop, calls=%fused_computation | loop fusion | flops 9437184 | bytes 8388608 | tf_op jit(solution)/shard_map/convert_element_type | solution.py:210
  (48 shorter events, 19.3 us)
Async XLA Ops:
  0.0 43.8 %collective-permute-start.5 = (bf16[1024,4096]{1,0:T(8,128)(2,1)}, bf16[1024,4096]{1,0:T(8,128)(2,1)}, u32[]{:S(2)}, u32[]{:S(2)}) collective-permute-start(bf16[1024,4096]{1,0:T(8,128)(2,1)} %own_w_ref.7), channel_id=1, source_target_pairs={{0,1},{1,0},{2,3},{3,2},{4,5},{5,4},{6,7},{7,6},{8,9},{9,8},{10,11... | collective-permute-start | bytes 25165832 | tf_op jit(solution)/shard_map/ppermute | solution.py:255
  0.8 5.0 %collective-permute-start = (bf16[2,3,1024]{2,0,1:T(2,128)(2,1)S(1)}, bf16[2,3,1024]{2,0,1:T(2,128)(2,1)S(1)}, u32[]{:S(2)}, u32[]{:S(2)}) collective-permute-start(bf16[2,3,1024]{2,0,1:T(2,128)(2,1)S(1)} %slice.15), channel_id=1, source_target_pairs={{0,8},{8,16},{16,24},{1,9},{9,17},{17,25},{2,10},{10,18},{18,26},{... | collective-permute-start | bytes 36872 | tf_op jit(solution)/shard_map/ppermute | solution.py:199
  6.0 0.8 copy-start.1
  17.5 2.0 copy-start
  19.5 10.8 %copy-start.2 = (f32[3,3,1024]{2,1,0:T(4,128)S(1)}, f32[3,3,1024]{2,1,0:T(4,128)}, u32[]{:S(2)}) copy-start(f32[3,3,1024]{2,1,0:T(4,128)} %taps_ref.5) | copy-start | bytes 110596
  19.5 10.8 %copy-start.3 = (f32[1024]{0:T(1024)S(1)}, f32[1024]{0:T(1024)}, u32[]{:S(2)}) copy-start(f32[1024]{0:T(1024)} %param.10) | copy-start | bytes 12292
  19.5 18.8 %collective-permute-start.1 = (bf16[128,128]{1,0:T(8,128)(2,1)S(1)}, bf16[128,128]{1,0:T(8,128)(2,1)S(1)}, u32[]{:S(2)}, u32[]{:S(2)}) collective-permute-start(bf16[128,128]{1,0:T(8,128)(2,1)S(1)} %get-tuple-element.20), channel_id=1, source_target_pairs={{0,8},{8,16},{16,24},{1,9},{9,17},{17,25},{2,10},{10,18},{18,26},{... | collective-permute-start | bytes 98312 | tf_op jit(solution)/shard_map/ppermute | solution.py:199
  23.6 14.7 %collective-permute-start.2 = (bf16[128,128]{1,0:T(8,128)(2,1)S(1)}, bf16[128,128]{1,0:T(8,128)(2,1)S(1)}, u32[]{:S(2)}, u32[]{:S(2)}) collective-permute-start(bf16[128,128]{1,0:T(8,128)(2,1)S(1)} %get-tuple-element.20), channel_id=1, source_target_pairs={{0,16},{8,24},{1,17},{9,25},{2,18},{10,26},{3,19},{11,27},{4,20},{... | collective-permute-start | bytes 98312 | tf_op jit(solution)/shard_map/ppermute | solution.py:199
  27.0 11.2 %collective-permute-start.3 = (bf16[128,128]{1,0:T(8,128)(2,1)S(1)}, bf16[128,128]{1,0:T(8,128)(2,1)S(1)}, u32[]{:S(2)}, u32[]{:S(2)}) collective-permute-start(bf16[128,128]{1,0:T(8,128)(2,1)S(1)} %get-tuple-element.20), channel_id=1, source_target_pairs={{0,24},{1,25},{2,26},{3,27},{4,28},{5,29},{6,30},{7,31}} | collective-permute-start | bytes 98312 | tf_op jit(solution)/shard_map/ppermute | solution.py:199
  41.8 2.0 collective-permute-start.4
  53.9 50.7 %collective-permute-start.8 = (bf16[256,4096]{1,0:T(8,128)(2,1)}, bf16[256,4096]{1,0:T(8,128)(2,1)}, u32[]{:S(2)}, u32[]{:S(2)}) collective-permute-start(bf16[256,4096]{1,0:T(8,128)(2,1)} %product.4.rest_0_), channel_id=1, source_target_pairs={{0,2},{1,3},{6,4},{7,5},{8,10},{9,11},{14,12},{15,13},{16,18},{17,... | collective-permute-start | bytes 6291464 | tf_op jit(solution)/shard_map/ppermute | solution.py:386
  80.4 2.0 collective-permute-start.12
  91.4 65.2 %collective-permute-start.13 = (bf16[256,4096]{1,0:T(8,128)(2,1)S(1)}, bf16[256,4096]{1,0:T(8,128)(2,1)S(1)}, u32[]{:S(2)}, u32[]{:S(2)}) collective-permute-start(bf16[256,4096]{1,0:T(8,128)(2,1)S(1)} %product.7), channel_id=1, source_target_pairs={{0,2},{1,3},{6,4},{7,5},{8,10},{9,11},{14,12},{15,13},{16,18},{17,... | collective-permute-start | bytes 6291464 | tf_op jit(solution)/shard_map/ppermute | solution.py:386
  107.9 28.0 %collective-permute-start.10 = (bf16[256,2048]{1,0:T(8,128)(2,1)S(1)}, bf16[256,2048]{1,0:T(8,128)(2,1)S(1)}, u32[]{:S(2)}, u32[]{:S(2)}) collective-permute-start(bf16[256,2048]{1,0:T(8,128)(2,1)S(1)} %get-tuple-element.33), channel_id=1, source_target_pairs={{2,4},{3,5},{4,2},{5,3},{10,12},{11,13},{12,10},{13,11},{18,20},{1... | collective-permute-start | bytes 3145736 | tf_op jit(solution)/shard_map/ppermute | solution.py:386
  110.2 45.6 %collective-permute-start.9 = (bf16[256,2048]{1,0:T(8,128)(2,1)S(1)}, bf16[256,2048]{1,0:T(8,128)(2,1)S(1)}, u32[]{:S(2)}, u32[]{:S(2)}) collective-permute-start(bf16[256,2048]{1,0:T(8,128)(2,1)S(1)} %get-tuple-element.32), channel_id=1, source_target_pairs={{2,4},{3,5},{4,2},{5,3},{10,12},{11,13},{12,10},{13,11},{18,20},{1... | collective-permute-start | bytes 3145736 | tf_op jit(solution)/shard_map/ppermute | solution.py:386
  113.7 2.0 collective-permute-start.7
  156.6 48.1 %collective-permute-start.11 = (bf16[256,4096]{1,0:T(8,128)(2,1)S(1)}, bf16[256,4096]{1,0:T(8,128)(2,1)S(1)}, u32[]{:S(2)}, u32[]{:S(2)}) collective-permute-start(bf16[256,4096]{1,0:T(8,128)(2,1)S(1)} %add_convert_fusion.2), channel_id=1, source_target_pairs={{0,2},{1,3},{6,4},{7,5},{2,0},{3,1},{4,6},{5,7},{8,10},{9,11},{14,... | collective-permute-start | bytes 6291464 | tf_op jit(solution)/shard_map/ppermute | solution.py:386
  157.7 28.0 %collective-permute-start.14 = (bf16[256,2048]{1,0:T(8,128)(2,1)S(1)}, bf16[256,2048]{1,0:T(8,128)(2,1)S(1)}, u32[]{:S(2)}, u32[]{:S(2)}) collective-permute-start(bf16[256,2048]{1,0:T(8,128)(2,1)S(1)} %get-tuple-element.27), channel_id=1, source_target_pairs={{2,4},{3,5},{4,2},{5,3},{10,12},{11,13},{12,10},{13,11},{18,20},{1... | collective-permute-start | bytes 3145736 | tf_op jit(solution)/shard_map/ppermute | solution.py:386
  160.1 44.6 %collective-permute-start.15 = (bf16[256,2048]{1,0:T(8,128)(2,1)S(1)}, bf16[256,2048]{1,0:T(8,128)(2,1)S(1)}, u32[]{:S(2)}, u32[]{:S(2)}) collective-permute-start(bf16[256,2048]{1,0:T(8,128)(2,1)S(1)} %get-tuple-element.28), channel_id=1, source_target_pairs={{2,4},{3,5},{4,2},{5,3},{10,12},{11,13},{12,10},{13,11},{18,20},{1... | collective-permute-start | bytes 3145736 | tf_op jit(solution)/shard_map/ppermute | solution.py:386
  163.5 2.0 collective-permute-start.6

commit v3 on v2

--- a/solution.py
+++ b/solution.py
@@ -140,8 +140,9 @@
         query_ref[rows, :] = short_conv(0, q_stage, q_ref, rim_ref, taps_ref, k).astype(BF16)
 
 
-def mix_kernel(modes, group, tok_rows, size, where_ref, near_ref, query_ref, *rest):
-    *piece_refs, row_rate_ref, row_scale_ref, keep_ref, give_ref, mixed_ref = rest
+def mix_kernel(modes, group, tok_rows, size, where_ref, near_ref, query_ref, row_rate_ref, row_scale_ref, *rest):
+    keep_ref, give_ref, mixed_ref = rest[-3:]
+    piece_refs = rest[: lax.axis_size("ctx") - 1]
     core = where_ref[0]
     first = (where_ref[1] * near_ref.shape[0]).astype(F32)
     row_rate = row_rate_ref[0]
@@ -164,43 +165,73 @@
     give_ref[...] = mixed_ref[1]
 
 
-def product_kernel(which_ref, own_ref, other_ref, own_w_ref, other_w_ref, out_ref):
+def product_kernel(which_ref, own_ref, other_ref, own_w_ref, other_w_ref, *rest):
+    out_ref = rest[-1]
     out_ref[...] = (dot(own_ref[0], own_w_ref[...]) + dot(other_ref[0], other_w_ref[...])).astype(BF16)
 
 
-def product(which, own, other, own_w, other_w, part, split, other_which=None):
+def corner(value):
+    zeros = (0,) * value.ndim
+    return pl.BlockSpec((1,) * (value.ndim - 2) + (16, LANES), lambda *at: zeros)
+
+
+def product(which, own, other, own_w, other_w, columns, other_which=None, earlier=()):
     _, rows, depth = own.shape
-    width = own_w.shape[1] // split
-    tile = min(1024, width)
-    steps = width // tile
-    grid_spec = pltpu.PrefetchScalarGridSpec(
-        num_scalar_prefetch=1,
-        grid=(steps,),
-        in_specs=[
-            pl.BlockSpec((1, rows, depth), lambda j, which: (which[0], 0, 0)),
-            pl.BlockSpec((1, rows, depth), lambda j, which: (which[1], 0, 0)),
-            pl.BlockSpec((depth, tile), lambda j, which: (0, part * steps + j)),
-            pl.BlockSpec((depth, tile), lambda j, which: (0, part * steps + j)),
-        ],
-        out_specs=pl.BlockSpec((rows, tile), lambda j, which: (0, j)),
-    )
+    first, stop = columns
+    tile = min(1024, stop - first)
+    base = first // tile
+    width = stop - first
     return pl.pallas_call(
         product_kernel,
-        grid_spec=grid_spec,
+        grid_spec=pltpu.PrefetchScalarGridSpec(
+            num_scalar_prefetch=1,
+            grid=(width // tile,),
+            in_specs=[
+                pl.BlockSpec((1, rows, depth), lambda j, which: (which[0], 0, 0)),
+                pl.BlockSpec((1, rows, depth), lambda j, which: (which[1], 0, 0)),
+                pl.BlockSpec((depth, tile), lambda j, which: (0, base + j)),
+                pl.BlockSpec((depth, tile), lambda j, which: (0, base + j)),
+            ]
+            + [corner(value) for value in earlier],
+            out_specs=pl.BlockSpec((rows, tile), lambda j, which: (0, j)),
+        ),
         out_shape=jax.ShapeDtypeStruct((rows, width), BF16),
         compiler_params=params(),
         cost_estimate=cost(4 * rows * depth * width, 4 * depth * width + 6 * rows * width),
         name="product",
-    )(jnp.stack([which, which if other_which is None else other_which]).astype(jnp.int32), own, other, own_w, other_w)
+    )(
+        jnp.stack([which, which if other_which is None else other_which]).astype(jnp.int32),
+        own,
+        other,
+        own_w,
+        other_w,
+        *earlier,
+    )
+
+
+def sum_kernel(count, *refs):
+    refs[-1][...] = add(*(ref[...] for ref in refs[:count]))
+
+
+def add_after(values, earlier):
+    rows, width = values[0].shape
+    tile = min(512, width)
+    block = pl.BlockSpec((rows, tile), lambda j: (0, j))
+    return pl.pallas_call(
+        functools.partial(sum_kernel, len(values)),
+        grid=(width // tile,),
+        in_specs=[block] * len(values) + [corner(value) for value in earlier],
+        out_specs=block,
+        out_shape=jax.ShapeDtypeStruct((rows, width), BF16),
+        compiler_params=params(),
+        cost_estimate=cost(rows * width * len(values), rows * width * 6),
+        name="sum",
+    )(*values, *earlier)
 
 
 def shifted(value, axis, steps):
     count = lax.axis_size(axis)
     return lax.ppermute(value, axis, [(i, i + steps) for i in range(count - steps)])
-
-
-def tie(*values):
-    return lax.optimization_barrier(values)
 
 
 def add(*values):
@@ -218,7 +249,10 @@
     parts = keep.shape[0]
     split = 2
     last = parts - 1
-    multiply = lambda which, j: product(jnp.clip(which, 0, last), keep, other, out_weight, other_weight, j, split)
+    width = out_weight.shape[1] // split
+    multiply = lambda which, j: product(
+        jnp.clip(which, 0, last), keep, other, out_weight, other_weight, (j * width, (j + 1) * width)
+    )
     up = [None] * split
     down = [None] * split
     for s in range(1, parts):
@@ -326,7 +360,7 @@
                     row_spec,
                     row_spec,
                 ]
-                + [pl.BlockSpec(memory_space=pl.ANY)] * len(earlier),
+                + [corner(value) for value in earlier],
                 out_specs=[pl.BlockSpec((rows, LANES), lambda g, at: (0, g))] * 2,
                 scratch_shapes=[
                     pltpu.VMEM((8 + rows, LANES), F32),
@@ -353,7 +387,7 @@
             *earlier,
         )
 
-    def finish(near, query, window):
+    def finish(near, query, window, *earlier):
         rows = near.shape[0]
         held = rows // (2 * size)
         out_spec = pl.BlockSpec((held, size, LANES), lambda g, at: (0, 0, g))
@@ -363,8 +397,9 @@
                 num_scalar_prefetch=1,
                 grid=(blocks,),
                 in_specs=[pl.BlockSpec((rows, LANES), lambda g, at: (0, g))] * 2
+                + [row_spec, row_spec]
                 + [pl.BlockSpec((group, LANES), lambda g, at: (g, 0))] * len(pieces)
-                + [row_spec, row_spec],
+                + [corner(value) for value in earlier],
                 out_specs=[out_spec, out_spec],
                 scratch_shapes=[pltpu.VMEM((2, held, size, LANES), BF16)],
             ),
@@ -372,7 +407,7 @@
             compiler_params=params(),
             cost_estimate=cost(rows * channels * 256, rows * channels * 8),
             name="mix",
-        )(jnp.stack([core, window]).astype(jnp.int32), near, query, *pieces, rate_rows, scale_rows)
+        )(jnp.stack([core, window]).astype(jnp.int32), near, query, rate_rows, scale_rows, *pieces, *earlier)
 
     nothing = core * 0
     if parts != 4:
@@ -381,29 +416,41 @@
 
     far, far_inner = jnp.where(place < 2, 3, 0), jnp.where(place < 2, 2, 1)
     close, close_inner = 3 - far, 3 - far_inner
-    at_end = (place == 0) | (place == 3)
     inward, across, outward = pairs([(0, 1), (3, 2)]), pairs([(1, 2), (2, 1)]), pairs([(1, 0), (2, 3)])
     send = lambda value, hops: lax.ppermute(value, "chan", hops)
 
     keep, give = finish(*convolve(gated, far, tok_rows // parts), far)
     other = send(give, swap)
-    first = product(nothing, keep, other, out_weight, other_weight, 0, 1)
-    from_end = send(first, inward)
-
-    keep, give = finish(*convolve(gated, nothing, tok_rows, first), nothing)
+    width = out_weight.shape[1]
+    whole, even = (0, width), ((0, width // 2), (width // 2, width))
+    join = lambda values: jnp.concatenate(values, axis=1)
+    first = []
+    for c in even:
+        first.append(product(nothing, keep, other, out_weight, other_weight, c, nothing, first))
+    from_end = [send(value, inward) for value in first]
+    keep, give = finish(*convolve(gated, far_inner, tok_rows // parts, first[1]), far_inner)
+    second = product(nothing, keep, send(give, swap), out_weight, other_weight, whole)
+    through = send(second, inward)
+    far_sum = [add(first[0], from_end[0])]
+    crossed = [send(far_sum[0], across)]
+
+    near, query = convolve(gated, nothing, tok_rows, second, far_sum[0])
+    far_sum.append(add_after((first[1], from_end[1]), (near,)))
+    crossed.append(send(far_sum[1], across))
+    keep, give = finish(near, query, nothing, far_sum[1])
     swapped = lambda which: send(lax.dynamic_slice_in_dim(give, which, 1, 0), swap)
-    multiply = lambda which, other: product(which, keep, other, out_weight, other_weight, 0, 1, nothing)
-    half = out_weight.shape[1] // 2
-    halves = lambda value: (value[:, :half], value[:, half:])
-    second = multiply(far_inner, swapped(far_inner))
-    through = send(second, inward)
-    crossed = [send(value, across) for value in halves(add(first, from_end))]
-    which = jnp.where(at_end, close_inner, close)
-    third = multiply(which, swapped(which))
-    last = send(add(third, jnp.concatenate(crossed, axis=1)), inward + outward)
-    inner = [send(value, across) for value in halves(add(second, through))]
-    own = multiply(place, swapped(place))
-    return add(own, last, jnp.concatenate(inner, axis=1))
+    multiply = lambda which, other, *earlier: product(
+        which, keep, other, out_weight, other_weight, whole, nothing, earlier
+    )
+    others = [swapped(which) for which in (close_inner, close, place)]
+    third = multiply(close_inner, others[0])
+    last = send(third, inward)
+    outer = multiply(close, others[1], third, crossed[0])
+    inner_sum = add(second, through)
+    inner = send(inner_sum, across)
+    own = multiply(place, others[2], outer, inner_sum)
+    outer = send(add(outer, join(crossed)), outward)
+    return add(add(own, outer, last), inner)
 
 
 def solution(mesh):

time: 208 us -> 203 us (0.976)
  waiting for transfers between devices: 80.2 us -> 41.1 us
  Pallas kernels: 85.8 us -> 109 us
  other arithmetic: 7.96 us -> 13.7 us
  starting transfers between devices: 27 us -> 32.7 us
    ppermute x11 -> x13, waiting for transfers between devices: 80.2 us -> 41.1 us  [on_device(): send = lambda value, hops: lax.ppermute(value, 'chan', hops)]
    pallas_call x4 -> x7, Pallas kernels: 37.3 us -> 48.3 us  [the longest x6 47.2 us: product(): pl.pallas_call(product_kernel, grid_spec=pltpu.PrefetchScalarGridSpec(num...]
    pallas_call x2 -> x3, Pallas kernels: 23.8 us -> 32 us  [convolve(): pl.pallas_call(functools.partial(near_kernel, modes, group), grid_spec=pl...]
    ppermute x11 -> x13, starting transfers between devices: 14.7 us -> 20.5 us  [on_device(): send = lambda value, hops: lax.ppermute(value, 'chan', hops)]
    convert_element_type x4, other arithmetic: 6.92 us -> 12.6 us  [add(): return total.astype(BF16)]
    pallas_call x2 -> x3, Pallas kernels: 12.6 us -> 16.2 us  [finish(): pl.pallas_call(functools.partial(mix_kernel, modes, group, tok_rows, size...]
  transfers between devices with their start and end apart: 16 -> 18, of which waited for: 9 -> 7; matrix products, arithmetic and copies ran while one was open for 4% -> 6% of each run, Pallas kernels for 37% -> 51%
where the time goes in v3:
time: 203 us; the launch traced here: 202 us
  Pallas kernels  109 us (54%)
  waiting for transfers between devices  41.1 us (20%)
  starting transfers between devices  32.7 us (16%)
  other arithmetic  13.7 us (7%)
  local copies, waits for them, and re-layouts  5.27 us (3%)
    pallas_call x6, Pallas kernels, product(): pl.pallas_call(product_kernel, grid_spec=pltpu.PrefetchScalarGridSpec(num...  47.2 us
    ppermute x13, waiting for transfers between devices, on_device(): send = lambda value, hops: lax.ppermute(value, 'chan', hops)  41.1 us
    pallas_call x3, Pallas kernels, convolve(): pl.pallas_call(functools.partial(near_kernel, modes, group), grid_spec=pl...  32 us
    ppermute x13, starting transfers between devices, on_device(): send = lambda value, hops: lax.ppermute(value, 'chan', hops)  20.5 us
    pallas_call x3, Pallas kernels, finish(): pl.pallas_call(functools.partial(mix_kernel, modes, group, tok_rows, size...  16.2 us
    convert_element_type x4, other arithmetic, add(): return total.astype(BF16)  12.6 us
    ppermute x4, starting transfers between devices, shifted(): lax.ppermute(value, axis, [(i, i + steps) for i in range(count - steps)])  12.2 us
    pallas_call x1, Pallas kernels, on_device(): pl.pallas_call(functools.partial(gate_kernel, modes, group), grid=(blocks...  10.7 us
  transfers between devices with their start and end apart: 18, of which 7 were waited for; matrix products, arithmetic and copies ran while one was open for 6% of the time, Pallas kernels for 51%

profile of v3, /device:TPU:16, one launch (start us, length us, event | category | flops | bytes accessed | tf_op | source)
XLA Modules:
  0.0 201.6 jit_solution(12669674600902655469)
XLA Ops:
  0.8 3.4 %collective-permute-start = (bf16[2,3,1024]{2,0,1:T(2,128)(2,1)S(1)}, bf16[2,3,1024]{2,0,1:T(2,128)(2,1)S(1)}, u32[]{:S(2)}, u32[]{:S(2)}) collective-permute-start(bf16[2,3,1024]{2,0,1:T(2,128)(2,1)S(1)} %slice.3), channel_id=1, source_target_pairs={{0,8},{8,16},{16,24},{1,9},{9,17},{17,25},{2,10},{10,18},{18,26},{... | collective-permute-start | bytes 36872 | tf_op jit(solution)/shard_map/ppermute | solution.py:234
  6.8 10.7 %gate.1 = (bf16[2048,1024]{1,0:T(8,128)(2,1)S(1)}, bf16[4,128,128]{2,1,0:T(8,128)(2,1)S(1)}, bf16[128,128]{1,0:T(8,128)(2,1)S(1)}) custom-call(bf16[3,2048,1024]{2,1,0:T(8,128)(2,1)} %bitcast.30, bf16[3,2048,1024]{2,1,0:T(8,128)(2,1)} %bitcast.31, bf16[3,2,1024]{2,1,0:T(2,128)(2,1)S(1)} %bitcast.23, f32[3,3,1024]{2,1,0:T(4,128)S(1)} %copy-done.3, ...), custom_call_target="tpu_custom_call" | custom-call | flops 8388608 | bytes 196608 | tf_op jit(solution)/shard_map/gate/pallas_call | solution.py:321
  19.5 4.1 %collective-permute-start.1 = (bf16[128,128]{1,0:T(8,128)(2,1)S(1)}, bf16[128,128]{1,0:T(8,128)(2,1)S(1)}, u32[]{:S(2)}, u32[]{:S(2)}) collective-permute-start(bf16[128,128]{1,0:T(8,128)(2,1)S(1)} %get-tuple-element.24), channel_id=1, source_target_pairs={{0,8},{8,16},{16,24},{1,9},{9,17},{17,25},{2,10},{10,18},{18,26},{... | collective-permute-start | bytes 98312 | tf_op jit(solution)/shard_map/ppermute | solution.py:234
  23.6 3.4 %collective-permute-start.2 = (bf16[128,128]{1,0:T(8,128)(2,1)S(1)}, bf16[128,128]{1,0:T(8,128)(2,1)S(1)}, u32[]{:S(2)}, u32[]{:S(2)}) collective-permute-start(bf16[128,128]{1,0:T(8,128)(2,1)S(1)} %get-tuple-element.24), channel_id=1, source_target_pairs={{0,16},{8,24},{1,17},{9,25},{2,18},{10,26},{3,19},{11,27},{4,20},{... | collective-permute-start | bytes 98312 | tf_op jit(solution)/shard_map/ppermute | solution.py:234
  30.3 8.0 %near.3 = (bf16[512,1024]{1,0:T(8,128)(2,1)S(1)}, bf16[512,1024]{1,0:T(8,128)(2,1)S(1)}) custom-call(s32[1]{0:T(128)} %bitcast.8.window_ref, bf16[2048,1024]{1,0:T(8,128)(2,1)} %copy-done, bf16[4,128,128]{2,1,0:T(8,128)(2,1)S(1)} %get-tuple-element.21.start_ref, bf16[64,128,128]{2,1,0:T(8,128)(2,1)S(1)} %toeplitz.1.tile_ref, ...), custom_call_target="tpu_custom_call" | custom-call | flops 8388608 | bytes 65536 | tf_op jit(solution)/shard_map/near/pallas_call | solution.py:346
  38.3 3.5 %mix.3 = (bf16[1,256,1024]{2,1,0:T(8,128)(2,1)S(1)}, bf16[1,256,1024]{2,1,0:T(8,128)(2,1)S(1)}) custom-call(s32[2]{0:T(128)S(1)} %get-tuple-element.39.where_ref, bf16[512,1024]{1,0:T(8,128)(2,1)S(1)} %get-tuple-element.22.near_ref, bf16[512,1024]{1,0:T(8,128)(2,1)S(1)} %get-tuple-element.23.query_ref, f32[8,1,128]{2,1,0:T(1,128)S(1)} %bitcast.12, ...), custom_call_target="tpu_custom_call" | custom-call | flops 2097152 | bytes 65536 | tf_op jit(solution)/shard_map/mix/pallas_call | solution.py:394
  43.8 5.4 %product.6.rest_0_ = bf16[256,2048]{1,0:T(8,128)(2,1)S(1)} custom-call(s32[2]{0:T(128)S(1)} %broadcast_1_which_ref.2.which_ref, bf16[1,256,1024]{2,1,0:T(8,128)(2,1)S(1)} %get-tuple-element.25.own_ref, bf16[1,256,1024]{2,1,0:T(8,128)(2,1)S(1)} %collective-permute-done.4.other_ref, bf16[1024,4096]{1,0:T(8,128)(2,1)} %own_w_ref.11, ...), custom_call_target="tpu_custom_call" | custom-call | flops 33554432 | bytes 180224 | tf_op jit(solution)/shard_map/product/pallas_call | solution.py:184
  50.5 5.4 %product.7.rest_0_.refs_0_ = bf16[256,2048]{1,0:T(8,128)(2,1)S(1)} custom-call(s32[2]{0:T(128)S(1)} %broadcast_1_which_ref.2.which_ref, bf16[1,256,1024]{2,1,0:T(8,128)(2,1)S(1)} %get-tuple-element.25.own_ref, bf16[1,256,1024]{2,1,0:T(8,128)(2,1)S(1)} %collective-permute-done.4.other_ref, bf16[1024,4096]{1,0:T(8,128)(2,1)} %own_w_ref.11, ...), custom_call_target="tpu_custom_call" | custom-call | flops 33554432 | bytes 180224 | tf_op jit(solution)/shard_map/product/pallas_call | solution.py:184
  55.9 8.0 %near.4 = (bf16[512,1024]{1,0:T(8,128)(2,1)S(1)}, bf16[512,1024]{1,0:T(8,128)(2,1)S(1)}) custom-call(s32[1]{0:T(128)} %bitcast.7.window_ref, bf16[2048,1024]{1,0:T(8,128)(2,1)} %copy-done, bf16[4,128,128]{2,1,0:T(8,128)(2,1)S(1)} %get-tuple-element.21.start_ref, bf16[64,128,128]{2,1,0:T(8,128)(2,1)S(1)} %toeplitz.1.tile_ref, ...), custom_call_target="tpu_custom_call" | custom-call | flops 8388608 | bytes 65536 | tf_op jit(solution)/shard_map/near/pallas_call | solution.py:346
  63.9 3.5 %mix.4 = (bf16[1,256,1024]{2,1,0:T(8,128)(2,1)S(1)}, bf16[1,256,1024]{2,1,0:T(8,128)(2,1)S(1)}) custom-call(s32[2]{0:T(128)S(1)} %get-tuple-element.38.where_ref, bf16[512,1024]{1,0:T(8,128)(2,1)S(1)} %get-tuple-element.27.near_ref, bf16[512,1024]{1,0:T(8,128)(2,1)S(1)} %get-tuple-element.28.query_ref, f32[8,1,128]{2,1,0:T(1,128)S(1)} %bitcast.14, ...), custom_call_target="tpu_custom_call" | custom-call | flops 2097152 | bytes 65536 | tf_op jit(solution)/shard_map/mix/pallas_call | solution.py:394
  69.4 9.1 %product.8.rest_0_ = bf16[256,4096]{1,0:T(8,128)(2,1)S(1)} custom-call(s32[2]{0:T(128)S(1)} %broadcast_1_which_ref.2.which_ref, bf16[1,256,1024]{2,1,0:T(8,128)(2,1)S(1)} %get-tuple-element.29.own_ref, bf16[1,256,1024]{2,1,0:T(8,128)(2,1)S(1)} %collective-permute-done.6.other_ref, bf16[1024,4096]{1,0:T(8,128)(2,1)} %own_w_ref.11, ...), custom_call_target="tpu_custom_call" | custom-call | flops 67108864 | bytes 360448 | tf_op jit(solution)/shard_map/product/pallas_call | solution.py:184
  81.3 2.3 %collective-permute-start.12 = (bf16[256,2048]{1,0:T(8,128)(2,1)}, bf16[256,2048]{1,0:T(8,128)(2,1)}, u32[]{:S(2)}, u32[]{:S(2)}) collective-permute-start(bf16[256,2048]{1,0:T(8,128)(2,1)} %add_convert_fusion.4.rest_1_), channel_id=1, source_target_pairs={{2,4},{3,5},{4,2},{5,3},{10,12},{11,13},{12,10},{13,11},{18,20},{1... | collective-permute-start | bytes 3145736 | tf_op jit(solution)/shard_map/ppermute | solution.py:420
  83.6 16.0 %near.5 = (bf16[2048,1024]{1,0:T(8,128)(2,1)}, bf16[2048,1024]{1,0:T(8,128)(2,1)}) custom-call(s32[1]{0:T(128)} %constant.36.clone.1.window_ref, bf16[2048,1024]{1,0:T(8,128)(2,1)} %copy-done, bf16[4,128,128]{2,1,0:T(8,128)(2,1)S(1)} %get-tuple-element.21.start_ref, bf16[64,128,128]{2,1,0:T(8,128)(2,1)S(1)} %toeplitz.1.tile_ref, ...), custom_call_target="tpu_custom_call" | custom-call | flops 33554432 | bytes 262144 | tf_op jit(solution)/shard_map/near/pallas_call | solution.py:346
  100.8 3.6 %collective-permute-start.14 = (bf16[256,2048]{1,0:T(8,128)(2,1)S(1)}, bf16[256,2048]{1,0:T(8,128)(2,1)}, u32[]{:S(2)}, u32[]{:S(2)}) collective-permute-start(bf16[256,2048]{1,0:T(8,128)(2,1)S(1)} %sum.1.rest_3_), channel_id=1, source_target_pairs={{2,4},{3,5},{4,2},{5,3},{10,12},{11,13},{12,10},{13,11},{18,20},{1... | collective-permute-start | bytes 3145736 | tf_op jit(solution)/shard_map/ppermute | solution.py:420
  104.5 9.1 %mix.5 = (bf16[4,256,1024]{2,1,0:T(8,128)(2,1)S(1)}, bf16[4,256,1024]{2,1,0:T(8,128)(2,1)S(1)}) custom-call(s32[2]{0:T(128)S(1)} %pad_add_fusion.2.where_ref, bf16[2048,1024]{1,0:T(8,128)(2,1)} %get-tuple-element.31.refs_2_.near_ref, bf16[2048,1024]{1,0:T(8,128)(2,1)} %get-tuple-element.32.query_ref, f32[8,1,128]{2,1,0:T(1,128)S(1)} %bitcast.16, ...), custom_call_target="tpu_custom_call" | custom-call | flops 8388608 | bytes 262144 | tf_op jit(solution)/shard_map/mix/pallas_call | solution.py:394
  115.8 9.1 %product.9.rest_0_ = bf16[256,4096]{1,0:T(8,128)(2,1)S(1)} custom-call(s32[2]{0:T(128)S(1)} %pad_add_fusion.which_ref, bf16[4,256,1024]{2,1,0:T(8,128)(2,1)S(1)} %get-tuple-element.33.own_ref, bf16[1,256,1024]{2,1,0:T(8,128)(2,1)S(1)} %collective-permute-done.11.other_ref, bf16[1024,4096]{1,0:T(8,128)(2,1)} %own_w_ref.11, ...), custom_call_target="tpu_custom_call" | custom-call | flops 67108864 | bytes 360448 | tf_op jit(solution)/shard_map/product/pallas_call | solution.py:184
  126.4 9.1 %product.10.rest_0_ = bf16[256,4096]{1,0:T(8,128)(2,1)S(1)} custom-call(s32[2]{0:T(128)S(1)} %pad_add_fusion.1.which_ref, bf16[4,256,1024]{2,1,0:T(8,128)(2,1)S(1)} %get-tuple-element.33.own_ref, bf16[1,256,1024]{2,1,0:T(8,128)(2,1)S(1)} %collective-permute-done.10.other_ref, bf16[1024,4096]{1,0:T(8,128)(2,1)} %own_w_ref.11, ...), custom_call_target="tpu_custom_call" | custom-call | flops 67108864 | bytes 360448 | tf_op jit(solution)/shard_map/product/pallas_call | solution.py:184
  135.5 4.4 %add_convert_fusion.2 = bf16[256,4096]{1,0:T(8,128)(2,1)} fusion(bf16[256,4096]{1,0:T(8,128)(2,1)S(1)} %product.10.rest_0_, bf16[256,2048]{1,0:T(8,128)(2,1)} %collective-permute-done.14, bf16[256,2048]{1,0:T(8,128)(2,1)} %collective-permute-done.12.rest_1_), kind=kLoop, calls=%fused_computation.2 | loop fusion | flops 7340032 | bytes 6291456 | tf_op jit(solution)/shard_map/convert_element_type | solution.py:241
  139.9 6.0 %collective-permute-start.15 = (bf16[256,4096]{1,0:T(8,128)(2,1)}, bf16[256,4096]{1,0:T(8,128)(2,1)}, u32[]{:S(2)}, u32[]{:S(2)}) collective-permute-start(bf16[256,4096]{1,0:T(8,128)(2,1)} %add_convert_fusion.2), channel_id=1, source_target_pairs={{2,0},{3,1},{4,6},{5,7},{10,8},{11,9},{12,14},{13,15},{18,16},{19,... | collective-permute-start | bytes 6291464 | tf_op jit(solution)/shard_map/ppermute | solution.py:420
  145.9 2.4 %add_convert_fusion.3.rest_1_ = bf16[256,4096]{1,0:T(8,128)(2,1)S(1)} fusion(bf16[256,4096]{1,0:T(8,128)(2,1)} %collective-permute-done.13, bf16[256,4096]{1,0:T(8,128)(2,1)S(1)} %product.8.rest_0_), kind=kLoop, calls=%fused_computation.3 | loop fusion | flops 4194304 | bytes 6291456 | tf_op jit(solution)/shard_map/convert_element_type | solution.py:241
  152.6 9.1 %product.11 = bf16[256,4096]{1,0:T(8,128)(2,1)S(1)} custom-call(s32[2]{0:T(128)S(1)} %pad_add_fusion.3.which_ref, bf16[4,256,1024]{2,1,0:T(8,128)(2,1)S(1)} %get-tuple-element.33.own_ref, bf16[1,256,1024]{2,1,0:T(8,128)(2,1)S(1)} %collective-permute-done.9.other_ref, bf16[1024,4096]{1,0:T(8,128)(2,1)} %own_w_ref.11, ...), custom_call_target="tpu_custom_call" | custom-call | flops 67108864 | bytes 360448 | tf_op jit(solution)/shard_map/product/pallas_call | solution.py:184
  161.7 26.9 %collective-permute-done.16 = bf16[256,4096]{1,0:T(8,128)(2,1)S(1)} collective-permute-done((bf16[256,4096]{1,0:T(8,128)(2,1)S(1)}, bf16[256,4096]{1,0:T(8,128)(2,1)S(1)}, u32[]{:S(2)}, u32[]{:S(2)}) %collective-permute-start.16) | collective-permute-done | bytes 2097184 | tf_op jit(solution)/shard_map/ppermute | solution.py:420
  189.8 7.6 %collective-permute-done.17 = bf16[256,4096]{1,0:T(8,128)(2,1)S(1)} collective-permute-done((bf16[256,4096]{1,0:T(8,128)(2,1)S(1)}, bf16[256,4096]{1,0:T(8,128)(2,1)S(1)}, u32[]{:S(2)}, u32[]{:S(2)}) %collective-permute-start.17) | collective-permute-done | bytes 2097184 | tf_op jit(solution)/shard_map/ppermute | solution.py:420
  197.4 4.3 %add_convert_fusion = bf16[256,4096]{1,0:T(8,128)(2,1)} fusion(bf16[256,4096]{1,0:T(8,128)(2,1)S(1)} %collective-permute-done.17, bf16[256,4096]{1,0:T(8,128)(2,1)S(1)} %collective-permute-done.16, bf16[256,4096]{1,0:T(8,128)(2,1)} %collective-permute-done.15, bf16[256,4096]{1,0:T(8,128)(2,1)S(1)} %product.11), kind=kLoop, calls=%fused_computation | loop fusion | flops 10485760 | bytes 10485760 | tf_op jit(solution)/shard_map/convert_element_type | solution.py:241
  (62 shorter events, 26.8 us)
Async XLA Ops:
  0.0 43.8 %collective-permute-start.5 = (bf16[1024,4096]{1,0:T(8,128)(2,1)}, bf16[1024,4096]{1,0:T(8,128)(2,1)}, u32[]{:S(2)}, u32[]{:S(2)}) collective-permute-start(bf16[1024,4096]{1,0:T(8,128)(2,1)} %own_w_ref.11), channel_id=1, source_target_pairs={{0,1},{1,0},{2,3},{3,2},{4,5},{5,4},{6,7},{7,6},{8,9},{9,8},{10,11... | collective-permute-start | bytes 25165832 | tf_op jit(solution)/shard_map/ppermute | solution.py:289
  0.8 5.0 %collective-permute-start = (bf16[2,3,1024]{2,0,1:T(2,128)(2,1)S(1)}, bf16[2,3,1024]{2,0,1:T(2,128)(2,1)S(1)}, u32[]{:S(2)}, u32[]{:S(2)}) collective-permute-start(bf16[2,3,1024]{2,0,1:T(2,128)(2,1)S(1)} %slice.3), channel_id=1, source_target_pairs={{0,8},{8,16},{16,24},{1,9},{9,17},{17,25},{2,10},{10,18},{18,26},{... | collective-permute-start | bytes 36872 | tf_op jit(solution)/shard_map/ppermute | solution.py:234
  17.5 2.0 copy-start
  19.5 10.8 %copy-start.4 = (f32[3,3,1024]{2,1,0:T(4,128)S(1)}, f32[3,3,1024]{2,1,0:T(4,128)}, u32[]{:S(2)}) copy-start(f32[3,3,1024]{2,1,0:T(4,128)} %taps_ref.7) | copy-start | bytes 110596
  19.5 10.8 %copy-start.5 = (f32[1024]{0:T(1024)S(1)}, f32[1024]{0:T(1024)}, u32[]{:S(2)}) copy-start(f32[1024]{0:T(1024)} %param.10) | copy-start | bytes 12292
  19.5 18.8 %collective-permute-start.1 = (bf16[128,128]{1,0:T(8,128)(2,1)S(1)}, bf16[128,128]{1,0:T(8,128)(2,1)S(1)}, u32[]{:S(2)}, u32[]{:S(2)}) collective-permute-start(bf16[128,128]{1,0:T(8,128)(2,1)S(1)} %get-tuple-element.24), channel_id=1, source_target_pairs={{0,8},{8,16},{16,24},{1,9},{9,17},{17,25},{2,10},{10,18},{18,26},{... | collective-permute-start | bytes 98312 | tf_op jit(solution)/shard_map/ppermute | solution.py:234
  23.6 14.7 %collective-permute-start.2 = (bf16[128,128]{1,0:T(8,128)(2,1)S(1)}, bf16[128,128]{1,0:T(8,128)(2,1)S(1)}, u32[]{:S(2)}, u32[]{:S(2)}) collective-permute-start(bf16[128,128]{1,0:T(8,128)(2,1)S(1)} %get-tuple-element.24), channel_id=1, source_target_pairs={{0,16},{8,24},{1,17},{9,25},{2,18},{10,26},{3,19},{11,27},{4,20},{... | collective-permute-start | bytes 98312 | tf_op jit(solution)/shard_map/ppermute | solution.py:234
  27.0 11.3 %collective-permute-start.3 = (bf16[128,128]{1,0:T(8,128)(2,1)S(1)}, bf16[128,128]{1,0:T(8,128)(2,1)S(1)}, u32[]{:S(2)}, u32[]{:S(2)}) collective-permute-start(bf16[128,128]{1,0:T(8,128)(2,1)S(1)} %get-tuple-element.24), channel_id=1, source_target_pairs={{0,24},{1,25},{2,26},{3,27},{4,28},{5,29},{6,30},{7,31}} | collective-permute-start | bytes 98312 | tf_op jit(solution)/shard_map/ppermute | solution.py:234
  41.8 2.0 collective-permute-start.4
  49.2 30.6 %collective-permute-start.7 = (bf16[256,2048]{1,0:T(8,128)(2,1)S(1)}, bf16[256,2048]{1,0:T(8,128)(2,1)S(1)}, u32[]{:S(2)}, u32[]{:S(2)}) collective-permute-start(bf16[256,2048]{1,0:T(8,128)(2,1)S(1)} %product.6.rest_0_), channel_id=1, source_target_pairs={{0,2},{1,3},{6,4},{7,5},{8,10},{9,11},{14,12},{15,13},{16,18},{17,... | collective-permute-start | bytes 3145736 | tf_op jit(solution)/shard_map/ppermute | solution.py:420
  67.4 2.0 collective-permute-start.6
  67.6 32.0 %collective-permute-start.8 = (bf16[256,2048]{1,0:T(8,128)(2,1)S(1)}, bf16[256,2048]{1,0:T(8,128)(2,1)S(1)}, u32[]{:S(2)}, u32[]{:S(2)}) collective-permute-start(bf16[256,2048]{1,0:T(8,128)(2,1)S(1)} %product.7.rest_0_.refs_0_), channel_id=1, source_target_pairs={{0,2},{1,3},{6,4},{7,5},{8,10},{9,11},{14,12},{15,13},{16,18},{17,... | collective-permute-start | bytes 3145736 | tf_op jit(solution)/shard_map/ppermute | solution.py:420
  78.5 67.4 %collective-permute-start.13 = (bf16[256,4096]{1,0:T(8,128)(2,1)S(1)}, bf16[256,4096]{1,0:T(8,128)(2,1)}, u32[]{:S(2)}, u32[]{:S(2)}) collective-permute-start(bf16[256,4096]{1,0:T(8,128)(2,1)S(1)} %product.8.rest_0_), channel_id=1, source_target_pairs={{0,2},{1,3},{6,4},{7,5},{8,10},{9,11},{14,12},{15,13},{16,18},{17,... | collective-permute-start | bytes 6291464 | tf_op jit(solution)/shard_map/ppermute | solution.py:420
  81.3 45.1 %collective-permute-start.12 = (bf16[256,2048]{1,0:T(8,128)(2,1)}, bf16[256,2048]{1,0:T(8,128)(2,1)}, u32[]{:S(2)}, u32[]{:S(2)}) collective-permute-start(bf16[256,2048]{1,0:T(8,128)(2,1)} %add_convert_fusion.4.rest_1_), channel_id=1, source_target_pairs={{2,4},{3,5},{4,2},{5,3},{10,12},{11,13},{12,10},{13,11},{18,20},{1... | collective-permute-start | bytes 3145736 | tf_op jit(solution)/shard_map/ppermute | solution.py:420
  100.8 34.7 %collective-permute-start.14 = (bf16[256,2048]{1,0:T(8,128)(2,1)S(1)}, bf16[256,2048]{1,0:T(8,128)(2,1)}, u32[]{:S(2)}, u32[]{:S(2)}) collective-permute-start(bf16[256,2048]{1,0:T(8,128)(2,1)S(1)} %sum.1.rest_3_), channel_id=1, source_target_pairs={{2,4},{3,5},{4,2},{5,3},{10,12},{11,13},{12,10},{13,11},{18,20},{1... | collective-permute-start | bytes 3145736 | tf_op jit(solution)/shard_map/ppermute | solution.py:420
  113.8 2.0 collective-permute-start.11
  113.9 12.5 %collective-permute-start.10 = (bf16[1,256,1024]{2,1,0:T(8,128)(2,1)S(1)}, bf16[1,256,1024]{2,1,0:T(8,128)(2,1)S(1)}, u32[]{:S(2)}, u32[]{:S(2)}) collective-permute-start(bf16[1,256,1024]{2,1,0:T(8,128)(2,1)S(1)} %get-tuple-element.37), channel_id=1, source_target_pairs={{0,1},{1,0},{2,3},{3,2},{4,5},{5,4},{6,7},{7,6},{8,9},{9,8},{10,11... | collective-permute-start | bytes 1572872 | tf_op jit(solution)/shard_map/ppermute | solution.py:420
  124.8 1.5 copy-start.2
  124.8 63.8 %collective-permute-start.16 = (bf16[256,4096]{1,0:T(8,128)(2,1)S(1)}, bf16[256,4096]{1,0:T(8,128)(2,1)S(1)}, u32[]{:S(2)}, u32[]{:S(2)}) collective-permute-start(bf16[256,4096]{1,0:T(8,128)(2,1)S(1)} %product.9.rest_0_), channel_id=1, source_target_pairs={{0,2},{1,3},{6,4},{7,5},{8,10},{9,11},{14,12},{15,13},{16,18},{17,... | collective-permute-start | bytes 6291464 | tf_op jit(solution)/shard_map/ppermute | solution.py:420
  135.5 4.4 %copy-start.1 = (bf16[256,4096]{1,0:T(8,128)(2,1)}, bf16[256,4096]{1,0:T(8,128)(2,1)S(1)}, u32[]{:S(2)}) copy-start(bf16[256,4096]{1,0:T(8,128)(2,1)S(1)} %product.10.rest_0_) | copy-start | bytes 6291460
  139.9 49.9 %collective-permute-start.15 = (bf16[256,4096]{1,0:T(8,128)(2,1)}, bf16[256,4096]{1,0:T(8,128)(2,1)}, u32[]{:S(2)}, u32[]{:S(2)}) collective-permute-start(bf16[256,4096]{1,0:T(8,128)(2,1)} %add_convert_fusion.2), channel_id=1, source_target_pairs={{2,0},{3,1},{4,6},{5,7},{10,8},{11,9},{12,14},{13,15},{18,16},{19,... | collective-permute-start | bytes 6291464 | tf_op jit(solution)/shard_map/ppermute | solution.py:420
  148.4 4.3 %copy-start.6 = (bf16[256,4096]{1,0:T(8,128)(2,1)}, bf16[256,4096]{1,0:T(8,128)(2,1)S(1)}, u32[]{:S(2)}) copy-start(bf16[256,4096]{1,0:T(8,128)(2,1)S(1)} %add_convert_fusion.3.rest_1_) | copy-start | bytes 6291460
  148.4 49.0 %collective-permute-start.17 = (bf16[256,4096]{1,0:T(8,128)(2,1)S(1)}, bf16[256,4096]{1,0:T(8,128)(2,1)S(1)}, u32[]{:S(2)}, u32[]{:S(2)}) collective-permute-start(bf16[256,4096]{1,0:T(8,128)(2,1)S(1)} %add_convert_fusion.3.rest_1_), channel_id=1, source_target_pairs={{2,4},{3,5},{4,2},{5,3},{10,12},{11,13},{12,10},{13,11},{18,20},{1... | collective-permute-start | bytes 6291464 | tf_op jit(solution)/shard_map/ppermute | solution.py:420
  150.6 2.0 collective-permute-start.9
  (1 other events, 0.8 us)

commit v4 on v3

--- a/solution.py
+++ b/solution.py
@@ -9,6 +9,7 @@
 
 LANES = 128
 CHUNK = 128
+PARTS = 2
 BF16 = jnp.bfloat16
 F32 = jnp.float32
 
@@ -37,7 +38,7 @@
         tile_ref[f] = jnp.where(keep, rolled, 0.0).astype(BF16)
 
 
-def short_conv(stream, stage_ref, x_ref, rim_ref, taps_ref, k):
+def short_conv(stream, stage_ref, taps_ref, k):
     at = 8 + k * CHUNK
     return (
         taps_ref[0, stream : stream + 1, :] * stage_ref[at : at + CHUNK, :]
@@ -46,10 +47,15 @@
     )
 
 
-def stage(stream, stage_ref, x_ref, rim_ref):
+def stage(stage_ref, x_ref, rim):
     stage_ref[0:8, :] = jnp.zeros((8, LANES), F32)
-    stage_ref[6:8, :] = rim_ref[stream].astype(F32)
+    stage_ref[6:8, :] = rim.astype(F32)
     stage_ref[8:, :] = x_ref[0].astype(F32)
+
+
+def in_turns(body):
+    for _ in zip(*(body(part, slice(part * LANES, (part + 1) * LANES)) for part in range(PARTS))):
+        pass
 
 
 def diagonal(modes, group):
@@ -61,28 +67,35 @@
 
 
 def gate_kernel(
-    modes, group, k_ref, v_ref, rim_ref, taps_ref, rate_ref, gated_ref, start_ref, state_ref, k_stage, v_stage
+    modes, group, k_ref, v_ref, rim_ref, taps_ref, rate_ref, gated_ref, start_ref, state_ref, k_stages, v_stages
 ):
-    stage(1, k_stage, k_ref, rim_ref)
-    stage(2, v_stage, v_ref, rim_ref)
-    rate = rate_ref[...]
-    ends = jnp.exp(-rate * (CHUNK - 1 - iota((LANES, CHUNK), 1)).astype(F32)).astype(BF16)
-    fade = jnp.exp(-rate * CHUNK)
-    state = jnp.zeros((LANES, LANES), F32)
     chunks = gated_ref.shape[0] // CHUNK
     per_block = chunks // start_ref.shape[0]
     own_modes = diagonal(modes, group)
     spots = (iota((group, LANES), 0) == lax.rem(iota((group, LANES), 1), group)).astype(BF16)
     fold = lambda value: dot(spots, jnp.where(own_modes, value, 0.0).astype(BF16), ((1,), (1,))).astype(BF16)
-    for k in range(chunks):
-        if k % per_block == 0:
-            start_ref[k // per_block] = fold(state)
-        gated = (
-            short_conv(1, k_stage, k_ref, rim_ref, taps_ref, k) * short_conv(2, v_stage, v_ref, rim_ref, taps_ref, k)
-        ).astype(BF16)
-        gated_ref[k * CHUNK : (k + 1) * CHUNK, :] = gated
-        state = fade * state + dot(ends, gated)
-    state_ref[...] = fold(state)
+
+    def body(part, lanes):
+        k_stage, v_stage, taps = k_stages.at[part], v_stages.at[part], taps_ref.at[:, :, lanes]
+        folded = slice(part * group, (part + 1) * group)
+        stage(k_stage, k_ref.at[:, :, lanes], rim_ref[1, :, lanes])
+        stage(v_stage, v_ref.at[:, :, lanes], rim_ref[2, :, lanes])
+        rate = rate_ref[lanes, :]
+        ends = jnp.exp(-rate * (CHUNK - 1 - iota((LANES, CHUNK), 1)).astype(F32)).astype(BF16)
+        fade = jnp.exp(-rate * CHUNK)
+        state = jnp.zeros((LANES, LANES), F32)
+        yield
+        for k in range(chunks):
+            if k % per_block == 0:
+                start_ref[k // per_block, folded, :] = fold(state)
+            gated = (short_conv(1, k_stage, taps, k) * short_conv(2, v_stage, taps, k)).astype(BF16)
+            gated_ref[k * CHUNK : (k + 1) * CHUNK, lanes] = gated
+            state = fade * state + dot(ends, gated)
+            yield
+        state_ref[folded, :] = fold(state)
+        yield
+
+    in_turns(body)
 
 
 def spread(modes, group, folded):
@@ -105,39 +118,45 @@
     row_scale_ref,
     *rest,
 ):
-    near_ref, query_ref, q_stage, sources, sums = rest[-5:]
-
-    stage(0, q_stage, q_ref, rim_ref)
-
-    @pl.when(window_ref[0] > 0)
-    def _():
-        q_stage[6:8, :] = before_ref[0].astype(F32)[before_ref.shape[1] - 2 :]
-
+    near_ref, query_ref, q_stages, all_sources, all_sums = rest[-5:]
     filters = LANES // group
     chunks = gated_ref.shape[0] // CHUNK
     eye = (iota((CHUNK, CHUNK), 0) == iota((CHUNK, CHUNK), 1)).astype(BF16)
-    for k in range(0, chunks, 2):
-        turned = dot(eye, gated_ref[k * CHUNK : (k + 2) * CHUNK, :], ((1,), (1,))).astype(BF16)
-        sources[k] = turned[:, :CHUNK]
-        sources[k + 1] = turned[:, CHUNK:]
-    for f in range(filters):
-        rows = slice(f * group, (f + 1) * group)
-        block = sources[:, rows, :].reshape(chunks * group, CHUNK)
-        sums[:, rows, :] = dot(block, tile_ref[f]).astype(BF16).reshape(chunks, group, CHUNK)
-    row_rate = row_rate_ref[0]
-    ends = jnp.exp(-row_rate * (CHUNK - 1 - iota((CHUNK, LANES), 0)).astype(F32)).astype(BF16)
-    reads = (row_scale_ref[0] * jnp.exp(-row_rate * (iota((CHUNK, LANES), 0) + 1).astype(F32))).astype(BF16)
-    both = jnp.concatenate([eye, reads], axis=1)
-    fade = jnp.exp(-row_rate * CHUNK)
     own_modes = diagonal(group, modes)
-    gain = gain_ref[...]
-    state = spread(modes, group, start_ref[0].astype(F32))
-    for k in range(chunks):
-        rows = slice(k * CHUNK, (k + 1) * CHUNK)
-        summed = dot(both, jnp.concatenate([sums[k], state.astype(BF16)], axis=1), ((1,), (1,)))
-        state = fade * state + jnp.where(own_modes, dot(sources[k], ends), 0.0)
-        near_ref[rows, :] = (summed + gain * gated_ref[rows, :].astype(F32)).astype(BF16)
-        query_ref[rows, :] = short_conv(0, q_stage, q_ref, rim_ref, taps_ref, k).astype(BF16)
+    inside = window_ref[0] > 0
+
+    def body(part, lanes):
+        q_stage, sources, sums = q_stages.at[part], all_sources.at[part], all_sums.at[part]
+        taps = taps_ref.at[:, :, lanes]
+        before = before_ref[0, :, lanes].astype(F32)[before_ref.shape[1] - 2 :]
+        stage(q_stage, q_ref.at[:, :, lanes], jnp.where(inside, before, rim_ref[0, :, lanes].astype(F32)))
+        yield
+        for k in range(0, chunks, 2):
+            turned = dot(eye, gated_ref[k * CHUNK : (k + 2) * CHUNK, lanes], ((1,), (1,))).astype(BF16)
+            sources[k] = turned[:, :CHUNK]
+            sources[k + 1] = turned[:, CHUNK:]
+            yield
+        for f in range(filters):
+            rows = slice(f * group, (f + 1) * group)
+            block = sources[:, rows, :].reshape(chunks * group, CHUNK)
+            sums[:, rows, :] = dot(block, tile_ref[part * filters + f]).astype(BF16).reshape(chunks, group, CHUNK)
+            yield
+        row_rate = row_rate_ref[part]
+        ends = jnp.exp(-row_rate * (CHUNK - 1 - iota((CHUNK, LANES), 0)).astype(F32)).astype(BF16)
+        reads = (row_scale_ref[part] * jnp.exp(-row_rate * (iota((CHUNK, LANES), 0) + 1).astype(F32))).astype(BF16)
+        both = jnp.concatenate([eye, reads], axis=1)
+        fade = jnp.exp(-row_rate * CHUNK)
+        gain = gain_ref[:, lanes]
+        state = spread(modes, group, start_ref[0, part * group : (part + 1) * group, :].astype(F32))
+        for k in range(chunks):
+            rows = slice(k * CHUNK, (k + 1) * CHUNK)
+            summed = dot(both, jnp.concatenate([sums[k], state.astype(BF16)], axis=1), ((1,), (1,)))
+            state = fade * state + jnp.where(own_modes, dot(sources[k], ends), 0.0)
+            near_ref[rows, lanes] = (summed + gain * gated_ref[rows, lanes].astype(F32)).astype(BF16)
+            query_ref[rows, lanes] = short_conv(0, q_stage, taps, k).astype(BF16)
+            yield
+
+    in_turns(body)
 
 
 def mix_kernel(modes, group, tok_rows, size, where_ref, near_ref, query_ref, row_rate_ref, row_scale_ref, *rest):
@@ -297,13 +316,13 @@
 
     square = pl.BlockSpec((LANES, LANES), lambda g: (g, 0))
     tile_spec = pl.BlockSpec((per_block, CHUNK, CHUNK), lambda g: (g, 0, 0))
-    lanes_spec = pl.BlockSpec((tok_rows, LANES), lambda g: (0, g))
-    rim_spec = pl.BlockSpec((streams, 2, LANES), lambda g: (0, 0, g))
-    taps_spec = pl.BlockSpec((3, streams, LANES), lambda g: (0, 0, g))
-    state_spec = pl.BlockSpec((group, LANES), lambda g: (g, 0))
+    wide_lanes = PARTS * LANES
+    lanes_spec = pl.BlockSpec((tok_rows, wide_lanes), lambda g: (0, g))
+    rim_spec = pl.BlockSpec((streams, 2, wide_lanes), lambda g: (0, 0, g))
+    taps_spec = pl.BlockSpec((3, streams, wide_lanes), lambda g: (0, 0, g))
 
     def stream_spec(i):
-        return pl.BlockSpec((1, tok_rows, LANES), lambda g: (i, 0, g))
+        return pl.BlockSpec((1, tok_rows, wide_lanes), lambda g: (i, 0, g))
 
     tiles = pl.pallas_call(
         functools.partial(toeplitz_kernel, modes),
@@ -316,13 +335,23 @@
         name="toeplitz",
     )(rate_cols, scale_cols)
 
-    stage_shape = pltpu.VMEM((8 + tok_rows, LANES), F32)
+    stage_shape = pltpu.VMEM((PARTS, 8 + tok_rows, LANES), F32)
     wide = jax.ShapeDtypeStruct((tok_rows, channels), BF16)
     gated, starts, state = pl.pallas_call(
         functools.partial(gate_kernel, modes, group),
-        grid=(blocks,),
-        in_specs=[stream_spec(1), stream_spec(2), rim_spec, taps_spec, square],
-        out_specs=[lanes_spec, pl.BlockSpec((parts, group, LANES), lambda g: (0, g, 0)), state_spec],
+        grid=(blocks // PARTS,),
+        in_specs=[
+            stream_spec(1),
+            stream_spec(2),
+            rim_spec,
+            taps_spec,
+            pl.BlockSpec((wide_lanes, LANES), lambda g: (g, 0)),
+        ],
+        out_specs=[
+            lanes_spec,
+            pl.BlockSpec((parts, PARTS * group, LANES), lambda g: (0, g, 0)),
+            pl.BlockSpec((PARTS * group, LANES), lambda g: (g, 0)),
+        ],
         out_shape=[
             wide,
             jax.ShapeDtypeStruct((parts, blocks * group, LANES), BF16),
@@ -342,31 +371,29 @@
 
     def convolve(source, window, rows, *earlier):
         spans = rows // tail
-        window_spec = pl.BlockSpec((rows, LANES), lambda g, at: (at[0], g))
+        window_spec = pl.BlockSpec((rows, wide_lanes), lambda g, at: (at[0], g))
+        rows_spec = pl.BlockSpec((PARTS, 1, LANES), lambda g, at: (g, 0, 0))
+        turned_shape = pltpu.VMEM((PARTS, rows // CHUNK, LANES, CHUNK), BF16)
         return pl.pallas_call(
             functools.partial(near_kernel, modes, group),
             grid_spec=pltpu.PrefetchScalarGridSpec(
                 num_scalar_prefetch=1,
-                grid=(blocks,),
+                grid=(blocks // PARTS,),
                 in_specs=[
                     window_spec,
-                    pl.BlockSpec((1, group, LANES), lambda g, at: (at[0], g, 0)),
-                    pl.BlockSpec((per_block, CHUNK, CHUNK), lambda g, at: (g, 0, 0)),
-                    pl.BlockSpec((1, rows, LANES), lambda g, at: (0, at[0], g)),
-                    pl.BlockSpec((1, tail, LANES), lambda g, at: (0, jnp.maximum(at[0] * spans - 1, 0), g)),
-                    pl.BlockSpec((streams, 2, LANES), lambda g, at: (0, 0, g)),
-                    pl.BlockSpec((3, streams, LANES), lambda g, at: (0, 0, g)),
-                    pl.BlockSpec((1, LANES), lambda g, at: (0, g)),
-                    row_spec,
-                    row_spec,
+                    pl.BlockSpec((1, PARTS * group, LANES), lambda g, at: (at[0], g, 0)),
+                    pl.BlockSpec((PARTS * per_block, CHUNK, CHUNK), lambda g, at: (g, 0, 0)),
+                    pl.BlockSpec((1, rows, wide_lanes), lambda g, at: (0, at[0], g)),
+                    pl.BlockSpec((1, tail, wide_lanes), lambda g, at: (0, jnp.maximum(at[0] * spans - 1, 0), g)),
+                    pl.BlockSpec((streams, 2, wide_lanes), lambda g, at: (0, 0, g)),
+                    pl.BlockSpec((3, streams, wide_lanes), lambda g, at: (0, 0, g)),
+                    pl.BlockSpec((1, wide_lanes), lambda g, at: (0, g)),
+                    rows_spec,
+                    rows_spec,
                 ]
                 + [corner(value) for value in earlier],
-                out_specs=[pl.BlockSpec((rows, LANES), lambda g, at: (0, g))] * 2,
-                scratch_shapes=[
-                    pltpu.VMEM((8 + rows, LANES), F32),
-                    pltpu.VMEM((rows // CHUNK, LANES, CHUNK), BF16),
-                    pltpu.VMEM((rows // CHUNK, LANES, CHUNK), BF16),
-                ],
+                out_specs=[pl.BlockSpec((rows, wide_lanes), lambda g, at: (0, g))] * 2,
+                scratch_shapes=[pltpu.VMEM((PARTS, 8 + rows, LANES), F32), turned_shape, turned_shape],
             ),
             out_shape=[jax.ShapeDtypeStruct((rows, channels), BF16)] * 2,
             compiler_params=params(),
@@ -450,7 +477,7 @@
     inner = send(inner_sum, across)
     own = multiply(place, others[2], outer, inner_sum)
     outer = send(add(outer, join(crossed)), outward)
-    return add(add(own, outer, last), inner)
+    return add(add_after((own, outer, last), ()), inner)
 
 
 def solution(mesh):

time: 203 us -> 197 us (0.970)
  other arithmetic: 13.7 us -> 10.2 us
  Pallas kernels: 109 us -> 106 us
  waiting for transfers between devices: 41.1 us -> 38.7 us
    pallas_call x3, Pallas kernels: 32 us -> 25.8 us  [convolve(): pl.pallas_call(functools.partial(near_kernel, modes, group), grid_spec=pl...]
    pallas_call x1 -> x2, Pallas kernels: 1.18 us -> 6.13 us  [add_after(): pl.pallas_call(functools.partial(sum_kernel, len(values)), grid=(width //...]
    convert_element_type x4, other arithmetic: 12.6 us -> 9.08 us  [add(): return total.astype(BF16)]
    ppermute x13, waiting for transfers between devices: 41.1 us -> 38.7 us  [on_device(): send = lambda value, hops: lax.ppermute(value, 'chan', hops)]
  transfers between devices with their start and end apart: 18 -> 18, of which waited for: 7 -> 7; matrix products, arithmetic and copies ran while one was open for 6% -> 5% of each run, Pallas kernels for 51% -> 52%
where the time goes in v4:
time: 197 us; the launch traced here: 194 us
  Pallas kernels  106 us (54%)
  waiting for transfers between devices  38.7 us (20%)
  starting transfers between devices  33.9 us (17%)
  other arithmetic  10.2 us (5%)
  local copies, waits for them, and re-layouts  5.27 us (3%)
    pallas_call x6, Pallas kernels, product(): pl.pallas_call(product_kernel, grid_spec=pltpu.PrefetchScalarGridSpec(num...  47.1 us
    ppermute x13, waiting for transfers between devices, on_device(): send = lambda value, hops: lax.ppermute(value, 'chan', hops)  38.7 us
    pallas_call x3, Pallas kernels, convolve(): pl.pallas_call(functools.partial(near_kernel, modes, group), grid_spec=pl...  25.8 us
    ppermute x13, starting transfers between devices, on_device(): send = lambda value, hops: lax.ppermute(value, 'chan', hops)  21.7 us
    pallas_call x3, Pallas kernels, finish(): pl.pallas_call(functools.partial(mix_kernel, modes, group, tok_rows, size...  16.2 us
    ppermute x4, starting transfers between devices, shifted(): lax.ppermute(value, axis, [(i, i + steps) for i in range(count - steps)])  12.2 us
    pallas_call x1, Pallas kernels, on_device(): pl.pallas_call(functools.partial(gate_kernel, modes, group), grid=(blocks...  9.35 us
    convert_element_type x4, other arithmetic, add(): return total.astype(BF16)  9.08 us
  transfers between devices with their start and end apart: 18, of which 7 were waited for; matrix products, arithmetic and copies ran while one was open for 5% of the time, Pallas kernels for 52%

profile of v4, /device:TPU:16, one launch (start us, length us, event | category | flops | bytes accessed | tf_op | source)
XLA Modules:
  0.0 194.4 jit_solution(11903089491732276534)
XLA Ops:
  0.8 3.4 %collective-permute-start = (bf16[2,3,1024]{2,0,1:T(2,128)(2,1)S(1)}, bf16[2,3,1024]{2,0,1:T(2,128)(2,1)S(1)}, u32[]{:S(2)}, u32[]{:S(2)}) collective-permute-start(bf16[2,3,1024]{2,0,1:T(2,128)(2,1)S(1)} %slice.3), channel_id=1, source_target_pairs={{0,8},{8,16},{16,24},{1,9},{9,17},{17,25},{2,10},{10,18},{18,26},{... | collective-permute-start | bytes 36872 | tf_op jit(solution)/shard_map/ppermute | solution.py:253
  6.8 9.3 %gate.1 = (bf16[2048,1024]{1,0:T(8,128)(2,1)S(1)}, bf16[4,128,128]{2,1,0:T(8,128)(2,1)S(1)}, bf16[128,128]{1,0:T(8,128)(2,1)S(1)}) custom-call(bf16[3,2048,1024]{2,1,0:T(8,128)(2,1)} %bitcast.30, bf16[3,2048,1024]{2,1,0:T(8,128)(2,1)} %bitcast.31, bf16[3,2,1024]{2,1,0:T(2,128)(2,1)S(1)} %bitcast.23, f32[3,3,1024]{2,1,0:T(4,128)S(1)} %copy-done.3, ...), custom_call_target="tpu_custom_call" | custom-call | flops 8388608 | bytes 196608 | tf_op jit(solution)/shard_map/gate/pallas_call | solution.py:340
  18.2 4.1 %collective-permute-start.1 = (bf16[128,128]{1,0:T(8,128)(2,1)S(1)}, bf16[128,128]{1,0:T(8,128)(2,1)S(1)}, u32[]{:S(2)}, u32[]{:S(2)}) collective-permute-start(bf16[128,128]{1,0:T(8,128)(2,1)S(1)} %get-tuple-element.24), channel_id=1, source_target_pairs={{0,8},{8,16},{16,24},{1,9},{9,17},{17,25},{2,10},{10,18},{18,26},{... | collective-permute-start | bytes 98312 | tf_op jit(solution)/shard_map/ppermute | solution.py:253
  22.3 3.4 %collective-permute-start.2 = (bf16[128,128]{1,0:T(8,128)(2,1)S(1)}, bf16[128,128]{1,0:T(8,128)(2,1)S(1)}, u32[]{:S(2)}, u32[]{:S(2)}) collective-permute-start(bf16[128,128]{1,0:T(8,128)(2,1)S(1)} %get-tuple-element.24), channel_id=1, source_target_pairs={{0,16},{8,24},{1,17},{9,25},{2,18},{10,26},{3,19},{11,27},{4,20},{... | collective-permute-start | bytes 98312 | tf_op jit(solution)/shard_map/ppermute | solution.py:253
  29.0 5.5 %near.3 = (bf16[512,1024]{1,0:T(8,128)(2,1)S(1)}, bf16[512,1024]{1,0:T(8,128)(2,1)S(1)}) custom-call(s32[1]{0:T(128)} %bitcast.8.window_ref, bf16[2048,1024]{1,0:T(8,128)(2,1)} %copy-done, bf16[4,128,128]{2,1,0:T(8,128)(2,1)S(1)} %get-tuple-element.21.start_ref, bf16[64,128,128]{2,1,0:T(8,128)(2,1)S(1)} %toeplitz.1.tile_ref, ...), custom_call_target="tpu_custom_call" | custom-call | flops 8388608 | bytes 65536 | tf_op jit(solution)/shard_map/near/pallas_call | solution.py:377
  34.5 3.5 %mix.3 = (bf16[1,256,1024]{2,1,0:T(8,128)(2,1)S(1)}, bf16[1,256,1024]{2,1,0:T(8,128)(2,1)S(1)}) custom-call(s32[2]{0:T(128)S(1)} %get-tuple-element.39.where_ref, bf16[512,1024]{1,0:T(8,128)(2,1)S(1)} %get-tuple-element.22.near_ref, bf16[512,1024]{1,0:T(8,128)(2,1)S(1)} %get-tuple-element.23.query_ref, f32[8,1,128]{2,1,0:T(1,128)S(1)} %bitcast.12, ...), custom_call_target="tpu_custom_call" | custom-call | flops 2097152 | bytes 65536 | tf_op jit(solution)/shard_map/mix/pallas_call | solution.py:421
  40.0 5.4 %product.6.rest_0_ = bf16[256,2048]{1,0:T(8,128)(2,1)S(1)} custom-call(s32[2]{0:T(128)S(1)} %broadcast_1_which_ref.2.which_ref, bf16[1,256,1024]{2,1,0:T(8,128)(2,1)S(1)} %get-tuple-element.25.own_ref, bf16[1,256,1024]{2,1,0:T(8,128)(2,1)S(1)} %collective-permute-done.4.other_ref, bf16[1024,4096]{1,0:T(8,128)(2,1)} %own_w_ref.11, ...), custom_call_target="tpu_custom_call" | custom-call | flops 33554432 | bytes 180224 | tf_op jit(solution)/shard_map/product/pallas_call | solution.py:203
  46.7 5.4 %product.7.rest_0_.refs_0_ = bf16[256,2048]{1,0:T(8,128)(2,1)S(1)} custom-call(s32[2]{0:T(128)S(1)} %broadcast_1_which_ref.2.which_ref, bf16[1,256,1024]{2,1,0:T(8,128)(2,1)S(1)} %get-tuple-element.25.own_ref, bf16[1,256,1024]{2,1,0:T(8,128)(2,1)S(1)} %collective-permute-done.4.other_ref, bf16[1024,4096]{1,0:T(8,128)(2,1)} %own_w_ref.11, ...), custom_call_target="tpu_custom_call" | custom-call | flops 33554432 | bytes 180224 | tf_op jit(solution)/shard_map/product/pallas_call | solution.py:203
  52.1 5.5 %near.4 = (bf16[512,1024]{1,0:T(8,128)(2,1)S(1)}, bf16[512,1024]{1,0:T(8,128)(2,1)S(1)}) custom-call(s32[1]{0:T(128)} %bitcast.7.window_ref, bf16[2048,1024]{1,0:T(8,128)(2,1)} %copy-done, bf16[4,128,128]{2,1,0:T(8,128)(2,1)S(1)} %get-tuple-element.21.start_ref, bf16[64,128,128]{2,1,0:T(8,128)(2,1)S(1)} %toeplitz.1.tile_ref, ...), custom_call_target="tpu_custom_call" | custom-call | flops 8388608 | bytes 65536 | tf_op jit(solution)/shard_map/near/pallas_call | solution.py:377
  57.6 3.5 %mix.4 = (bf16[1,256,1024]{2,1,0:T(8,128)(2,1)S(1)}, bf16[1,256,1024]{2,1,0:T(8,128)(2,1)S(1)}) custom-call(s32[2]{0:T(128)S(1)} %get-tuple-element.38.where_ref, bf16[512,1024]{1,0:T(8,128)(2,1)S(1)} %get-tuple-element.27.near_ref, bf16[512,1024]{1,0:T(8,128)(2,1)S(1)} %get-tuple-element.28.query_ref, f32[8,1,128]{2,1,0:T(1,128)S(1)} %bitcast.14, ...), custom_call_target="tpu_custom_call" | custom-call | flops 2097152 | bytes 65536 | tf_op jit(solution)/shard_map/mix/pallas_call | solution.py:421
  63.2 9.1 %product.8.rest_0_ = bf16[256,4096]{1,0:T(8,128)(2,1)S(1)} custom-call(s32[2]{0:T(128)S(1)} %broadcast_1_which_ref.2.which_ref, bf16[1,256,1024]{2,1,0:T(8,128)(2,1)S(1)} %get-tuple-element.29.own_ref, bf16[1,256,1024]{2,1,0:T(8,128)(2,1)S(1)} %collective-permute-done.6.other_ref, bf16[1024,4096]{1,0:T(8,128)(2,1)} %own_w_ref.11, ...), custom_call_target="tpu_custom_call" | custom-call | flops 67108864 | bytes 360448 | tf_op jit(solution)/shard_map/product/pallas_call | solution.py:203
  77.3 14.8 %near.5 = (bf16[2048,1024]{1,0:T(8,128)(2,1)}, bf16[2048,1024]{1,0:T(8,128)(2,1)}) custom-call(s32[1]{0:T(128)} %constant.36.clone.1.window_ref, bf16[2048,1024]{1,0:T(8,128)(2,1)} %copy-done, bf16[4,128,128]{2,1,0:T(8,128)(2,1)S(1)} %get-tuple-element.21.start_ref, bf16[64,128,128]{2,1,0:T(8,128)(2,1)S(1)} %toeplitz.1.tile_ref, ...), custom_call_target="tpu_custom_call" | custom-call | flops 33554432 | bytes 262144 | tf_op jit(solution)/shard_map/near/pallas_call | solution.py:377
  92.0 3.8 %collective-permute-done.8.refs_1_ = bf16[256,2048]{1,0:T(8,128)(2,1)S(1)} collective-permute-done((bf16[256,2048]{1,0:T(8,128)(2,1)S(1)}, bf16[256,2048]{1,0:T(8,128)(2,1)S(1)}, u32[]{:S(2)}, u32[]{:S(2)}) %collective-permute-start.8) | collective-permute-done | bytes 1048608 | tf_op jit(solution)/shard_map/ppermute | solution.py:447
  97.0 2.5 %collective-permute-start.14 = (bf16[256,2048]{1,0:T(8,128)(2,1)S(1)}, bf16[256,2048]{1,0:T(8,128)(2,1)}, u32[]{:S(2)}, u32[]{:S(2)}) collective-permute-start(bf16[256,2048]{1,0:T(8,128)(2,1)S(1)} %sum.2.rest_3_), channel_id=1, source_target_pairs={{2,4},{3,5},{4,2},{5,3},{10,12},{11,13},{12,10},{13,11},{18,20},{1... | collective-permute-start | bytes 3145736 | tf_op jit(solution)/shard_map/ppermute | solution.py:447
  99.6 9.1 %mix.5 = (bf16[4,256,1024]{2,1,0:T(8,128)(2,1)S(1)}, bf16[4,256,1024]{2,1,0:T(8,128)(2,1)S(1)}) custom-call(s32[2]{0:T(128)S(1)} %pad_add_fusion.2.where_ref, bf16[2048,1024]{1,0:T(8,128)(2,1)} %get-tuple-element.31.refs_2_.near_ref, bf16[2048,1024]{1,0:T(8,128)(2,1)} %get-tuple-element.32.query_ref, f32[8,1,128]{2,1,0:T(1,128)S(1)} %bitcast.16, ...), custom_call_target="tpu_custom_call" | custom-call | flops 8388608 | bytes 262144 | tf_op jit(solution)/shard_map/mix/pallas_call | solution.py:421
  110.8 9.1 %product.9.rest_0_ = bf16[256,4096]{1,0:T(8,128)(2,1)S(1)} custom-call(s32[2]{0:T(128)S(1)} %pad_add_fusion.which_ref, bf16[4,256,1024]{2,1,0:T(8,128)(2,1)S(1)} %get-tuple-element.33.own_ref, bf16[1,256,1024]{2,1,0:T(8,128)(2,1)S(1)} %collective-permute-done.11.other_ref, bf16[1024,4096]{1,0:T(8,128)(2,1)} %own_w_ref.11, ...), custom_call_target="tpu_custom_call" | custom-call | flops 67108864 | bytes 360448 | tf_op jit(solution)/shard_map/product/pallas_call | solution.py:203
  121.2 9.1 %product.10.rest_0_ = bf16[256,4096]{1,0:T(8,128)(2,1)S(1)} custom-call(s32[2]{0:T(128)S(1)} %pad_add_fusion.1.which_ref, bf16[4,256,1024]{2,1,0:T(8,128)(2,1)S(1)} %get-tuple-element.33.own_ref, bf16[1,256,1024]{2,1,0:T(8,128)(2,1)S(1)} %collective-permute-done.10.other_ref, bf16[1024,4096]{1,0:T(8,128)(2,1)} %own_w_ref.11, ...), custom_call_target="tpu_custom_call" | custom-call | flops 67108864 | bytes 360448 | tf_op jit(solution)/shard_map/product/pallas_call | solution.py:203
  130.4 3.2 %add_convert_fusion.1 = bf16[256,4096]{1,0:T(8,128)(2,1)S(1)} fusion(bf16[256,4096]{1,0:T(8,128)(2,1)S(1)} %product.10.rest_0_, bf16[256,2048]{1,0:T(8,128)(2,1)} %collective-permute-done.14, bf16[256,2048]{1,0:T(8,128)(2,1)} %collective-permute-done.12.rest_1_), kind=kLoop, calls=%fused_computation.1 | loop fusion | flops 7340032 | bytes 6291456 | tf_op jit(solution)/shard_map/convert_element_type | solution.py:260
  133.6 7.2 %collective-permute-start.15 = (bf16[256,4096]{1,0:T(8,128)(2,1)S(1)}, bf16[256,4096]{1,0:T(8,128)(2,1)}, u32[]{:S(2)}, u32[]{:S(2)}) collective-permute-start(bf16[256,4096]{1,0:T(8,128)(2,1)S(1)} %add_convert_fusion.1), channel_id=1, source_target_pairs={{2,0},{3,1},{4,6},{5,7},{10,8},{11,9},{12,14},{13,15},{18,16},{19,... | collective-permute-start | bytes 6291464 | tf_op jit(solution)/shard_map/ppermute | solution.py:447
  140.9 2.4 %add_convert_fusion.2.rest_1_ = bf16[256,4096]{1,0:T(8,128)(2,1)S(1)} fusion(bf16[256,4096]{1,0:T(8,128)(2,1)} %collective-permute-done.13, bf16[256,4096]{1,0:T(8,128)(2,1)S(1)} %product.8.rest_0_), kind=kLoop, calls=%fused_computation.2 | loop fusion | flops 4194304 | bytes 6291456 | tf_op jit(solution)/shard_map/convert_element_type | solution.py:260
  143.3 3.5 %collective-permute-start.17 = (bf16[256,4096]{1,0:T(8,128)(2,1)S(1)}, bf16[256,4096]{1,0:T(8,128)(2,1)S(1)}, u32[]{:S(2)}, u32[]{:S(2)}) collective-permute-start(bf16[256,4096]{1,0:T(8,128)(2,1)S(1)} %add_convert_fusion.2.rest_1_), channel_id=1, source_target_pairs={{2,4},{3,5},{4,2},{5,3},{10,12},{11,13},{12,10},{13,11},{18,20},{1... | collective-permute-start | bytes 6291464 | tf_op jit(solution)/shard_map/ppermute | solution.py:447
  148.8 9.1 %product.11.refs_0_ = bf16[256,4096]{1,0:T(8,128)(2,1)S(1)} custom-call(s32[2]{0:T(128)S(1)} %pad_add_fusion.3.which_ref, bf16[4,256,1024]{2,1,0:T(8,128)(2,1)S(1)} %get-tuple-element.33.own_ref, bf16[1,256,1024]{2,1,0:T(8,128)(2,1)S(1)} %collective-permute-done.9.other_ref, bf16[1024,4096]{1,0:T(8,128)(2,1)} %own_w_ref.11, ...), custom_call_target="tpu_custom_call" | custom-call | flops 67108864 | bytes 360448 | tf_op jit(solution)/shard_map/product/pallas_call | solution.py:203
  157.9 27.1 %collective-permute-done.16.refs_2_ = bf16[256,4096]{1,0:T(8,128)(2,1)} collective-permute-done((bf16[256,4096]{1,0:T(8,128)(2,1)S(1)}, bf16[256,4096]{1,0:T(8,128)(2,1)}, u32[]{:S(2)}, u32[]{:S(2)}) %collective-permute-start.16) | collective-permute-done | bytes 2097184 | tf_op jit(solution)/shard_map/ppermute | solution.py:447
  185.0 5.0 %sum.3 = bf16[256,4096]{1,0:T(8,128)(2,1)S(1)} custom-call(bf16[256,4096]{1,0:T(8,128)(2,1)S(1)} %product.11.refs_0_, bf16[256,4096]{1,0:T(8,128)(2,1)} %collective-permute-done.15.refs_1_, bf16[256,4096]{1,0:T(8,128)(2,1)} %collective-permute-done.16.refs_2_), custom_call_target="tpu_custom_call" | custom-call | flops 49152 | bytes 98304 | tf_op jit(solution)/shard_map/sum/pallas_call | solution.py:239
  (63 shorter events, 29.9 us)
Async XLA Ops:
  0.0 40.0 %collective-permute-start.5 = (bf16[1024,4096]{1,0:T(8,128)(2,1)}, bf16[1024,4096]{1,0:T(8,128)(2,1)}, u32[]{:S(2)}, u32[]{:S(2)}) collective-permute-start(bf16[1024,4096]{1,0:T(8,128)(2,1)} %own_w_ref.11), channel_id=1, source_target_pairs={{0,1},{1,0},{2,3},{3,2},{4,5},{5,4},{6,7},{7,6},{8,9},{9,8},{10,11... | collective-permute-start | bytes 25165832 | tf_op jit(solution)/shard_map/ppermute | solution.py:308
  0.8 5.0 %collective-permute-start = (bf16[2,3,1024]{2,0,1:T(2,128)(2,1)S(1)}, bf16[2,3,1024]{2,0,1:T(2,128)(2,1)S(1)}, u32[]{:S(2)}, u32[]{:S(2)}) collective-permute-start(bf16[2,3,1024]{2,0,1:T(2,128)(2,1)S(1)} %slice.3), channel_id=1, source_target_pairs={{0,8},{8,16},{16,24},{1,9},{9,17},{17,25},{2,10},{10,18},{18,26},{... | collective-permute-start | bytes 36872 | tf_op jit(solution)/shard_map/ppermute | solution.py:253
  16.2 2.0 %copy-start = (bf16[2048,1024]{1,0:T(8,128)(2,1)}, bf16[2048,1024]{1,0:T(8,128)(2,1)S(1)}, u32[]{:S(2)}) copy-start(bf16[2048,1024]{1,0:T(8,128)(2,1)S(1)} %get-tuple-element.20.gated_ref) | copy-start | bytes 12582916
  18.2 10.8 %copy-start.4 = (f32[3,3,1024]{2,1,0:T(4,128)S(1)}, f32[3,3,1024]{2,1,0:T(4,128)}, u32[]{:S(2)}) copy-start(f32[3,3,1024]{2,1,0:T(4,128)} %taps_ref.7) | copy-start | bytes 110596
  18.2 10.8 %copy-start.5 = (f32[1024]{0:T(1024)S(1)}, f32[1024]{0:T(1024)}, u32[]{:S(2)}) copy-start(f32[1024]{0:T(1024)} %param.10) | copy-start | bytes 12292
  18.2 16.3 %collective-permute-start.1 = (bf16[128,128]{1,0:T(8,128)(2,1)S(1)}, bf16[128,128]{1,0:T(8,128)(2,1)S(1)}, u32[]{:S(2)}, u32[]{:S(2)}) collective-permute-start(bf16[128,128]{1,0:T(8,128)(2,1)S(1)} %get-tuple-element.24), channel_id=1, source_target_pairs={{0,8},{8,16},{16,24},{1,9},{9,17},{17,25},{2,10},{10,18},{18,26},{... | collective-permute-start | bytes 98312 | tf_op jit(solution)/shard_map/ppermute | solution.py:253
  22.3 12.2 %collective-permute-start.2 = (bf16[128,128]{1,0:T(8,128)(2,1)S(1)}, bf16[128,128]{1,0:T(8,128)(2,1)S(1)}, u32[]{:S(2)}, u32[]{:S(2)}) collective-permute-start(bf16[128,128]{1,0:T(8,128)(2,1)S(1)} %get-tuple-element.24), channel_id=1, source_target_pairs={{0,16},{8,24},{1,17},{9,25},{2,18},{10,26},{3,19},{11,27},{4,20},{... | collective-permute-start | bytes 98312 | tf_op jit(solution)/shard_map/ppermute | solution.py:253
  25.7 8.8 %collective-permute-start.3 = (bf16[128,128]{1,0:T(8,128)(2,1)S(1)}, bf16[128,128]{1,0:T(8,128)(2,1)S(1)}, u32[]{:S(2)}, u32[]{:S(2)}) collective-permute-start(bf16[128,128]{1,0:T(8,128)(2,1)S(1)} %get-tuple-element.24), channel_id=1, source_target_pairs={{0,24},{1,25},{2,26},{3,27},{4,28},{5,29},{6,30},{7,31}} | collective-permute-start | bytes 98312 | tf_op jit(solution)/shard_map/ppermute | solution.py:253
  38.0 2.0 %collective-permute-start.4 = (bf16[1,256,1024]{2,1,0:T(8,128)(2,1)S(1)}, bf16[1,256,1024]{2,1,0:T(8,128)(2,1)S(1)}, u32[]{:S(2)}, u32[]{:S(2)}) collective-permute-start(bf16[1,256,1024]{2,1,0:T(8,128)(2,1)S(1)} %get-tuple-element.26), channel_id=1, source_target_pairs={{0,1},{1,0},{2,3},{3,2},{4,5},{5,4},{6,7},{7,6},{8,9},{9,8},{10,11... | collective-permute-start | bytes 1572872 | tf_op jit(solution)/shard_map/ppermute | solution.py:447
  45.4 28.1 %collective-permute-start.7 = (bf16[256,2048]{1,0:T(8,128)(2,1)S(1)}, bf16[256,2048]{1,0:T(8,128)(2,1)S(1)}, u32[]{:S(2)}, u32[]{:S(2)}) collective-permute-start(bf16[256,2048]{1,0:T(8,128)(2,1)S(1)} %product.6.rest_0_), channel_id=1, source_target_pairs={{0,2},{1,3},{6,4},{7,5},{8,10},{9,11},{14,12},{15,13},{16,18},{17,... | collective-permute-start | bytes 3145736 | tf_op jit(solution)/shard_map/ppermute | solution.py:447
  61.2 2.0 %collective-permute-start.6 = (bf16[1,256,1024]{2,1,0:T(8,128)(2,1)S(1)}, bf16[1,256,1024]{2,1,0:T(8,128)(2,1)S(1)}, u32[]{:S(2)}, u32[]{:S(2)}) collective-permute-start(bf16[1,256,1024]{2,1,0:T(8,128)(2,1)S(1)} %get-tuple-element.30), channel_id=1, source_target_pairs={{0,1},{1,0},{2,3},{3,2},{4,5},{5,4},{6,7},{7,6},{8,9},{9,8},{10,11... | collective-permute-start | bytes 1572872 | tf_op jit(solution)/shard_map/ppermute | solution.py:447
  61.4 34.4 %collective-permute-start.8 = (bf16[256,2048]{1,0:T(8,128)(2,1)S(1)}, bf16[256,2048]{1,0:T(8,128)(2,1)S(1)}, u32[]{:S(2)}, u32[]{:S(2)}) collective-permute-start(bf16[256,2048]{1,0:T(8,128)(2,1)S(1)} %product.7.rest_0_.refs_0_), channel_id=1, source_target_pairs={{0,2},{1,3},{6,4},{7,5},{8,10},{9,11},{14,12},{15,13},{16,18},{17,... | collective-permute-start | bytes 3145736 | tf_op jit(solution)/shard_map/ppermute | solution.py:447
  72.3 68.6 %collective-permute-start.13 = (bf16[256,4096]{1,0:T(8,128)(2,1)S(1)}, bf16[256,4096]{1,0:T(8,128)(2,1)}, u32[]{:S(2)}, u32[]{:S(2)}) collective-permute-start(bf16[256,4096]{1,0:T(8,128)(2,1)S(1)} %product.8.rest_0_), channel_id=1, source_target_pairs={{0,2},{1,3},{6,4},{7,5},{8,10},{9,11},{14,12},{15,13},{16,18},{17,... | collective-permute-start | bytes 6291464 | tf_op jit(solution)/shard_map/ppermute | solution.py:447
  74.9 46.3 %collective-permute-start.12 = (bf16[256,2048]{1,0:T(8,128)(2,1)}, bf16[256,2048]{1,0:T(8,128)(2,1)}, u32[]{:S(2)}, u32[]{:S(2)}) collective-permute-start(bf16[256,2048]{1,0:T(8,128)(2,1)} %add_convert_fusion.3.rest_1_), channel_id=1, source_target_pairs={{2,4},{3,5},{4,2},{5,3},{10,12},{11,13},{12,10},{13,11},{18,20},{1... | collective-permute-start | bytes 3145736 | tf_op jit(solution)/shard_map/ppermute | solution.py:447
  97.0 33.4 %collective-permute-start.14 = (bf16[256,2048]{1,0:T(8,128)(2,1)S(1)}, bf16[256,2048]{1,0:T(8,128)(2,1)}, u32[]{:S(2)}, u32[]{:S(2)}) collective-permute-start(bf16[256,2048]{1,0:T(8,128)(2,1)S(1)} %sum.2.rest_3_), channel_id=1, source_target_pairs={{2,4},{3,5},{4,2},{5,3},{10,12},{11,13},{12,10},{13,11},{18,20},{1... | collective-permute-start | bytes 3145736 | tf_op jit(solution)/shard_map/ppermute | solution.py:447
  108.8 2.0 %collective-permute-start.11 = (bf16[1,256,1024]{2,1,0:T(8,128)(2,1)S(1)}, bf16[1,256,1024]{2,1,0:T(8,128)(2,1)S(1)}, u32[]{:S(2)}, u32[]{:S(2)}) collective-permute-start(bf16[1,256,1024]{2,1,0:T(8,128)(2,1)S(1)} %get-tuple-element.35), channel_id=1, source_target_pairs={{0,1},{1,0},{2,3},{3,2},{4,5},{5,4},{6,7},{7,6},{8,9},{9,8},{10,11... | collective-permute-start | bytes 1572872 | tf_op jit(solution)/shard_map/ppermute | solution.py:447
  108.9 12.3 %collective-permute-start.10 = (bf16[1,256,1024]{2,1,0:T(8,128)(2,1)S(1)}, bf16[1,256,1024]{2,1,0:T(8,128)(2,1)S(1)}, u32[]{:S(2)}, u32[]{:S(2)}) collective-permute-start(bf16[1,256,1024]{2,1,0:T(8,128)(2,1)S(1)} %get-tuple-element.36), channel_id=1, source_target_pairs={{0,1},{1,0},{2,3},{3,2},{4,5},{5,4},{6,7},{7,6},{8,9},{9,8},{10,11... | collective-permute-start | bytes 1572872 | tf_op jit(solution)/shard_map/ppermute | solution.py:447
  119.9 1.3 copy-start.2
  119.9 65.0 %collective-permute-start.16 = (bf16[256,4096]{1,0:T(8,128)(2,1)S(1)}, bf16[256,4096]{1,0:T(8,128)(2,1)}, u32[]{:S(2)}, u32[]{:S(2)}) collective-permute-start(bf16[256,4096]{1,0:T(8,128)(2,1)S(1)} %product.9.rest_0_), channel_id=1, source_target_pairs={{0,2},{1,3},{6,4},{7,5},{8,10},{9,11},{14,12},{15,13},{16,18},{17,... | collective-permute-start | bytes 6291464 | tf_op jit(solution)/shard_map/ppermute | solution.py:447
  130.4 3.3 %copy-start.1 = (bf16[256,4096]{1,0:T(8,128)(2,1)}, bf16[256,4096]{1,0:T(8,128)(2,1)S(1)}, u32[]{:S(2)}) copy-start(bf16[256,4096]{1,0:T(8,128)(2,1)S(1)} %product.10.rest_0_) | copy-start | bytes 6291460
  133.6 51.3 %collective-permute-start.15 = (bf16[256,4096]{1,0:T(8,128)(2,1)S(1)}, bf16[256,4096]{1,0:T(8,128)(2,1)}, u32[]{:S(2)}, u32[]{:S(2)}) collective-permute-start(bf16[256,4096]{1,0:T(8,128)(2,1)S(1)} %add_convert_fusion.1), channel_id=1, source_target_pairs={{2,0},{3,1},{4,6},{5,7},{10,8},{11,9},{12,14},{13,15},{18,16},{19,... | collective-permute-start | bytes 6291464 | tf_op jit(solution)/shard_map/ppermute | solution.py:447
  143.3 5.5 %copy-start.6 = (bf16[256,4096]{1,0:T(8,128)(2,1)}, bf16[256,4096]{1,0:T(8,128)(2,1)S(1)}, u32[]{:S(2)}) copy-start(bf16[256,4096]{1,0:T(8,128)(2,1)S(1)} %add_convert_fusion.2.rest_1_) | copy-start | bytes 6291460
  143.3 49.0 %collective-permute-start.17 = (bf16[256,4096]{1,0:T(8,128)(2,1)S(1)}, bf16[256,4096]{1,0:T(8,128)(2,1)S(1)}, u32[]{:S(2)}, u32[]{:S(2)}) collective-permute-start(bf16[256,4096]{1,0:T(8,128)(2,1)S(1)} %add_convert_fusion.2.rest_1_), channel_id=1, source_target_pairs={{2,4},{3,5},{4,2},{5,3},{10,12},{11,13},{12,10},{13,11},{18,20},{1... | collective-permute-start | bytes 6291464 | tf_op jit(solution)/shard_map/ppermute | solution.py:447
  146.8 2.0 %collective-permute-start.9 = (bf16[1,256,1024]{2,1,0:T(8,128)(2,1)S(1)}, bf16[1,256,1024]{2,1,0:T(8,128)(2,1)S(1)}, u32[]{:S(2)}, u32[]{:S(2)}) collective-permute-start(bf16[1,256,1024]{2,1,0:T(8,128)(2,1)S(1)} %get-tuple-element.37), channel_id=1, source_target_pairs={{0,1},{1,0},{2,3},{3,2},{4,5},{5,4},{6,7},{7,6},{8,9},{9,8},{10,11... | collective-permute-start | bytes 1572872 | tf_op jit(solution)/shard_map/ppermute | solution.py:447
  (1 other events, 0.8 us)

commit v5 on v4

--- a/solution.py
+++ b/solution.py
@@ -9,7 +9,7 @@
 
 LANES = 128
 CHUNK = 128
-PARTS = 2
+PARTS = 4
 BF16 = jnp.bfloat16
 F32 = jnp.float32
 
@@ -164,22 +164,29 @@
     piece_refs = rest[: lax.axis_size("ctx") - 1]
     core = where_ref[0]
     first = (where_ref[1] * near_ref.shape[0]).astype(F32)
-    row_rate = row_rate_ref[0]
-    carried = jnp.zeros((group, LANES), F32)
-    for d, piece_ref in enumerate(piece_refs):
-        carried = carried + jnp.exp(-row_rate * float(d * tok_rows)) * piece_ref[...].astype(F32)
-    state = spread(modes, group, carried).astype(BF16)
-    reads = row_scale_ref[0] * jnp.exp(-row_rate * (iota((CHUNK, LANES), 0) + 1).astype(F32))
-    for k in range(near_ref.shape[0] // CHUNK):
-        rows = slice(k * CHUNK, (k + 1) * CHUNK)
-        fade = jnp.exp(-row_rate * (first + float(k * CHUNK)))
-        far = dot((reads * fade).astype(BF16), state, ((1,), (1,)))
-        mixed = (query_ref[rows, :].astype(F32) * (near_ref[rows, :].astype(F32) + far)).astype(BF16)
-        width = min(size, CHUNK)
-        for piece in range(0, CHUNK, width):
-            block, inner = divmod(k * CHUNK + piece, size)
-            side = lax.rem(core + block, 2)
-            mixed_ref[side, block // 2, inner : inner + width, :] = mixed[piece : piece + width]
+
+    def body(part, lanes):
+        row_rate = row_rate_ref[part]
+        folded = slice(part * group, (part + 1) * group)
+        carried = jnp.zeros((group, LANES), F32)
+        for d, piece_ref in enumerate(piece_refs):
+            carried = carried + jnp.exp(-row_rate * float(d * tok_rows)) * piece_ref[folded, :].astype(F32)
+        state = spread(modes, group, carried).astype(BF16)
+        reads = row_scale_ref[part] * jnp.exp(-row_rate * (iota((CHUNK, LANES), 0) + 1).astype(F32))
+        yield
+        for k in range(near_ref.shape[0] // CHUNK):
+            rows = slice(k * CHUNK, (k + 1) * CHUNK)
+            fade = jnp.exp(-row_rate * (first + float(k * CHUNK)))
+            far = dot((reads * fade).astype(BF16), state, ((1,), (1,)))
+            mixed = (query_ref[rows, lanes].astype(F32) * (near_ref[rows, lanes].astype(F32) + far)).astype(BF16)
+            width = min(size, CHUNK)
+            for piece in range(0, CHUNK, width):
+                block, inner = divmod(k * CHUNK + piece, size)
+                side = lax.rem(core + block, 2)
+                mixed_ref[side, block // 2, inner : inner + width, lanes] = mixed[piece : piece + width]
+            yield
+
+    in_turns(body)
     keep_ref[...] = mixed_ref[0]
     give_ref[...] = mixed_ref[1]
 
@@ -417,18 +424,19 @@
     def finish(near, query, window, *earlier):
         rows = near.shape[0]
         held = rows // (2 * size)
-        out_spec = pl.BlockSpec((held, size, LANES), lambda g, at: (0, 0, g))
+        out_spec = pl.BlockSpec((held, size, wide_lanes), lambda g, at: (0, 0, g))
+        rows_spec = pl.BlockSpec((PARTS, 1, LANES), lambda g, at: (g, 0, 0))
         return pl.pallas_call(
             functools.partial(mix_kernel, modes, group, tok_rows, size),
             grid_spec=pltpu.PrefetchScalarGridSpec(
                 num_scalar_prefetch=1,
-                grid=(blocks,),
-                in_specs=[pl.BlockSpec((rows, LANES), lambda g, at: (0, g))] * 2
-                + [row_spec, row_spec]
-                + [pl.BlockSpec((group, LANES), lambda g, at: (g, 0))] * len(pieces)
+                grid=(blocks // PARTS,),
+                in_specs=[pl.BlockSpec((rows, wide_lanes), lambda g, at: (0, g))] * 2
+                + [rows_spec, rows_spec]
+                + [pl.BlockSpec((PARTS * group, LANES), lambda g, at: (g, 0))] * len(pieces)
                 + [corner(value) for value in earlier],
                 out_specs=[out_spec, out_spec],
-                scratch_shapes=[pltpu.VMEM((2, held, size, LANES), BF16)],
+                scratch_shapes=[pltpu.VMEM((2, held, size, wide_lanes), BF16)],
             ),
             out_shape=[jax.ShapeDtypeStruct((held, size, channels), BF16)] * 2,
             compiler_params=params(),

time: 197 us -> 193 us (0.980)
  Pallas kernels: 106 us -> 97.2 us
  waiting for transfers between devices: 38.7 us -> 44.8 us
    ppermute x13, waiting for transfers between devices: 38.7 us -> 44.8 us  [on_device(): send = lambda value, hops: lax.ppermute(value, 'chan', hops)]
    pallas_call x3, Pallas kernels: 16.2 us -> 11.4 us  [finish(): pl.pallas_call(functools.partial(mix_kernel, modes, group, tok_rows, size...]
    pallas_call x3, Pallas kernels: 25.8 us -> 21.9 us  [convolve(): pl.pallas_call(functools.partial(near_kernel, modes, group), grid_spec=pl...]
  transfers between devices with their start and end apart: 18 -> 18, of which waited for: 7 -> 9; matrix products, arithmetic and copies ran while one was open for 5% -> 6% of each run, Pallas kernels for 52% -> 48%
where the time goes in v5:
time: 193 us; the launch traced here: 191 us
  Pallas kernels  97.2 us (50%)
  waiting for transfers between devices  44.8 us (23%)
  starting transfers between devices  32.8 us (17%)
  other arithmetic  10.2 us (5%)
  local copies, waits for them, and re-layouts  5.27 us (3%)
    pallas_call x6, Pallas kernels, product(): pl.pallas_call(product_kernel, grid_spec=pltpu.PrefetchScalarGridSpec(num...  47.2 us
    ppermute x13, waiting for transfers between devices, on_device(): send = lambda value, hops: lax.ppermute(value, 'chan', hops)  44.8 us
    pallas_call x3, Pallas kernels, convolve(): pl.pallas_call(functools.partial(near_kernel, modes, group), grid_spec=pl...  21.9 us
    ppermute x13, starting transfers between devices, on_device(): send = lambda value, hops: lax.ppermute(value, 'chan', hops)  20.6 us
    ppermute x4, starting transfers between devices, shifted(): lax.ppermute(value, axis, [(i, i + steps) for i in range(count - steps)])  12.2 us
    pallas_call x3, Pallas kernels, finish(): pl.pallas_call(functools.partial(mix_kernel, modes, group, tok_rows, size...  11.4 us
    pallas_call x1, Pallas kernels, on_device(): pl.pallas_call(functools.partial(gate_kernel, modes, group), grid=(blocks...  9.31 us
    convert_element_type x4, other arithmetic, add(): return total.astype(BF16)  9.07 us
  transfers between devices with their start and end apart: 18, of which 9 were waited for; matrix products, arithmetic and copies ran while one was open for 6% of the time, Pallas kernels for 48%

profile of v5, /device:TPU:16, one launch (start us, length us, event | category | flops | bytes accessed | tf_op | source)
XLA Modules:
  0.0 190.8 jit_solution(6835536751224782431)
XLA Ops:
  0.8 3.4 %collective-permute-start = (bf16[2,3,1024]{2,0,1:T(2,128)(2,1)S(1)}, bf16[2,3,1024]{2,0,1:T(2,128)(2,1)S(1)}, u32[]{:S(2)}, u32[]{:S(2)}) collective-permute-start(bf16[2,3,1024]{2,0,1:T(2,128)(2,1)S(1)} %slice.3), channel_id=1, source_target_pairs={{0,8},{8,16},{16,24},{1,9},{9,17},{17,25},{2,10},{10,18},{18,26},{... | collective-permute-start | bytes 36872 | tf_op jit(solution)/shard_map/ppermute | solution.py:260
  6.8 9.3 %gate.1 = (bf16[2048,1024]{1,0:T(8,128)(2,1)S(1)}, bf16[4,128,128]{2,1,0:T(8,128)(2,1)S(1)}, bf16[128,128]{1,0:T(8,128)(2,1)S(1)}) custom-call(bf16[3,2048,1024]{2,1,0:T(8,128)(2,1)} %bitcast.30, bf16[3,2048,1024]{2,1,0:T(8,128)(2,1)} %bitcast.31, bf16[3,2,1024]{2,1,0:T(2,128)(2,1)S(1)} %bitcast.23, f32[3,3,1024]{2,1,0:T(4,128)S(1)} %copy-done.3, ...), custom_call_target="tpu_custom_call" | custom-call | flops 8388608 | bytes 196608 | tf_op jit(solution)/shard_map/gate/pallas_call | solution.py:347
  18.1 4.1 %collective-permute-start.1 = (bf16[128,128]{1,0:T(8,128)(2,1)S(1)}, bf16[128,128]{1,0:T(8,128)(2,1)S(1)}, u32[]{:S(2)}, u32[]{:S(2)}) collective-permute-start(bf16[128,128]{1,0:T(8,128)(2,1)S(1)} %get-tuple-element.24), channel_id=1, source_target_pairs={{0,8},{8,16},{16,24},{1,9},{9,17},{17,25},{2,10},{10,18},{18,26},{... | collective-permute-start | bytes 98312 | tf_op jit(solution)/shard_map/ppermute | solution.py:260
  22.2 3.4 %collective-permute-start.2 = (bf16[128,128]{1,0:T(8,128)(2,1)S(1)}, bf16[128,128]{1,0:T(8,128)(2,1)S(1)}, u32[]{:S(2)}, u32[]{:S(2)}) collective-permute-start(bf16[128,128]{1,0:T(8,128)(2,1)S(1)} %get-tuple-element.24), channel_id=1, source_target_pairs={{0,16},{8,24},{1,17},{9,25},{2,18},{10,26},{3,19},{11,27},{4,20},{... | collective-permute-start | bytes 98312 | tf_op jit(solution)/shard_map/ppermute | solution.py:260
  28.9 4.6 %near.3 = (bf16[512,1024]{1,0:T(8,128)(2,1)S(1)}, bf16[512,1024]{1,0:T(8,128)(2,1)S(1)}) custom-call(s32[1]{0:T(128)} %bitcast.8.window_ref, bf16[2048,1024]{1,0:T(8,128)(2,1)} %copy-done, bf16[4,128,128]{2,1,0:T(8,128)(2,1)S(1)} %get-tuple-element.21.start_ref, bf16[64,128,128]{2,1,0:T(8,128)(2,1)S(1)} %toeplitz.1.tile_ref, ...), custom_call_target="tpu_custom_call" | custom-call | flops 8388608 | bytes 65536 | tf_op jit(solution)/shard_map/near/pallas_call | solution.py:384
  37.5 5.4 %product.6.rest_0_ = bf16[256,2048]{1,0:T(8,128)(2,1)S(1)} custom-call(s32[2]{0:T(128)S(1)} %broadcast_1_which_ref.2.which_ref, bf16[1,256,1024]{2,1,0:T(8,128)(2,1)S(1)} %get-tuple-element.25.own_ref, bf16[1,256,1024]{2,1,0:T(8,128)(2,1)S(1)} %collective-permute-done.4.other_ref, bf16[1024,4096]{1,0:T(8,128)(2,1)} %own_w_ref.11, ...), custom_call_target="tpu_custom_call" | custom-call | flops 33554432 | bytes 180224 | tf_op jit(solution)/shard_map/product/pallas_call | solution.py:210
  44.2 5.4 %product.7.rest_0_.refs_0_ = bf16[256,2048]{1,0:T(8,128)(2,1)S(1)} custom-call(s32[2]{0:T(128)S(1)} %broadcast_1_which_ref.2.which_ref, bf16[1,256,1024]{2,1,0:T(8,128)(2,1)S(1)} %get-tuple-element.25.own_ref, bf16[1,256,1024]{2,1,0:T(8,128)(2,1)S(1)} %collective-permute-done.4.other_ref, bf16[1024,4096]{1,0:T(8,128)(2,1)} %own_w_ref.11, ...), custom_call_target="tpu_custom_call" | custom-call | flops 33554432 | bytes 180224 | tf_op jit(solution)/shard_map/product/pallas_call | solution.py:210
  49.6 4.6 %near.4 = (bf16[512,1024]{1,0:T(8,128)(2,1)S(1)}, bf16[512,1024]{1,0:T(8,128)(2,1)S(1)}) custom-call(s32[1]{0:T(128)} %bitcast.7.window_ref, bf16[2048,1024]{1,0:T(8,128)(2,1)} %copy-done, bf16[4,128,128]{2,1,0:T(8,128)(2,1)S(1)} %get-tuple-element.21.start_ref, bf16[64,128,128]{2,1,0:T(8,128)(2,1)S(1)} %toeplitz.1.tile_ref, ...), custom_call_target="tpu_custom_call" | custom-call | flops 8388608 | bytes 65536 | tf_op jit(solution)/shard_map/near/pallas_call | solution.py:384
  58.2 9.1 %product.8.rest_0_ = bf16[256,4096]{1,0:T(8,128)(2,1)S(1)} custom-call(s32[2]{0:T(128)S(1)} %broadcast_1_which_ref.2.which_ref, bf16[1,256,1024]{2,1,0:T(8,128)(2,1)S(1)} %get-tuple-element.29.own_ref, bf16[1,256,1024]{2,1,0:T(8,128)(2,1)S(1)} %collective-permute-done.6.other_ref, bf16[1024,4096]{1,0:T(8,128)(2,1)} %own_w_ref.11, ...), custom_call_target="tpu_custom_call" | custom-call | flops 67108864 | bytes 360448 | tf_op jit(solution)/shard_map/product/pallas_call | solution.py:210
  68.6 2.2 %collective-permute-done.7 = bf16[256,2048]{1,0:T(8,128)(2,1)S(1)} collective-permute-done((bf16[256,2048]{1,0:T(8,128)(2,1)S(1)}, bf16[256,2048]{1,0:T(8,128)(2,1)S(1)}, u32[]{:S(2)}, u32[]{:S(2)}) %collective-permute-start.7) | collective-permute-done | bytes 1048608 | tf_op jit(solution)/shard_map/ppermute | solution.py:455
  72.1 2.5 %collective-permute-start.12 = (bf16[256,2048]{1,0:T(8,128)(2,1)}, bf16[256,2048]{1,0:T(8,128)(2,1)}, u32[]{:S(2)}, u32[]{:S(2)}) collective-permute-start(bf16[256,2048]{1,0:T(8,128)(2,1)} %add_convert_fusion.3.rest_1_), channel_id=1, source_target_pairs={{2,4},{3,5},{4,2},{5,3},{10,12},{11,13},{12,10},{13,11},{18,20},{1... | collective-permute-start | bytes 3145736 | tf_op jit(solution)/shard_map/ppermute | solution.py:455
  74.7 12.8 %near.5 = (bf16[2048,1024]{1,0:T(8,128)(2,1)}, bf16[2048,1024]{1,0:T(8,128)(2,1)}) custom-call(s32[1]{0:T(128)} %constant.36.clone.1.window_ref, bf16[2048,1024]{1,0:T(8,128)(2,1)} %copy-done, bf16[4,128,128]{2,1,0:T(8,128)(2,1)S(1)} %get-tuple-element.21.start_ref, bf16[64,128,128]{2,1,0:T(8,128)(2,1)S(1)} %toeplitz.1.tile_ref, ...), custom_call_target="tpu_custom_call" | custom-call | flops 33554432 | bytes 262144 | tf_op jit(solution)/shard_map/near/pallas_call | solution.py:384
  87.5 5.8 %collective-permute-done.8.refs_1_ = bf16[256,2048]{1,0:T(8,128)(2,1)S(1)} collective-permute-done((bf16[256,2048]{1,0:T(8,128)(2,1)S(1)}, bf16[256,2048]{1,0:T(8,128)(2,1)S(1)}, u32[]{:S(2)}, u32[]{:S(2)}) %collective-permute-start.8) | collective-permute-done | bytes 1048608 | tf_op jit(solution)/shard_map/ppermute | solution.py:455
  94.4 2.4 %collective-permute-start.14 = (bf16[256,2048]{1,0:T(8,128)(2,1)S(1)}, bf16[256,2048]{1,0:T(8,128)(2,1)}, u32[]{:S(2)}, u32[]{:S(2)}) collective-permute-start(bf16[256,2048]{1,0:T(8,128)(2,1)S(1)} %sum.2.rest_3_), channel_id=1, source_target_pairs={{2,4},{3,5},{4,2},{5,3},{10,12},{11,13},{12,10},{13,11},{18,20},{1... | collective-permute-start | bytes 3145736 | tf_op jit(solution)/shard_map/ppermute | solution.py:455
  96.9 7.3 %mix.5 = (bf16[4,256,1024]{2,1,0:T(8,128)(2,1)S(1)}, bf16[4,256,1024]{2,1,0:T(8,128)(2,1)S(1)}) custom-call(s32[2]{0:T(128)S(1)} %pad_add_fusion.2.where_ref, bf16[2048,1024]{1,0:T(8,128)(2,1)} %get-tuple-element.31.refs_2_.near_ref, bf16[2048,1024]{1,0:T(8,128)(2,1)} %get-tuple-element.32.query_ref, f32[8,1,128]{2,1,0:T(1,128)S(1)} %bitcast.16, ...), custom_call_target="tpu_custom_call" | custom-call | flops 8388608 | bytes 262144 | tf_op jit(solution)/shard_map/mix/pallas_call | solution.py:429
  106.3 9.1 %product.9.rest_0_ = bf16[256,4096]{1,0:T(8,128)(2,1)S(1)} custom-call(s32[2]{0:T(128)S(1)} %pad_add_fusion.which_ref, bf16[4,256,1024]{2,1,0:T(8,128)(2,1)S(1)} %get-tuple-element.33.own_ref, bf16[1,256,1024]{2,1,0:T(8,128)(2,1)S(1)} %collective-permute-done.11.other_ref, bf16[1024,4096]{1,0:T(8,128)(2,1)} %own_w_ref.11, ...), custom_call_target="tpu_custom_call" | custom-call | flops 67108864 | bytes 360448 | tf_op jit(solution)/shard_map/product/pallas_call | solution.py:210
  116.8 9.1 %product.10.rest_0_ = bf16[256,4096]{1,0:T(8,128)(2,1)S(1)} custom-call(s32[2]{0:T(128)S(1)} %pad_add_fusion.1.which_ref, bf16[4,256,1024]{2,1,0:T(8,128)(2,1)S(1)} %get-tuple-element.33.own_ref, bf16[1,256,1024]{2,1,0:T(8,128)(2,1)S(1)} %collective-permute-done.10.other_ref, bf16[1024,4096]{1,0:T(8,128)(2,1)} %own_w_ref.11, ...), custom_call_target="tpu_custom_call" | custom-call | flops 67108864 | bytes 360448 | tf_op jit(solution)/shard_map/product/pallas_call | solution.py:210
  125.9 3.2 %add_convert_fusion.1 = bf16[256,4096]{1,0:T(8,128)(2,1)S(1)} fusion(bf16[256,4096]{1,0:T(8,128)(2,1)S(1)} %product.10.rest_0_, bf16[256,2048]{1,0:T(8,128)(2,1)} %collective-permute-done.14, bf16[256,2048]{1,0:T(8,128)(2,1)} %collective-permute-done.12.rest_1_), kind=kLoop, calls=%fused_computation.1 | loop fusion | flops 7340032 | bytes 6291456 | tf_op jit(solution)/shard_map/convert_element_type | solution.py:267
  129.2 7.2 %collective-permute-start.15 = (bf16[256,4096]{1,0:T(8,128)(2,1)S(1)}, bf16[256,4096]{1,0:T(8,128)(2,1)}, u32[]{:S(2)}, u32[]{:S(2)}) collective-permute-start(bf16[256,4096]{1,0:T(8,128)(2,1)S(1)} %add_convert_fusion.1), channel_id=1, source_target_pairs={{2,0},{3,1},{4,6},{5,7},{10,8},{11,9},{12,14},{13,15},{18,16},{19,... | collective-permute-start | bytes 6291464 | tf_op jit(solution)/shard_map/ppermute | solution.py:455
  138.3 2.4 %add_convert_fusion.2.rest_1_ = bf16[256,4096]{1,0:T(8,128)(2,1)S(1)} fusion(bf16[256,4096]{1,0:T(8,128)(2,1)} %collective-permute-done.13, bf16[256,4096]{1,0:T(8,128)(2,1)S(1)} %product.8.rest_0_), kind=kLoop, calls=%fused_computation.2 | loop fusion | flops 4194304 | bytes 6291456 | tf_op jit(solution)/shard_map/convert_element_type | solution.py:267
  140.7 2.4 %collective-permute-start.17 = (bf16[256,4096]{1,0:T(8,128)(2,1)S(1)}, bf16[256,4096]{1,0:T(8,128)(2,1)S(1)}, u32[]{:S(2)}, u32[]{:S(2)}) collective-permute-start(bf16[256,4096]{1,0:T(8,128)(2,1)S(1)} %add_convert_fusion.2.rest_1_), channel_id=1, source_target_pairs={{2,4},{3,5},{4,2},{5,3},{10,12},{11,13},{12,10},{13,11},{18,20},{1... | collective-permute-start | bytes 6291464 | tf_op jit(solution)/shard_map/ppermute | solution.py:455
  145.1 9.1 %product.11.refs_0_ = bf16[256,4096]{1,0:T(8,128)(2,1)S(1)} custom-call(s32[2]{0:T(128)S(1)} %pad_add_fusion.3.which_ref, bf16[4,256,1024]{2,1,0:T(8,128)(2,1)S(1)} %get-tuple-element.33.own_ref, bf16[1,256,1024]{2,1,0:T(8,128)(2,1)S(1)} %collective-permute-done.9.other_ref, bf16[1024,4096]{1,0:T(8,128)(2,1)} %own_w_ref.11, ...), custom_call_target="tpu_custom_call" | custom-call | flops 67108864 | bytes 360448 | tf_op jit(solution)/shard_map/product/pallas_call | solution.py:210
  154.2 28.2 %collective-permute-done.16.refs_2_ = bf16[256,4096]{1,0:T(8,128)(2,1)} collective-permute-done((bf16[256,4096]{1,0:T(8,128)(2,1)S(1)}, bf16[256,4096]{1,0:T(8,128)(2,1)}, u32[]{:S(2)}, u32[]{:S(2)}) %collective-permute-start.16) | collective-permute-done | bytes 2097184 | tf_op jit(solution)/shard_map/ppermute | solution.py:455
  182.5 5.0 %sum.3 = bf16[256,4096]{1,0:T(8,128)(2,1)S(1)} custom-call(bf16[256,4096]{1,0:T(8,128)(2,1)S(1)} %product.11.refs_0_, bf16[256,4096]{1,0:T(8,128)(2,1)} %collective-permute-done.15.refs_1_, bf16[256,4096]{1,0:T(8,128)(2,1)} %collective-permute-done.16.refs_2_), custom_call_target="tpu_custom_call" | custom-call | flops 49152 | bytes 98304 | tf_op jit(solution)/shard_map/sum/pallas_call | solution.py:246
  (63 shorter events, 32.4 us)
Async XLA Ops:
  0.0 37.5 %collective-permute-start.5 = (bf16[1024,4096]{1,0:T(8,128)(2,1)}, bf16[1024,4096]{1,0:T(8,128)(2,1)}, u32[]{:S(2)}, u32[]{:S(2)}) collective-permute-start(bf16[1024,4096]{1,0:T(8,128)(2,1)} %own_w_ref.11), channel_id=1, source_target_pairs={{0,1},{1,0},{2,3},{3,2},{4,5},{5,4},{6,7},{7,6},{8,9},{9,8},{10,11... | collective-permute-start | bytes 25165832 | tf_op jit(solution)/shard_map/ppermute | solution.py:315
  0.8 5.0 %collective-permute-start = (bf16[2,3,1024]{2,0,1:T(2,128)(2,1)S(1)}, bf16[2,3,1024]{2,0,1:T(2,128)(2,1)S(1)}, u32[]{:S(2)}, u32[]{:S(2)}) collective-permute-start(bf16[2,3,1024]{2,0,1:T(2,128)(2,1)S(1)} %slice.3), channel_id=1, source_target_pairs={{0,8},{8,16},{16,24},{1,9},{9,17},{17,25},{2,10},{10,18},{18,26},{... | collective-permute-start | bytes 36872 | tf_op jit(solution)/shard_map/ppermute | solution.py:260
  16.2 2.0 %copy-start = (bf16[2048,1024]{1,0:T(8,128)(2,1)}, bf16[2048,1024]{1,0:T(8,128)(2,1)S(1)}, u32[]{:S(2)}) copy-start(bf16[2048,1024]{1,0:T(8,128)(2,1)S(1)} %get-tuple-element.20.gated_ref) | copy-start | bytes 12582916
  18.1 10.8 %copy-start.4 = (f32[3,3,1024]{2,1,0:T(4,128)S(1)}, f32[3,3,1024]{2,1,0:T(4,128)}, u32[]{:S(2)}) copy-start(f32[3,3,1024]{2,1,0:T(4,128)} %taps_ref.7) | copy-start | bytes 110596
  18.1 10.8 %copy-start.5 = (f32[1024]{0:T(1024)S(1)}, f32[1024]{0:T(1024)}, u32[]{:S(2)}) copy-start(f32[1024]{0:T(1024)} %param.10) | copy-start | bytes 12292
  18.1 15.4 %collective-permute-start.1 = (bf16[128,128]{1,0:T(8,128)(2,1)S(1)}, bf16[128,128]{1,0:T(8,128)(2,1)S(1)}, u32[]{:S(2)}, u32[]{:S(2)}) collective-permute-start(bf16[128,128]{1,0:T(8,128)(2,1)S(1)} %get-tuple-element.24), channel_id=1, source_target_pairs={{0,8},{8,16},{16,24},{1,9},{9,17},{17,25},{2,10},{10,18},{18,26},{... | collective-permute-start | bytes 98312 | tf_op jit(solution)/shard_map/ppermute | solution.py:260
  22.2 11.3 %collective-permute-start.2 = (bf16[128,128]{1,0:T(8,128)(2,1)S(1)}, bf16[128,128]{1,0:T(8,128)(2,1)S(1)}, u32[]{:S(2)}, u32[]{:S(2)}) collective-permute-start(bf16[128,128]{1,0:T(8,128)(2,1)S(1)} %get-tuple-element.24), channel_id=1, source_target_pairs={{0,16},{8,24},{1,17},{9,25},{2,18},{10,26},{3,19},{11,27},{4,20},{... | collective-permute-start | bytes 98312 | tf_op jit(solution)/shard_map/ppermute | solution.py:260
  25.7 7.9 %collective-permute-start.3 = (bf16[128,128]{1,0:T(8,128)(2,1)S(1)}, bf16[128,128]{1,0:T(8,128)(2,1)S(1)}, u32[]{:S(2)}, u32[]{:S(2)}) collective-permute-start(bf16[128,128]{1,0:T(8,128)(2,1)S(1)} %get-tuple-element.24), channel_id=1, source_target_pairs={{0,24},{1,25},{2,26},{3,27},{4,28},{5,29},{6,30},{7,31}} | collective-permute-start | bytes 98312 | tf_op jit(solution)/shard_map/ppermute | solution.py:260
  35.5 2.0 %collective-permute-start.4 = (bf16[1,256,1024]{2,1,0:T(8,128)(2,1)S(1)}, bf16[1,256,1024]{2,1,0:T(8,128)(2,1)S(1)}, u32[]{:S(2)}, u32[]{:S(2)}) collective-permute-start(bf16[1,256,1024]{2,1,0:T(8,128)(2,1)S(1)} %get-tuple-element.26), channel_id=1, source_target_pairs={{0,1},{1,0},{2,3},{3,2},{4,5},{5,4},{6,7},{7,6},{8,9},{9,8},{10,11... | collective-permute-start | bytes 1572872 | tf_op jit(solution)/shard_map/ppermute | solution.py:455
  42.9 27.9 %collective-permute-start.7 = (bf16[256,2048]{1,0:T(8,128)(2,1)S(1)}, bf16[256,2048]{1,0:T(8,128)(2,1)S(1)}, u32[]{:S(2)}, u32[]{:S(2)}) collective-permute-start(bf16[256,2048]{1,0:T(8,128)(2,1)S(1)} %product.6.rest_0_), channel_id=1, source_target_pairs={{0,2},{1,3},{6,4},{7,5},{8,10},{9,11},{14,12},{15,13},{16,18},{17,... | collective-permute-start | bytes 3145736 | tf_op jit(solution)/shard_map/ppermute | solution.py:455
  56.2 2.0 %collective-permute-start.6 = (bf16[1,256,1024]{2,1,0:T(8,128)(2,1)S(1)}, bf16[1,256,1024]{2,1,0:T(8,128)(2,1)S(1)}, u32[]{:S(2)}, u32[]{:S(2)}) collective-permute-start(bf16[1,256,1024]{2,1,0:T(8,128)(2,1)S(1)} %get-tuple-element.30), channel_id=1, source_target_pairs={{0,1},{1,0},{2,3},{3,2},{4,5},{5,4},{6,7},{7,6},{8,9},{9,8},{10,11... | collective-permute-start | bytes 1572872 | tf_op jit(solution)/shard_map/ppermute | solution.py:455
  56.4 36.8 %collective-permute-start.8 = (bf16[256,2048]{1,0:T(8,128)(2,1)S(1)}, bf16[256,2048]{1,0:T(8,128)(2,1)S(1)}, u32[]{:S(2)}, u32[]{:S(2)}) collective-permute-start(bf16[256,2048]{1,0:T(8,128)(2,1)S(1)} %product.7.rest_0_.refs_0_), channel_id=1, source_target_pairs={{0,2},{1,3},{6,4},{7,5},{8,10},{9,11},{14,12},{15,13},{16,18},{17,... | collective-permute-start | bytes 3145736 | tf_op jit(solution)/shard_map/ppermute | solution.py:455
  67.3 71.1 %collective-permute-start.13 = (bf16[256,4096]{1,0:T(8,128)(2,1)S(1)}, bf16[256,4096]{1,0:T(8,128)(2,1)}, u32[]{:S(2)}, u32[]{:S(2)}) collective-permute-start(bf16[256,4096]{1,0:T(8,128)(2,1)S(1)} %product.8.rest_0_), channel_id=1, source_target_pairs={{0,2},{1,3},{6,4},{7,5},{8,10},{9,11},{14,12},{15,13},{16,18},{17,... | collective-permute-start | bytes 6291464 | tf_op jit(solution)/shard_map/ppermute | solution.py:455
  72.1 44.6 %collective-permute-start.12 = (bf16[256,2048]{1,0:T(8,128)(2,1)}, bf16[256,2048]{1,0:T(8,128)(2,1)}, u32[]{:S(2)}, u32[]{:S(2)}) collective-permute-start(bf16[256,2048]{1,0:T(8,128)(2,1)} %add_convert_fusion.3.rest_1_), channel_id=1, source_target_pairs={{2,4},{3,5},{4,2},{5,3},{10,12},{11,13},{12,10},{13,11},{18,20},{1... | collective-permute-start | bytes 3145736 | tf_op jit(solution)/shard_map/ppermute | solution.py:455
  94.4 31.5 %collective-permute-start.14 = (bf16[256,2048]{1,0:T(8,128)(2,1)S(1)}, bf16[256,2048]{1,0:T(8,128)(2,1)}, u32[]{:S(2)}, u32[]{:S(2)}) collective-permute-start(bf16[256,2048]{1,0:T(8,128)(2,1)S(1)} %sum.2.rest_3_), channel_id=1, source_target_pairs={{2,4},{3,5},{4,2},{5,3},{10,12},{11,13},{12,10},{13,11},{18,20},{1... | collective-permute-start | bytes 3145736 | tf_op jit(solution)/shard_map/ppermute | solution.py:455
  104.4 2.0 %collective-permute-start.11 = (bf16[1,256,1024]{2,1,0:T(8,128)(2,1)S(1)}, bf16[1,256,1024]{2,1,0:T(8,128)(2,1)S(1)}, u32[]{:S(2)}, u32[]{:S(2)}) collective-permute-start(bf16[1,256,1024]{2,1,0:T(8,128)(2,1)S(1)} %get-tuple-element.35), channel_id=1, source_target_pairs={{0,1},{1,0},{2,3},{3,2},{4,5},{5,4},{6,7},{7,6},{8,9},{9,8},{10,11... | collective-permute-start | bytes 1572872 | tf_op jit(solution)/shard_map/ppermute | solution.py:455
  104.4 12.3 %collective-permute-start.10 = (bf16[1,256,1024]{2,1,0:T(8,128)(2,1)S(1)}, bf16[1,256,1024]{2,1,0:T(8,128)(2,1)S(1)}, u32[]{:S(2)}, u32[]{:S(2)}) collective-permute-start(bf16[1,256,1024]{2,1,0:T(8,128)(2,1)S(1)} %get-tuple-element.36), channel_id=1, source_target_pairs={{0,1},{1,0},{2,3},{3,2},{4,5},{5,4},{6,7},{7,6},{8,9},{9,8},{10,11... | collective-permute-start | bytes 1572872 | tf_op jit(solution)/shard_map/ppermute | solution.py:455
  115.4 1.3 copy-start.2
  115.4 67.0 %collective-permute-start.16 = (bf16[256,4096]{1,0:T(8,128)(2,1)S(1)}, bf16[256,4096]{1,0:T(8,128)(2,1)}, u32[]{:S(2)}, u32[]{:S(2)}) collective-permute-start(bf16[256,4096]{1,0:T(8,128)(2,1)S(1)} %product.9.rest_0_), channel_id=1, source_target_pairs={{0,2},{1,3},{6,4},{7,5},{8,10},{9,11},{14,12},{15,13},{16,18},{17,... | collective-permute-start | bytes 6291464 | tf_op jit(solution)/shard_map/ppermute | solution.py:455
  125.9 3.3 %copy-start.1 = (bf16[256,4096]{1,0:T(8,128)(2,1)}, bf16[256,4096]{1,0:T(8,128)(2,1)S(1)}, u32[]{:S(2)}) copy-start(bf16[256,4096]{1,0:T(8,128)(2,1)S(1)} %product.10.rest_0_) | copy-start | bytes 6291460
  129.2 53.3 %collective-permute-start.15 = (bf16[256,4096]{1,0:T(8,128)(2,1)S(1)}, bf16[256,4096]{1,0:T(8,128)(2,1)}, u32[]{:S(2)}, u32[]{:S(2)}) collective-permute-start(bf16[256,4096]{1,0:T(8,128)(2,1)S(1)} %add_convert_fusion.1), channel_id=1, source_target_pairs={{2,0},{3,1},{4,6},{5,7},{10,8},{11,9},{12,14},{13,15},{18,16},{19,... | collective-permute-start | bytes 6291464 | tf_op jit(solution)/shard_map/ppermute | solution.py:455
  140.7 4.4 %copy-start.6 = (bf16[256,4096]{1,0:T(8,128)(2,1)}, bf16[256,4096]{1,0:T(8,128)(2,1)S(1)}, u32[]{:S(2)}) copy-start(bf16[256,4096]{1,0:T(8,128)(2,1)S(1)} %add_convert_fusion.2.rest_1_) | copy-start | bytes 6291460
  140.7 47.9 %collective-permute-start.17 = (bf16[256,4096]{1,0:T(8,128)(2,1)S(1)}, bf16[256,4096]{1,0:T(8,128)(2,1)S(1)}, u32[]{:S(2)}, u32[]{:S(2)}) collective-permute-start(bf16[256,4096]{1,0:T(8,128)(2,1)S(1)} %add_convert_fusion.2.rest_1_), channel_id=1, source_target_pairs={{2,4},{3,5},{4,2},{5,3},{10,12},{11,13},{12,10},{13,11},{18,20},{1... | collective-permute-start | bytes 6291464 | tf_op jit(solution)/shard_map/ppermute | solution.py:455
  143.1 2.0 %collective-permute-start.9 = (bf16[1,256,1024]{2,1,0:T(8,128)(2,1)S(1)}, bf16[1,256,1024]{2,1,0:T(8,128)(2,1)S(1)}, u32[]{:S(2)}, u32[]{:S(2)}) collective-permute-start(bf16[1,256,1024]{2,1,0:T(8,128)(2,1)S(1)} %get-tuple-element.37), channel_id=1, source_target_pairs={{0,1},{1,0},{2,3},{3,2},{4,5},{5,4},{6,7},{7,6},{8,9},{9,8},{10,11... | collective-permute-start | bytes 1572872 | tf_op jit(solution)/shard_map/ppermute | solution.py:455
  (1 other events, 0.8 us)

commit v6 on v5

--- a/solution.py
+++ b/solution.py
@@ -27,8 +27,8 @@
 
 
 def toeplitz_kernel(modes, rate_ref, scale_ref, tile_ref):
-    filters = LANES // modes
-    reach = iota((LANES, CHUNK), 1).astype(F32)
+    filters = rate_ref.shape[0] // modes
+    reach = iota(rate_ref.shape, 1).astype(F32)
     terms = scale_ref[...] * jnp.exp(-rate_ref[...] * reach)
     taps = terms.reshape(filters, modes, CHUNK).sum(axis=1)
     keep = iota((CHUNK, CHUNK), 0) <= iota((CHUNK, CHUNK), 1)
@@ -321,8 +321,8 @@
     scale_rows = scaled.reshape(blocks, 1, LANES)
     per_block = LANES // group
 
-    square = pl.BlockSpec((LANES, LANES), lambda g: (g, 0))
-    tile_spec = pl.BlockSpec((per_block, CHUNK, CHUNK), lambda g: (g, 0, 0))
+    square = pl.BlockSpec((PARTS * LANES, LANES), lambda g: (g, 0))
+    tile_spec = pl.BlockSpec((PARTS * per_block, CHUNK, CHUNK), lambda g: (g, 0, 0))
     wide_lanes = PARTS * LANES
     lanes_spec = pl.BlockSpec((tok_rows, wide_lanes), lambda g: (0, g))
     rim_spec = pl.BlockSpec((streams, 2, wide_lanes), lambda g: (0, 0, g))
@@ -333,7 +333,7 @@
 
     tiles = pl.pallas_call(
         functools.partial(toeplitz_kernel, modes),
-        grid=(blocks,),
+        grid=(blocks // PARTS,),
         in_specs=[square, square],
         out_specs=tile_spec,
         out_shape=jax.ShapeDtypeStruct((filters, CHUNK, CHUNK), BF16),

time: 193 us -> 192 us (level)
  no operation moved by 1% of the time
where the time goes in v6:
time: 192 us; the launch traced here: 190 us
  Pallas kernels  96.7 us (50%)
  waiting for transfers between devices  44.8 us (23%)
  starting transfers between devices  32.8 us (17%)
  other arithmetic  10.2 us (5%)
  local copies, waits for them, and re-layouts  5.27 us (3%)
    pallas_call x6, Pallas kernels, product(): pl.pallas_call(product_kernel, grid_spec=pltpu.PrefetchScalarGridSpec(num...  47.2 us
    ppermute x13, waiting for transfers between devices, on_device(): send = lambda value, hops: lax.ppermute(value, 'chan', hops)  44.8 us
    pallas_call x3, Pallas kernels, convolve(): pl.pallas_call(functools.partial(near_kernel, modes, group), grid_spec=pl...  22 us
    ppermute x13, starting transfers between devices, on_device(): send = lambda value, hops: lax.ppermute(value, 'chan', hops)  20.6 us
    ppermute x4, starting transfers between devices, shifted(): lax.ppermute(value, axis, [(i, i + steps) for i in range(count - steps)])  12.2 us
    pallas_call x3, Pallas kernels, finish(): pl.pallas_call(functools.partial(mix_kernel, modes, group, tok_rows, size...  11.4 us
    pallas_call x1, Pallas kernels, on_device(): pl.pallas_call(functools.partial(gate_kernel, modes, group), grid=(blocks...  9.31 us
    convert_element_type x4, other arithmetic, add(): return total.astype(BF16)  9.07 us
  transfers between devices with their start and end apart: 18, of which 9 were waited for; matrix products, arithmetic and copies ran while one was open for 6% of the time, Pallas kernels for 48%

profile of v6, /device:TPU:16, one launch (start us, length us, event | category | flops | bytes accessed | tf_op | source)
XLA Modules:
  0.0 190.2 jit_solution(6856763342152282691)
XLA Ops:
  0.8 3.4 %collective-permute-start = (bf16[2,3,1024]{2,0,1:T(2,128)(2,1)S(1)}, bf16[2,3,1024]{2,0,1:T(2,128)(2,1)S(1)}, u32[]{:S(2)}, u32[]{:S(2)}) collective-permute-start(bf16[2,3,1024]{2,0,1:T(2,128)(2,1)S(1)} %slice.3), channel_id=1, source_target_pairs={{0,8},{8,16},{16,24},{1,9},{9,17},{17,25},{2,10},{10,18},{18,26},{... | collective-permute-start | bytes 36872 | tf_op jit(solution)/shard_map/ppermute | solution.py:260
  6.8 9.3 %gate.1 = (bf16[2048,1024]{1,0:T(8,128)(2,1)S(1)}, bf16[4,128,128]{2,1,0:T(8,128)(2,1)S(1)}, bf16[128,128]{1,0:T(8,128)(2,1)S(1)}) custom-call(bf16[3,2048,1024]{2,1,0:T(8,128)(2,1)} %bitcast.30, bf16[3,2048,1024]{2,1,0:T(8,128)(2,1)} %bitcast.31, bf16[3,2,1024]{2,1,0:T(2,128)(2,1)S(1)} %bitcast.23, f32[3,3,1024]{2,1,0:T(4,128)S(1)} %copy-done.3, ...), custom_call_target="tpu_custom_call" | custom-call | flops 8388608 | bytes 196608 | tf_op jit(solution)/shard_map/gate/pallas_call | solution.py:347
  18.1 4.1 %collective-permute-start.1 = (bf16[128,128]{1,0:T(8,128)(2,1)S(1)}, bf16[128,128]{1,0:T(8,128)(2,1)S(1)}, u32[]{:S(2)}, u32[]{:S(2)}) collective-permute-start(bf16[128,128]{1,0:T(8,128)(2,1)S(1)} %get-tuple-element.24), channel_id=1, source_target_pairs={{0,8},{8,16},{16,24},{1,9},{9,17},{17,25},{2,10},{10,18},{18,26},{... | collective-permute-start | bytes 98312 | tf_op jit(solution)/shard_map/ppermute | solution.py:260
  22.2 3.4 %collective-permute-start.2 = (bf16[128,128]{1,0:T(8,128)(2,1)S(1)}, bf16[128,128]{1,0:T(8,128)(2,1)S(1)}, u32[]{:S(2)}, u32[]{:S(2)}) collective-permute-start(bf16[128,128]{1,0:T(8,128)(2,1)S(1)} %get-tuple-element.24), channel_id=1, source_target_pairs={{0,16},{8,24},{1,17},{9,25},{2,18},{10,26},{3,19},{11,27},{4,20},{... | collective-permute-start | bytes 98312 | tf_op jit(solution)/shard_map/ppermute | solution.py:260
  28.3 4.6 %near.3 = (bf16[512,1024]{1,0:T(8,128)(2,1)S(1)}, bf16[512,1024]{1,0:T(8,128)(2,1)S(1)}) custom-call(s32[1]{0:T(128)} %bitcast.8.window_ref, bf16[2048,1024]{1,0:T(8,128)(2,1)} %copy-done, bf16[4,128,128]{2,1,0:T(8,128)(2,1)S(1)} %get-tuple-element.21.start_ref, bf16[64,128,128]{2,1,0:T(8,128)(2,1)S(1)} %toeplitz.1.tile_ref, ...), custom_call_target="tpu_custom_call" | custom-call | flops 8388608 | bytes 65536 | tf_op jit(solution)/shard_map/near/pallas_call | solution.py:384
  36.9 5.4 %product.6.rest_0_ = bf16[256,2048]{1,0:T(8,128)(2,1)S(1)} custom-call(s32[2]{0:T(128)S(1)} %broadcast_1_which_ref.2.which_ref, bf16[1,256,1024]{2,1,0:T(8,128)(2,1)S(1)} %get-tuple-element.25.own_ref, bf16[1,256,1024]{2,1,0:T(8,128)(2,1)S(1)} %collective-permute-done.4.other_ref, bf16[1024,4096]{1,0:T(8,128)(2,1)} %own_w_ref.11, ...), custom_call_target="tpu_custom_call" | custom-call | flops 33554432 | bytes 180224 | tf_op jit(solution)/shard_map/product/pallas_call | solution.py:210
  43.6 5.4 %product.7.rest_0_.refs_0_ = bf16[256,2048]{1,0:T(8,128)(2,1)S(1)} custom-call(s32[2]{0:T(128)S(1)} %broadcast_1_which_ref.2.which_ref, bf16[1,256,1024]{2,1,0:T(8,128)(2,1)S(1)} %get-tuple-element.25.own_ref, bf16[1,256,1024]{2,1,0:T(8,128)(2,1)S(1)} %collective-permute-done.4.other_ref, bf16[1024,4096]{1,0:T(8,128)(2,1)} %own_w_ref.11, ...), custom_call_target="tpu_custom_call" | custom-call | flops 33554432 | bytes 180224 | tf_op jit(solution)/shard_map/product/pallas_call | solution.py:210
  49.0 4.6 %near.4 = (bf16[512,1024]{1,0:T(8,128)(2,1)S(1)}, bf16[512,1024]{1,0:T(8,128)(2,1)S(1)}) custom-call(s32[1]{0:T(128)} %bitcast.7.window_ref, bf16[2048,1024]{1,0:T(8,128)(2,1)} %copy-done, bf16[4,128,128]{2,1,0:T(8,128)(2,1)S(1)} %get-tuple-element.21.start_ref, bf16[64,128,128]{2,1,0:T(8,128)(2,1)S(1)} %toeplitz.1.tile_ref, ...), custom_call_target="tpu_custom_call" | custom-call | flops 8388608 | bytes 65536 | tf_op jit(solution)/shard_map/near/pallas_call | solution.py:384
  57.6 9.1 %product.8.rest_0_ = bf16[256,4096]{1,0:T(8,128)(2,1)S(1)} custom-call(s32[2]{0:T(128)S(1)} %broadcast_1_which_ref.2.which_ref, bf16[1,256,1024]{2,1,0:T(8,128)(2,1)S(1)} %get-tuple-element.29.own_ref, bf16[1,256,1024]{2,1,0:T(8,128)(2,1)S(1)} %collective-permute-done.6.other_ref, bf16[1024,4096]{1,0:T(8,128)(2,1)} %own_w_ref.11, ...), custom_call_target="tpu_custom_call" | custom-call | flops 67108864 | bytes 360448 | tf_op jit(solution)/shard_map/product/pallas_call | solution.py:210
  71.6 2.3 %collective-permute-start.12 = (bf16[256,2048]{1,0:T(8,128)(2,1)}, bf16[256,2048]{1,0:T(8,128)(2,1)}, u32[]{:S(2)}, u32[]{:S(2)}) collective-permute-start(bf16[256,2048]{1,0:T(8,128)(2,1)} %add_convert_fusion.3.rest_1_), channel_id=1, source_target_pairs={{2,4},{3,5},{4,2},{5,3},{10,12},{11,13},{12,10},{13,11},{18,20},{1... | collective-permute-start | bytes 3145736 | tf_op jit(solution)/shard_map/ppermute | solution.py:455
  73.9 12.8 %near.5 = (bf16[2048,1024]{1,0:T(8,128)(2,1)}, bf16[2048,1024]{1,0:T(8,128)(2,1)}) custom-call(s32[1]{0:T(128)} %constant.36.clone.1.window_ref, bf16[2048,1024]{1,0:T(8,128)(2,1)} %copy-done, bf16[4,128,128]{2,1,0:T(8,128)(2,1)S(1)} %get-tuple-element.21.start_ref, bf16[64,128,128]{2,1,0:T(8,128)(2,1)S(1)} %toeplitz.1.tile_ref, ...), custom_call_target="tpu_custom_call" | custom-call | flops 33554432 | bytes 262144 | tf_op jit(solution)/shard_map/near/pallas_call | solution.py:384
  86.8 5.9 %collective-permute-done.8.refs_1_ = bf16[256,2048]{1,0:T(8,128)(2,1)S(1)} collective-permute-done((bf16[256,2048]{1,0:T(8,128)(2,1)S(1)}, bf16[256,2048]{1,0:T(8,128)(2,1)S(1)}, u32[]{:S(2)}, u32[]{:S(2)}) %collective-permute-start.8) | collective-permute-done | bytes 1048608 | tf_op jit(solution)/shard_map/ppermute | solution.py:455
  93.9 2.4 %collective-permute-start.14 = (bf16[256,2048]{1,0:T(8,128)(2,1)S(1)}, bf16[256,2048]{1,0:T(8,128)(2,1)}, u32[]{:S(2)}, u32[]{:S(2)}) collective-permute-start(bf16[256,2048]{1,0:T(8,128)(2,1)S(1)} %sum.2.rest_3_), channel_id=1, source_target_pairs={{2,4},{3,5},{4,2},{5,3},{10,12},{11,13},{12,10},{13,11},{18,20},{1... | collective-permute-start | bytes 3145736 | tf_op jit(solution)/shard_map/ppermute | solution.py:455
  96.3 7.3 %mix.5 = (bf16[4,256,1024]{2,1,0:T(8,128)(2,1)S(1)}, bf16[4,256,1024]{2,1,0:T(8,128)(2,1)S(1)}) custom-call(s32[2]{0:T(128)S(1)} %pad_add_fusion.2.where_ref, bf16[2048,1024]{1,0:T(8,128)(2,1)} %get-tuple-element.31.refs_2_.near_ref, bf16[2048,1024]{1,0:T(8,128)(2,1)} %get-tuple-element.32.query_ref, f32[8,1,128]{2,1,0:T(1,128)S(1)} %bitcast.16, ...), custom_call_target="tpu_custom_call" | custom-call | flops 8388608 | bytes 262144 | tf_op jit(solution)/shard_map/mix/pallas_call | solution.py:429
  105.8 9.1 %product.9.rest_0_ = bf16[256,4096]{1,0:T(8,128)(2,1)S(1)} custom-call(s32[2]{0:T(128)S(1)} %pad_add_fusion.which_ref, bf16[4,256,1024]{2,1,0:T(8,128)(2,1)S(1)} %get-tuple-element.33.own_ref, bf16[1,256,1024]{2,1,0:T(8,128)(2,1)S(1)} %collective-permute-done.11.other_ref, bf16[1024,4096]{1,0:T(8,128)(2,1)} %own_w_ref.11, ...), custom_call_target="tpu_custom_call" | custom-call | flops 67108864 | bytes 360448 | tf_op jit(solution)/shard_map/product/pallas_call | solution.py:210
  116.2 9.1 %product.10.rest_0_ = bf16[256,4096]{1,0:T(8,128)(2,1)S(1)} custom-call(s32[2]{0:T(128)S(1)} %pad_add_fusion.1.which_ref, bf16[4,256,1024]{2,1,0:T(8,128)(2,1)S(1)} %get-tuple-element.33.own_ref, bf16[1,256,1024]{2,1,0:T(8,128)(2,1)S(1)} %collective-permute-done.10.other_ref, bf16[1024,4096]{1,0:T(8,128)(2,1)} %own_w_ref.11, ...), custom_call_target="tpu_custom_call" | custom-call | flops 67108864 | bytes 360448 | tf_op jit(solution)/shard_map/product/pallas_call | solution.py:210
  125.3 3.2 %add_convert_fusion.1 = bf16[256,4096]{1,0:T(8,128)(2,1)S(1)} fusion(bf16[256,4096]{1,0:T(8,128)(2,1)S(1)} %product.10.rest_0_, bf16[256,2048]{1,0:T(8,128)(2,1)} %collective-permute-done.14, bf16[256,2048]{1,0:T(8,128)(2,1)} %collective-permute-done.12.rest_1_), kind=kLoop, calls=%fused_computation.1 | loop fusion | flops 7340032 | bytes 6291456 | tf_op jit(solution)/shard_map/convert_element_type | solution.py:267
  128.6 7.2 %collective-permute-start.15 = (bf16[256,4096]{1,0:T(8,128)(2,1)S(1)}, bf16[256,4096]{1,0:T(8,128)(2,1)}, u32[]{:S(2)}, u32[]{:S(2)}) collective-permute-start(bf16[256,4096]{1,0:T(8,128)(2,1)S(1)} %add_convert_fusion.1), channel_id=1, source_target_pairs={{2,0},{3,1},{4,6},{5,7},{10,8},{11,9},{12,14},{13,15},{18,16},{19,... | collective-permute-start | bytes 6291464 | tf_op jit(solution)/shard_map/ppermute | solution.py:455
  137.7 2.4 %add_convert_fusion.2.rest_1_ = bf16[256,4096]{1,0:T(8,128)(2,1)S(1)} fusion(bf16[256,4096]{1,0:T(8,128)(2,1)} %collective-permute-done.13, bf16[256,4096]{1,0:T(8,128)(2,1)S(1)} %product.8.rest_0_), kind=kLoop, calls=%fused_computation.2 | loop fusion | flops 4194304 | bytes 6291456 | tf_op jit(solution)/shard_map/convert_element_type | solution.py:267
  140.2 2.4 %collective-permute-start.17 = (bf16[256,4096]{1,0:T(8,128)(2,1)S(1)}, bf16[256,4096]{1,0:T(8,128)(2,1)S(1)}, u32[]{:S(2)}, u32[]{:S(2)}) collective-permute-start(bf16[256,4096]{1,0:T(8,128)(2,1)S(1)} %add_convert_fusion.2.rest_1_), channel_id=1, source_target_pairs={{2,4},{3,5},{4,2},{5,3},{10,12},{11,13},{12,10},{13,11},{18,20},{1... | collective-permute-start | bytes 6291464 | tf_op jit(solution)/shard_map/ppermute | solution.py:455
  144.5 9.1 %product.11.refs_0_ = bf16[256,4096]{1,0:T(8,128)(2,1)S(1)} custom-call(s32[2]{0:T(128)S(1)} %pad_add_fusion.3.which_ref, bf16[4,256,1024]{2,1,0:T(8,128)(2,1)S(1)} %get-tuple-element.33.own_ref, bf16[1,256,1024]{2,1,0:T(8,128)(2,1)S(1)} %collective-permute-done.9.other_ref, bf16[1024,4096]{1,0:T(8,128)(2,1)} %own_w_ref.11, ...), custom_call_target="tpu_custom_call" | custom-call | flops 67108864 | bytes 360448 | tf_op jit(solution)/shard_map/product/pallas_call | solution.py:210
  153.6 28.2 %collective-permute-done.16.refs_2_ = bf16[256,4096]{1,0:T(8,128)(2,1)} collective-permute-done((bf16[256,4096]{1,0:T(8,128)(2,1)S(1)}, bf16[256,4096]{1,0:T(8,128)(2,1)}, u32[]{:S(2)}, u32[]{:S(2)}) %collective-permute-start.16) | collective-permute-done | bytes 2097184 | tf_op jit(solution)/shard_map/ppermute | solution.py:455
  181.9 5.0 %sum.3 = bf16[256,4096]{1,0:T(8,128)(2,1)S(1)} custom-call(bf16[256,4096]{1,0:T(8,128)(2,1)S(1)} %product.11.refs_0_, bf16[256,4096]{1,0:T(8,128)(2,1)} %collective-permute-done.15.refs_1_, bf16[256,4096]{1,0:T(8,128)(2,1)} %collective-permute-done.16.refs_2_), custom_call_target="tpu_custom_call" | custom-call | flops 49152 | bytes 98304 | tf_op jit(solution)/shard_map/sum/pallas_call | solution.py:246
  188.1 2.1 %add_convert_fusion = bf16[256,4096]{1,0:T(8,128)(2,1)} fusion(bf16[256,4096]{1,0:T(8,128)(2,1)S(1)} %collective-permute-done.17, bf16[256,4096]{1,0:T(8,128)(2,1)S(1)} %sum.3), kind=kLoop, calls=%fused_computation | loop fusion | flops 4194304 | bytes 6291456 | tf_op jit(solution)/shard_map/convert_element_type | solution.py:267
  (63 shorter events, 31.9 us)
Async XLA Ops:
  0.0 36.9 %collective-permute-start.5 = (bf16[1024,4096]{1,0:T(8,128)(2,1)}, bf16[1024,4096]{1,0:T(8,128)(2,1)}, u32[]{:S(2)}, u32[]{:S(2)}) collective-permute-start(bf16[1024,4096]{1,0:T(8,128)(2,1)} %own_w_ref.11), channel_id=1, source_target_pairs={{0,1},{1,0},{2,3},{3,2},{4,5},{5,4},{6,7},{7,6},{8,9},{9,8},{10,11... | collective-permute-start | bytes 25165832 | tf_op jit(solution)/shard_map/ppermute | solution.py:315
  0.8 5.0 %collective-permute-start = (bf16[2,3,1024]{2,0,1:T(2,128)(2,1)S(1)}, bf16[2,3,1024]{2,0,1:T(2,128)(2,1)S(1)}, u32[]{:S(2)}, u32[]{:S(2)}) collective-permute-start(bf16[2,3,1024]{2,0,1:T(2,128)(2,1)S(1)} %slice.3), channel_id=1, source_target_pairs={{0,8},{8,16},{16,24},{1,9},{9,17},{17,25},{2,10},{10,18},{18,26},{... | collective-permute-start | bytes 36872 | tf_op jit(solution)/shard_map/ppermute | solution.py:260
  16.2 2.0 %copy-start = (bf16[2048,1024]{1,0:T(8,128)(2,1)}, bf16[2048,1024]{1,0:T(8,128)(2,1)S(1)}, u32[]{:S(2)}) copy-start(bf16[2048,1024]{1,0:T(8,128)(2,1)S(1)} %get-tuple-element.20.gated_ref) | copy-start | bytes 12582916
  18.1 10.2 %copy-start.4 = (f32[3,3,1024]{2,1,0:T(4,128)S(1)}, f32[3,3,1024]{2,1,0:T(4,128)}, u32[]{:S(2)}) copy-start(f32[3,3,1024]{2,1,0:T(4,128)} %taps_ref.7) | copy-start | bytes 110596
  18.1 10.2 %copy-start.5 = (f32[1024]{0:T(1024)S(1)}, f32[1024]{0:T(1024)}, u32[]{:S(2)}) copy-start(f32[1024]{0:T(1024)} %param.10) | copy-start | bytes 12292
  18.1 14.8 %collective-permute-start.1 = (bf16[128,128]{1,0:T(8,128)(2,1)S(1)}, bf16[128,128]{1,0:T(8,128)(2,1)S(1)}, u32[]{:S(2)}, u32[]{:S(2)}) collective-permute-start(bf16[128,128]{1,0:T(8,128)(2,1)S(1)} %get-tuple-element.24), channel_id=1, source_target_pairs={{0,8},{8,16},{16,24},{1,9},{9,17},{17,25},{2,10},{10,18},{18,26},{... | collective-permute-start | bytes 98312 | tf_op jit(solution)/shard_map/ppermute | solution.py:260
  22.2 10.7 %collective-permute-start.2 = (bf16[128,128]{1,0:T(8,128)(2,1)S(1)}, bf16[128,128]{1,0:T(8,128)(2,1)S(1)}, u32[]{:S(2)}, u32[]{:S(2)}) collective-permute-start(bf16[128,128]{1,0:T(8,128)(2,1)S(1)} %get-tuple-element.24), channel_id=1, source_target_pairs={{0,16},{8,24},{1,17},{9,25},{2,18},{10,26},{3,19},{11,27},{4,20},{... | collective-permute-start | bytes 98312 | tf_op jit(solution)/shard_map/ppermute | solution.py:260
  25.7 7.3 %collective-permute-start.3 = (bf16[128,128]{1,0:T(8,128)(2,1)S(1)}, bf16[128,128]{1,0:T(8,128)(2,1)S(1)}, u32[]{:S(2)}, u32[]{:S(2)}) collective-permute-start(bf16[128,128]{1,0:T(8,128)(2,1)S(1)} %get-tuple-element.24), channel_id=1, source_target_pairs={{0,24},{1,25},{2,26},{3,27},{4,28},{5,29},{6,30},{7,31}} | collective-permute-start | bytes 98312 | tf_op jit(solution)/shard_map/ppermute | solution.py:260
  35.0 2.0 %collective-permute-start.4 = (bf16[1,256,1024]{2,1,0:T(8,128)(2,1)S(1)}, bf16[1,256,1024]{2,1,0:T(8,128)(2,1)S(1)}, u32[]{:S(2)}, u32[]{:S(2)}) collective-permute-start(bf16[1,256,1024]{2,1,0:T(8,128)(2,1)S(1)} %get-tuple-element.26), channel_id=1, source_target_pairs={{0,1},{1,0},{2,3},{3,2},{4,5},{5,4},{6,7},{7,6},{8,9},{9,8},{10,11... | collective-permute-start | bytes 1572872 | tf_op jit(solution)/shard_map/ppermute | solution.py:455
  42.3 27.9 %collective-permute-start.7 = (bf16[256,2048]{1,0:T(8,128)(2,1)S(1)}, bf16[256,2048]{1,0:T(8,128)(2,1)S(1)}, u32[]{:S(2)}, u32[]{:S(2)}) collective-permute-start(bf16[256,2048]{1,0:T(8,128)(2,1)S(1)} %product.6.rest_0_), channel_id=1, source_target_pairs={{0,2},{1,3},{6,4},{7,5},{8,10},{9,11},{14,12},{15,13},{16,18},{17,... | collective-permute-start | bytes 3145736 | tf_op jit(solution)/shard_map/ppermute | solution.py:455
  55.6 2.0 %collective-permute-start.6 = (bf16[1,256,1024]{2,1,0:T(8,128)(2,1)S(1)}, bf16[1,256,1024]{2,1,0:T(8,128)(2,1)S(1)}, u32[]{:S(2)}, u32[]{:S(2)}) collective-permute-start(bf16[1,256,1024]{2,1,0:T(8,128)(2,1)S(1)} %get-tuple-element.30), channel_id=1, source_target_pairs={{0,1},{1,0},{2,3},{3,2},{4,5},{5,4},{6,7},{7,6},{8,9},{9,8},{10,11... | collective-permute-start | bytes 1572872 | tf_op jit(solution)/shard_map/ppermute | solution.py:455
  55.9 36.8 %collective-permute-start.8 = (bf16[256,2048]{1,0:T(8,128)(2,1)S(1)}, bf16[256,2048]{1,0:T(8,128)(2,1)S(1)}, u32[]{:S(2)}, u32[]{:S(2)}) collective-permute-start(bf16[256,2048]{1,0:T(8,128)(2,1)S(1)} %product.7.rest_0_.refs_0_), channel_id=1, source_target_pairs={{0,2},{1,3},{6,4},{7,5},{8,10},{9,11},{14,12},{15,13},{16,18},{17,... | collective-permute-start | bytes 3145736 | tf_op jit(solution)/shard_map/ppermute | solution.py:455
  66.7 71.1 %collective-permute-start.13 = (bf16[256,4096]{1,0:T(8,128)(2,1)S(1)}, bf16[256,4096]{1,0:T(8,128)(2,1)}, u32[]{:S(2)}, u32[]{:S(2)}) collective-permute-start(bf16[256,4096]{1,0:T(8,128)(2,1)S(1)} %product.8.rest_0_), channel_id=1, source_target_pairs={{0,2},{1,3},{6,4},{7,5},{8,10},{9,11},{14,12},{15,13},{16,18},{17,... | collective-permute-start | bytes 6291464 | tf_op jit(solution)/shard_map/ppermute | solution.py:455
  71.6 44.6 %collective-permute-start.12 = (bf16[256,2048]{1,0:T(8,128)(2,1)}, bf16[256,2048]{1,0:T(8,128)(2,1)}, u32[]{:S(2)}, u32[]{:S(2)}) collective-permute-start(bf16[256,2048]{1,0:T(8,128)(2,1)} %add_convert_fusion.3.rest_1_), channel_id=1, source_target_pairs={{2,4},{3,5},{4,2},{5,3},{10,12},{11,13},{12,10},{13,11},{18,20},{1... | collective-permute-start | bytes 3145736 | tf_op jit(solution)/shard_map/ppermute | solution.py:455
  93.9 31.5 %collective-permute-start.14 = (bf16[256,2048]{1,0:T(8,128)(2,1)S(1)}, bf16[256,2048]{1,0:T(8,128)(2,1)}, u32[]{:S(2)}, u32[]{:S(2)}) collective-permute-start(bf16[256,2048]{1,0:T(8,128)(2,1)S(1)} %sum.2.rest_3_), channel_id=1, source_target_pairs={{2,4},{3,5},{4,2},{5,3},{10,12},{11,13},{12,10},{13,11},{18,20},{1... | collective-permute-start | bytes 3145736 | tf_op jit(solution)/shard_map/ppermute | solution.py:455
  103.8 2.0 %collective-permute-start.11 = (bf16[1,256,1024]{2,1,0:T(8,128)(2,1)S(1)}, bf16[1,256,1024]{2,1,0:T(8,128)(2,1)S(1)}, u32[]{:S(2)}, u32[]{:S(2)}) collective-permute-start(bf16[1,256,1024]{2,1,0:T(8,128)(2,1)S(1)} %get-tuple-element.35), channel_id=1, source_target_pairs={{0,1},{1,0},{2,3},{3,2},{4,5},{5,4},{6,7},{7,6},{8,9},{9,8},{10,11... | collective-permute-start | bytes 1572872 | tf_op jit(solution)/shard_map/ppermute | solution.py:455
  103.9 12.3 %collective-permute-start.10 = (bf16[1,256,1024]{2,1,0:T(8,128)(2,1)S(1)}, bf16[1,256,1024]{2,1,0:T(8,128)(2,1)S(1)}, u32[]{:S(2)}, u32[]{:S(2)}) collective-permute-start(bf16[1,256,1024]{2,1,0:T(8,128)(2,1)S(1)} %get-tuple-element.36), channel_id=1, source_target_pairs={{0,1},{1,0},{2,3},{3,2},{4,5},{5,4},{6,7},{7,6},{8,9},{9,8},{10,11... | collective-permute-start | bytes 1572872 | tf_op jit(solution)/shard_map/ppermute | solution.py:455
  114.8 1.3 copy-start.2
  114.9 67.0 %collective-permute-start.16 = (bf16[256,4096]{1,0:T(8,128)(2,1)S(1)}, bf16[256,4096]{1,0:T(8,128)(2,1)}, u32[]{:S(2)}, u32[]{:S(2)}) collective-permute-start(bf16[256,4096]{1,0:T(8,128)(2,1)S(1)} %product.9.rest_0_), channel_id=1, source_target_pairs={{0,2},{1,3},{6,4},{7,5},{8,10},{9,11},{14,12},{15,13},{16,18},{17,... | collective-permute-start | bytes 6291464 | tf_op jit(solution)/shard_map/ppermute | solution.py:455
  125.3 3.3 %copy-start.1 = (bf16[256,4096]{1,0:T(8,128)(2,1)}, bf16[256,4096]{1,0:T(8,128)(2,1)S(1)}, u32[]{:S(2)}) copy-start(bf16[256,4096]{1,0:T(8,128)(2,1)S(1)} %product.10.rest_0_) | copy-start | bytes 6291460
  128.6 53.3 %collective-permute-start.15 = (bf16[256,4096]{1,0:T(8,128)(2,1)S(1)}, bf16[256,4096]{1,0:T(8,128)(2,1)}, u32[]{:S(2)}, u32[]{:S(2)}) collective-permute-start(bf16[256,4096]{1,0:T(8,128)(2,1)S(1)} %add_convert_fusion.1), channel_id=1, source_target_pairs={{2,0},{3,1},{4,6},{5,7},{10,8},{11,9},{12,14},{13,15},{18,16},{19,... | collective-permute-start | bytes 6291464 | tf_op jit(solution)/shard_map/ppermute | solution.py:455
  140.2 4.4 %copy-start.6 = (bf16[256,4096]{1,0:T(8,128)(2,1)}, bf16[256,4096]{1,0:T(8,128)(2,1)S(1)}, u32[]{:S(2)}) copy-start(bf16[256,4096]{1,0:T(8,128)(2,1)S(1)} %add_convert_fusion.2.rest_1_) | copy-start | bytes 6291460
  140.2 47.9 %collective-permute-start.17 = (bf16[256,4096]{1,0:T(8,128)(2,1)S(1)}, bf16[256,4096]{1,0:T(8,128)(2,1)S(1)}, u32[]{:S(2)}, u32[]{:S(2)}) collective-permute-start(bf16[256,4096]{1,0:T(8,128)(2,1)S(1)} %add_convert_fusion.2.rest_1_), channel_id=1, source_target_pairs={{2,4},{3,5},{4,2},{5,3},{10,12},{11,13},{12,10},{13,11},{18,20},{1... | collective-permute-start | bytes 6291464 | tf_op jit(solution)/shard_map/ppermute | solution.py:455
  142.5 2.0 %collective-permute-start.9 = (bf16[1,256,1024]{2,1,0:T(8,128)(2,1)S(1)}, bf16[1,256,1024]{2,1,0:T(8,128)(2,1)S(1)}, u32[]{:S(2)}, u32[]{:S(2)}) collective-permute-start(bf16[1,256,1024]{2,1,0:T(8,128)(2,1)S(1)} %get-tuple-element.37), channel_id=1, source_target_pairs={{0,1},{1,0},{2,3},{3,2},{4,5},{5,4},{6,7},{7,6},{8,9},{9,8},{10,11... | collective-permute-start | bytes 1572872 | tf_op jit(solution)/shard_map/ppermute | solution.py:455
  (1 other events, 0.8 us)
